TPU v7x, 32 devices: a whole 2x2x4 slice. The times are simulated.
32 devices in a mesh: dp: 32 (over z, y, x, core).
Axes of the slice: x: 2, y: 2, z: 4, core: 2. Of those that a mesh axis runs over, the one named last changes fastest.
Arguments:
- inputs: bfloat16 [130560, 256], P('dp'), may hold values from -6 to 6
- frames: int32 [128, 4], P('dp'), may hold values from 1 to 20, 60 in all within a row
- cotangent: float32 [130560, 256], P('dp'), may hold values from -28 to 28
- proj_in: float32 [256, 768], replicated, may hold values from -0.375 to 0.375
- proj_out: float32 [256, 256], replicated, may hold values from -2 to 2
- ffn_up: float32 [256, 1024], replicated, may hold values from -0.375 to 0.375
- ffn_down: float32 [1024, 256], replicated, may hold values from -0.1875 to 0.1875
- vectors: float32 [8, 256], replicated, may hold values from -1 to 2
- ffn_bias: float32 [1024], replicated, may hold values from -1.2 to 1.2
- first_in: float32 [196608], P('dp'), may hold values from -433.59705 to 433.59705
- second_in: float32 [196608], P('dp'), may hold values from 0 to 130560, as said below
- first_out: float32 [65536], P('dp'), may hold values from -433.59705 to 433.59705
- second_out: float32 [65536], P('dp'), may hold values from 0 to 130560, as said below
- first_up: float32 [262144], P('dp'), may hold values from -1011.72645 to 1011.72645
- second_up: float32 [262144], P('dp'), may hold values from 0 to 652800, as said below
- first_down: float32 [262144], P('dp'), may hold values from -1156.2588 to 1156.2588
- second_down: float32 [262144], P('dp'), may hold values from 0 to 913920, as said below
- first_vec: float32 [8, 256], replicated, may hold values from -1156.2588 to 1156.2588
- second_vec: float32 [8, 256], replicated, may hold values from 0 to 913920, as said below
- first_bias: float32 [1024], replicated, may hold values from -1011.72645 to 1011.72645
- second_bias: float32 [1024], replicated, may hold values from 0 to 652800, as said below
Outputs:
- block_out: bfloat16 [130560, 256], P('dp')
- grad_inputs: float32 [130560, 256], P('dp')
- grad_in: float32 [196608], P('dp')
- grad_out: float32 [65536], P('dp')
- grad_up: float32 [262144], P('dp')
- grad_down: float32 [262144], P('dp')
- grad_vec: float32 [8, 256], replicated
- grad_bias: float32 [1024], replicated
- momentum_in: float32 [196608], P('dp')
- variance_in: float32 [196608], P('dp')
- weight_in: float32 [256, 768], replicated
- copy_in: bfloat16 [256, 768], replicated
- momentum_out: float32 [65536], P('dp')
- variance_out: float32 [65536], P('dp')
- weight_out: float32 [256, 256], replicated
- copy_out: bfloat16 [256, 256], replicated
- momentum_up: float32 [262144], P('dp')
- variance_up: float32 [262144], P('dp')
- weight_up: float32 [256, 1024], replicated
- copy_up: bfloat16 [256, 1024], replicated
- momentum_down: float32 [262144], P('dp')
- variance_down: float32 [262144], P('dp')
- weight_down: float32 [1024, 256], replicated
- copy_down: bfloat16 [1024, 256], replicated
- momentum_vec: float32 [8, 256], replicated
- variance_vec: float32 [8, 256], replicated
- weight_vec: float32 [8, 256], replicated
- momentum_bias: float32 [1024], replicated
- variance_bias: float32 [1024], replicated
- weight_bias: float32 [1024], replicated
- norms: float32 [4, 2], replicated
Inputs may be any that keep to these rules, and one draw needn't show every extreme that they name: Row m gives in order the frames of the 4 sequences packed into micro-batch m, micro-batches in the order of the tokens; each row sums to 60 and its largest entry is 20. `second_in`: positive. `second_out`: positive. `second_up`: positive. `second_down`: positive. `second_vec`: positive. `second_bias`: positive.
All inputs are finite; a program needn't handle non-finite values.
Results may differ from a plain program's by a relative error of at most 0.007.
The roundings to bfloat16 on the way count: a program that leaves them out, or rounds other values in their place, can miss the bound.
Values sent between devices are 32-bit elements; how exact they have to be, the bound alone decides.
A program may use at most 192 MiB of HBM per device.

v0:
```python
import math

import jax
import jax.numpy as jnp
from jax import lax
from jax.sharding import PartitionSpec as P

HEADS = 4
HEAD_DIM = 64
FRAME = 17
STEP = 10


EPS_NORM = 1e-05
EPS_ADAM = 1e-06
BETA = 0.5
DECAY = 0.01
RATE = 0.5
RATE_VEC = 0.2


def layer_norm(values, gain, shift):
    center = values - jnp.mean(values, axis=-1, keepdims=True)
    spread = jnp.mean(center * center, axis=-1, keepdims=True)
    return center * lax.rsqrt(spread + EPS_NORM) * gain + shift


def gelu_exact(values):
    return jax.nn.gelu(values, approximate=False)


def allowed(counts, length):
    ends = jnp.cumsum(counts)
    frame = jnp.arange(length, dtype=jnp.int32) // FRAME
    owner = jnp.sum((frame[:, None] >= ends[None, :]).astype(jnp.int32), axis=1)
    return (owner[:, None] == owner[None, :]) & (frame[:, None] >= frame[None, :])


def over_rows(left, right):
    return lax.dot_general(
        left, right, (((0,), (0,)), ((), ())), preferred_element_type=jnp.float32
    )


def by_transpose(left, right):
    return lax.dot_general(
        left, right, (((1,), (1,)), ((), ())), preferred_element_type=jnp.float32
    )


def split_heads(block):
    width = block.shape[1] // 3
    length = block.shape[0]
    query = block[:, :width].reshape(length, HEADS, HEAD_DIM)
    keys = block[:, width : 2 * width].reshape(length, HEADS, HEAD_DIM)
    values = block[:, 2 * width :].reshape(length, HEADS, HEAD_DIM)
    return (query, keys, values)


def scores_of(query, keys, counts):
    raw = jnp.einsum("qhd,khd->hqk", query, keys, preferred_element_type=jnp.float32) * (
        1.0 / math.sqrt(HEAD_DIM)
    )
    return jnp.where(allowed(counts, query.shape[0])[None], raw, -1e30)


def attend(item):
    block, counts = item
    query, keys, values = split_heads(block)
    score = scores_of(query, keys, counts)
    peak = jnp.max(score, axis=-1, keepdims=True)
    weight = jnp.exp(score - peak)
    total = jnp.sum(weight, axis=-1, keepdims=True)
    prob = (weight / total).astype(jnp.bfloat16)
    mixed = jnp.einsum("hqk,khd->qhd", prob, values, preferred_element_type=jnp.float32)
    return (mixed.reshape(block.shape[0], -1).astype(jnp.bfloat16), peak + jnp.log(total))


def attend_back(item):
    block, counts, logsum, d_mixed = item
    query, keys, values = split_heads(block)
    scale = 1.0 / math.sqrt(HEAD_DIM)
    prob = jnp.exp(scores_of(query, keys, counts) - logsum)
    d_heads = d_mixed.reshape(query.shape)
    d_prob = jnp.einsum("qhd,khd->hqk", d_heads, values, preferred_element_type=jnp.float32)
    delta = jnp.sum(prob * d_prob, axis=-1, keepdims=True)
    d_score = (prob * (d_prob - delta)).astype(jnp.bfloat16)
    d_query = jnp.einsum("hqk,khd->qhd", d_score, keys, preferred_element_type=jnp.float32) * scale
    d_keys = jnp.einsum("hqk,qhd->khd", d_score, query, preferred_element_type=jnp.float32) * scale
    d_values = jnp.einsum(
        "hqk,qhd->khd", prob.astype(jnp.bfloat16), d_heads, preferred_element_type=jnp.float32
    )
    length = block.shape[0]
    joined = jnp.concatenate(
        [d_query.reshape(length, -1), d_keys.reshape(length, -1), d_values.reshape(length, -1)],
        axis=1,
    )
    return joined.astype(jnp.bfloat16)


def own_share(array, length, place):
    return lax.dynamic_slice_in_dim(array.reshape(-1), place * length, length)


def shard_steps(shares, firsts, seconds, weights, place, fix):
    results = []
    for share, first, second, weight in zip(shares, firsts, seconds, weights):
        momentum = BETA * first + (1.0 - BETA) * share
        variance = BETA * second + (1.0 - BETA) * share * share
        w_share = own_share(weight, first.shape[0], place)
        advance = momentum / fix / (jnp.sqrt(variance / fix) + EPS_ADAM) + DECAY * w_share
        results.append((momentum, variance, advance, w_share))
    return results


def adam_plain(weight, grad, first, second, fix):
    momentum = BETA * first + (1.0 - BETA) * grad
    variance = BETA * second + (1.0 - BETA) * grad * grad
    fresh = weight - RATE_VEC * (momentum / fix) / (jnp.sqrt(variance / fix) + EPS_ADAM)
    return (momentum, variance, fresh)


def on_device(
    inputs,
    frames,
    cotangent,
    proj_in,
    proj_out,
    ffn_up,
    ffn_down,
    vectors,
    ffn_bias,
    first_in,
    second_in,
    first_out,
    second_out,
    first_up,
    second_up,
    first_down,
    second_down,
    first_vec,
    second_vec,
    first_bias,
    second_bias,
):
    bf = jnp.bfloat16
    tokens = inputs.shape[0]
    blocks = frames.shape[0]
    block_rows = tokens // blocks
    width = inputs.shape[1]
    w_in = proj_in.astype(bf)
    w_out = proj_out.astype(bf)
    w_up = ffn_up.astype(bf)
    w_down = ffn_down.astype(bf)
    values = inputs.astype(jnp.float32)
    h_one, norm_one_pull = jax.vjp(layer_norm, values, vectors[3], vectors[4])
    h_one = h_one.astype(bf)
    bias_row = jnp.concatenate([vectors[0], jnp.zeros_like(vectors[0]), vectors[1]])
    joined = (jnp.dot(h_one, w_in, preferred_element_type=jnp.float32) + bias_row).astype(bf)
    joined_blocks = joined.reshape(blocks, block_rows, 3 * width)
    mixed, logsum = lax.map(attend, (joined_blocks, frames))
    mixed = mixed.reshape(tokens, width)
    resid = values + jnp.dot(mixed, w_out, preferred_element_type=jnp.float32) + vectors[2]
    h_two, norm_two_pull = jax.vjp(layer_norm, resid, vectors[5], vectors[6])
    h_two = h_two.astype(bf)
    pre = jnp.dot(h_two, w_up, preferred_element_type=jnp.float32) + ffn_bias
    hidden, gelu_pull = jax.vjp(gelu_exact, pre)
    hidden = hidden.astype(bf)
    feed = jnp.dot(hidden, w_down, preferred_element_type=jnp.float32) + vectors[7]
    block_out = (resid + feed).astype(bf)
    cot_low = cotangent.astype(bf)
    g_down = over_rows(hidden, cot_low)
    g_feed_bias = jnp.sum(cot_low.astype(jnp.float32), axis=0)
    (d_pre,) = gelu_pull(by_transpose(cot_low, w_down))
    d_pre = d_pre.astype(bf)
    g_up = over_rows(h_two, d_pre)
    g_bias = jnp.sum(d_pre.astype(jnp.float32), axis=0)
    d_resid_norm, g_gain_two, g_shift_two = norm_two_pull(by_transpose(d_pre, w_up))
    d_resid = cotangent + d_resid_norm
    d_branch = d_resid.astype(bf)
    g_out = over_rows(mixed, d_branch)
    g_out_bias = jnp.sum(d_branch.astype(jnp.float32), axis=0)
    d_mixed = by_transpose(d_branch, w_out).astype(bf)
    d_joined = lax.map(
        attend_back, (joined_blocks, frames, logsum, d_mixed.reshape(blocks, block_rows, width))
    )
    d_joined = d_joined.reshape(tokens, 3 * width)
    g_in = over_rows(h_one, d_joined)
    joined_sums = jnp.sum(d_joined.astype(jnp.float32), axis=0)
    d_values_norm, g_gain_one, g_shift_one = norm_one_pull(by_transpose(d_joined, w_in))
    grad_inputs = d_resid + d_values_norm
    g_vec = jnp.stack(
        [
            joined_sums[:width],
            joined_sums[2 * width :],
            g_out_bias,
            g_gain_one,
            g_shift_one,
            g_gain_two,
            g_shift_two,
            g_feed_bias,
        ]
    )
    fix = 1.0 - BETA**STEP
    place = lax.axis_index("dp")
    weights = (proj_in, proj_out, ffn_up, ffn_down)
    firsts = (first_in, first_out, first_up, first_down)
    seconds = (second_in, second_out, second_up, second_down)
    g_in, g_out, g_up, g_down, g_vec, g_bias = lax.psum(
        (g_in, g_out, g_up, g_down, g_vec, g_bias), "dp"
    )
    shares = [
        own_share(full, first.shape[0], place)
        for full, first in zip((g_in, g_out, g_up, g_down), firsts)
    ]
    updated = shard_steps(shares, firsts, seconds, weights, place, fix)
    squares = jnp.stack([jnp.sum(entry[2] * entry[2]) for entry in updated])
    squares = lax.psum(squares, "dp")
    w_norms = jnp.stack([jnp.sqrt(jnp.sum(weight * weight)) for weight in weights])
    u_norms = jnp.sqrt(squares)
    fresh_shares = tuple(
        (
            entry[3] - RATE * (w_norms[index] / (u_norms[index] + EPS_ADAM)) * entry[2]
            for index, entry in enumerate(updated)
        )
    )
    gathered = lax.all_gather(fresh_shares, "dp", axis=0, tiled=True)
    fresh = [full.reshape(weight.shape) for full, weight in zip(gathered, weights)]
    m_vec, v_vec, w_vec = adam_plain(vectors, g_vec, first_vec, second_vec, fix)
    m_bias, v_bias, w_bias = adam_plain(ffn_bias, g_bias, first_bias, second_bias, fix)
    norms = jnp.stack([w_norms, u_norms], axis=1)
    return (
        block_out,
        grad_inputs,
        shares[0],
        shares[1],
        shares[2],
        shares[3],
        g_vec,
        g_bias,
        updated[0][0],
        updated[0][1],
        fresh[0],
        fresh[0].astype(bf),
        updated[1][0],
        updated[1][1],
        fresh[1],
        fresh[1].astype(bf),
        updated[2][0],
        updated[2][1],
        fresh[2],
        fresh[2].astype(bf),
        updated[3][0],
        updated[3][1],
        fresh[3],
        fresh[3].astype(bf),
        m_vec,
        v_vec,
        w_vec,
        m_bias,
        v_bias,
        w_bias,
        norms,
    )


def solution(mesh):
    placed = (
        P("dp", None),
        P("dp", None),
        P("dp", None),
        P(),
        P(),
        P(),
        P(),
        P(),
        P(),
        P("dp"),
        P("dp"),
        P("dp"),
        P("dp"),
        P("dp"),
        P("dp"),
        P("dp"),
        P("dp"),
        P(),
        P(),
        P(),
        P(),
    )
    return jax.shard_map(
        on_device,
        mesh=mesh,
        in_specs=placed,
        out_specs=(
            P("dp", None),
            P("dp", None),
            P("dp"),
            P("dp"),
            P("dp"),
            P("dp"),
            P(),
            P(),
            P("dp"),
            P("dp"),
            P(),
            P(),
            P("dp"),
            P("dp"),
            P(),
            P(),
            P("dp"),
            P("dp"),
            P(),
            P(),
            P("dp"),
            P("dp"),
            P(),
            P(),
            P(),
            P(),
            P(),
            P(),
            P(),
            P(),
            P(),
        ),
        check_vma=False,
    )
```

profile of v0, /device:TPU:0, one launch (start us, length us, event | category | flops | bytes accessed | tf_op | source)
XLA Modules:
  0.0 729.0 jit_solution(10136085091503129624)
XLA Ops:
  15.0 5.1 add_convert_fusion.1
  20.1 5.2 reshape.558
  25.2 8.6 %copy.81 = bf16[4,1020,768]{1,2,0:T(8,128)(2,1)} copy(bf16[4,1020,768]{2,1,0:T(8,128)(2,1)} %reshape.558) | data formatting | bytes 12533760 | tf_op jit(solution)/shard_map/while | solution.py:161
  33.9 69.2 %while.26 = (s32[]{:T(128)}, bf16[4,1020,256]{2,1,0:T(8,128)(2,1)}, f32[4,4,1020,1]{2,1,3,0:T(4,128)S(1)}, bf16[4,1020,768]{1,2,0:T(8,128)(2,1)}, s32[4,4]{1,0:T(4,128)}, /*index=5*/s32[]{:T(128)}, s32[]{:T(128)}) while((s32[]{:T(128)}, bf16[4,1020,256]{2,1,0:T(8,128)(2,1)}, f32[4,4,1020,1]{2,1,3,0:T(4,128)S(1)}, ...), condition=%wide.region_7.8_spmd, body=%wide.region_2.7_spmd.sunk | while | flops 1118706432 | bytes 64698984 | solution.py:161
  62.4 5.0 fusion.137
  110.5 42.1 %multiply_convert_fusion.1 = (bf16[4080,1024]{1,0:T(8,128)(2,1)}, f32[4080,1024]{1,0:T(8,128)}, f32[4080,1024]{1,0:T(8,128)}) fusion(f32[1024]{0:T(1024)S(1)} %copy-done.44, f32[256,1024]{1,0:T(8,128)S(1)} %copy-done.14, f32[4080,256]{1,0:T(8,128)S(1)} %get-tuple-element.320, f32[256]{0:T(256)S(1)} %bitcast.216, f32[256]{0:T(256)S(1)} %bitcast.200, ...), kind=kOutput, calls=%fused_computation.52 | convolution fusion | flops 2420322304 | bytes 47044480 | tf_op jit(solution)/shard_map/dot_general | solution.py:166
  152.6 18.5 %convert_reduce_fusion.2 = (f32[1024]{0:T(1024)}, bf16[4080,1024]{1,0:T(8,128)(2,1)}) fusion(f32[4080,1024]{1,0:T(8,128)} %get-tuple-element.290, f32[1024,256]{1,0:T(8,128)S(1)} %copy-done.16, f32[4080,256]{1,0:T(8,128)} %param.27, f32[4080,1024]{1,0:T(8,128)} %get-tuple-element.321, f32[1024]{0:T(1024)S(1)} %copy-done.44), kind=kOutput, calls=%fused_computation.50 | convolution fusion | flops 2211425280 | bytes 47013888 | tf_op jit(solution)/shard_map/dot_general | solution.py:46
  171.1 8.2 %convolution_bitcast_fusion.1 = f32[32,8,8,128]{3,2,1,0:T(8,128)S(1)} fusion(bf16[4080,1024]{1,0:T(8,128)(2,1)} %get-tuple-element.325, f32[4080,256]{1,0:T(8,128)} %copy-done.8, f32[256]{0:T(256)S(1)} %bitcast.217, f32[256]{0:T(256)S(1)} %bitcast.201, f32[4080]{0:T(1024)S(1)} %fusion.57, f32[4080]{0:T(1024)S(1)} %broadcast_multiply_fusion), kind=kOutput, calls=%fused_computation.98 | convolution fusion | flops 2144317440 | bytes 13617024 | tf_op jit(solution)/shard_map/dot_general | solution.py:40
  199.4 194.6 %while.27 = (s32[]{:T(128)}, bf16[4,1020,768]{1,2,0:T(8,128)(2,1)}, bf16[4,1020,768]{1,2,0:T(8,128)(2,1)}, s32[4,4]{1,0:T(4,128)}, f32[4,4,1020,1]{2,1,3,0:T(4,1...) while((s32[]{:T(128)}, bf16[4,1020,768]{1,2,0:T(8,128)(2,1)}, ...), condition=%wide.region_16.17_spmd, body=%wide.region_12.16_spmd.sunk | while | flops 2710020608 | bytes 179130640 | solution.py:184
  218.5 11.5 %multiply_reduce_fusion.13 = (f32[4,1020]{1,0:T(4,128)}, f32[4,1020,1020]{1,2,0:T(8,128)}) fusion(f32[4,1020,1020]{1,2,0:T(8,128)S(1)} %fusion.149, f32[4,1020]{1,0:T(4,128)} %dynamic-slice_bitcast_fusion.8, bf16[1020,4,64]{0,2,1:T(8,128)(2,1)S(1)} %bitcast.166, bf16[1020,4,64]{0,2,1:T(8,128)(2,1)} %bitcast.168, ...), kind=kOutput, calls=%fused_computation.24.clone.1 | convolution fusion | flops 553488704 | bytes 35410320 | tf_op jit(solution)/shard_map/while/body/eval_jaxpr/qhd,khd->hqk/dot_general | solution.py:61
  229.9 10.3 %multiply_convert_fusion.3 = bf16[4,1020,1020]{1,2,0:T(8,128)(2,1)} fusion(f32[4,1020,1020]{1,2,0:T(8,128)} %get-tuple-element.417, f32[4,1020,1020]{1,2,0:T(8,128)S(1)} %fusion.149, f32[4,1020]{1,0:T(4,128)} %get-tuple-element.418), kind=kLoop, calls=%fused_computation.23.clone.1 | loop fusion | flops 12484800 | bytes 41632320 | tf_op jit(solution)/shard_map/while/body/eval_jaxpr/convert_element_type | solution.py:87
  240.3 8.6 %fusion.151 = bf16[4,64,1020]{2,1,0:T(8,128)(2,1)S(1)} fusion(bf16[1020,4,64]{0,2,1:T(8,128)(2,1)S(1)} %bitcast.165, f32[4,1020,1020]{1,2,0:T(8,128)} %get-tuple-element.417), kind=kOutput, calls=%fused_computation.33.clone.1 | convolution fusion | flops 537107520 | bytes 17690880 | tf_op jit(solution)/shard_map/while/body/eval_jaxpr/hqk,qhd->khd/dot_general | solution.py:90
  264.9 11.5 %multiply_reduce_fusion.13 = (f32[4,1020]{1,0:T(4,128)}, f32[4,1020,1020]{1,2,0:T(8,128)}) fusion(f32[4,1020,1020]{1,2,0:T(8,128)S(1)} %fusion.149, f32[4,1020]{1,0:T(4,128)} %dynamic-slice_bitcast_fusion.8, bf16[1020,4,64]{0,2,1:T(8,128)(2,1)S(1)} %bitcast.166, bf16[1020,4,64]{0,2,1:T(8,128)(2,1)} %bitcast.168, ...), kind=kOutput, calls=%fused_computation.24.clone.1 | convolution fusion | flops 553488704 | bytes 35410320 | tf_op jit(solution)/shard_map/while/body/eval_jaxpr/qhd,khd->hqk/dot_general | solution.py:61
  276.3 10.3 %multiply_convert_fusion.3 = bf16[4,1020,1020]{1,2,0:T(8,128)(2,1)} fusion(f32[4,1020,1020]{1,2,0:T(8,128)} %get-tuple-element.417, f32[4,1020,1020]{1,2,0:T(8,128)S(1)} %fusion.149, f32[4,1020]{1,0:T(4,128)} %get-tuple-element.418), kind=kLoop, calls=%fused_computation.23.clone.1 | loop fusion | flops 12484800 | bytes 41632320 | tf_op jit(solution)/shard_map/while/body/eval_jaxpr/convert_element_type | solution.py:87
  286.7 8.6 %fusion.151 = bf16[4,64,1020]{2,1,0:T(8,128)(2,1)S(1)} fusion(bf16[1020,4,64]{0,2,1:T(8,128)(2,1)S(1)} %bitcast.165, f32[4,1020,1020]{1,2,0:T(8,128)} %get-tuple-element.417), kind=kOutput, calls=%fused_computation.33.clone.1 | convolution fusion | flops 537107520 | bytes 17690880 | tf_op jit(solution)/shard_map/while/body/eval_jaxpr/hqk,qhd->khd/dot_general | solution.py:90
  311.3 11.5 %multiply_reduce_fusion.13 = (f32[4,1020]{1,0:T(4,128)}, f32[4,1020,1020]{1,2,0:T(8,128)}) fusion(f32[4,1020,1020]{1,2,0:T(8,128)S(1)} %fusion.149, f32[4,1020]{1,0:T(4,128)} %dynamic-slice_bitcast_fusion.8, bf16[1020,4,64]{0,2,1:T(8,128)(2,1)S(1)} %bitcast.166, bf16[1020,4,64]{0,2,1:T(8,128)(2,1)} %bitcast.168, ...), kind=kOutput, calls=%fused_computation.24.clone.1 | convolution fusion | flops 553488704 | bytes 35410320 | tf_op jit(solution)/shard_map/while/body/eval_jaxpr/qhd,khd->hqk/dot_general | solution.py:61
  322.8 10.3 %multiply_convert_fusion.3 = bf16[4,1020,1020]{1,2,0:T(8,128)(2,1)} fusion(f32[4,1020,1020]{1,2,0:T(8,128)} %get-tuple-element.417, f32[4,1020,1020]{1,2,0:T(8,128)S(1)} %fusion.149, f32[4,1020]{1,0:T(4,128)} %get-tuple-element.418), kind=kLoop, calls=%fused_computation.23.clone.1 | loop fusion | flops 12484800 | bytes 41632320 | tf_op jit(solution)/shard_map/while/body/eval_jaxpr/convert_element_type | solution.py:87
  333.1 8.6 %fusion.151 = bf16[4,64,1020]{2,1,0:T(8,128)(2,1)S(1)} fusion(bf16[1020,4,64]{0,2,1:T(8,128)(2,1)S(1)} %bitcast.165, f32[4,1020,1020]{1,2,0:T(8,128)} %get-tuple-element.417), kind=kOutput, calls=%fused_computation.33.clone.1 | convolution fusion | flops 537107520 | bytes 17690880 | tf_op jit(solution)/shard_map/while/body/eval_jaxpr/hqk,qhd->khd/dot_general | solution.py:90
  357.8 11.5 %multiply_reduce_fusion.13 = (f32[4,1020]{1,0:T(4,128)}, f32[4,1020,1020]{1,2,0:T(8,128)}) fusion(f32[4,1020,1020]{1,2,0:T(8,128)S(1)} %fusion.149, f32[4,1020]{1,0:T(4,128)} %dynamic-slice_bitcast_fusion.8, bf16[1020,4,64]{0,2,1:T(8,128)(2,1)S(1)} %bitcast.166, bf16[1020,4,64]{0,2,1:T(8,128)(2,1)} %bitcast.168, ...), kind=kOutput, calls=%fused_computation.24.clone.1 | convolution fusion | flops 553488704 | bytes 35410320 | tf_op jit(solution)/shard_map/while/body/eval_jaxpr/qhd,khd->hqk/dot_general | solution.py:61
  369.3 10.3 %multiply_convert_fusion.3 = bf16[4,1020,1020]{1,2,0:T(8,128)(2,1)} fusion(f32[4,1020,1020]{1,2,0:T(8,128)} %get-tuple-element.417, f32[4,1020,1020]{1,2,0:T(8,128)S(1)} %fusion.149, f32[4,1020]{1,0:T(4,128)} %get-tuple-element.418), kind=kLoop, calls=%fused_computation.23.clone.1 | loop fusion | flops 12484800 | bytes 41632320 | tf_op jit(solution)/shard_map/while/body/eval_jaxpr/convert_element_type | solution.py:87
  379.6 8.6 %fusion.151 = bf16[4,64,1020]{2,1,0:T(8,128)(2,1)S(1)} fusion(bf16[1020,4,64]{0,2,1:T(8,128)(2,1)S(1)} %bitcast.165, f32[4,1020,1020]{1,2,0:T(8,128)} %get-tuple-element.417), kind=kOutput, calls=%fused_computation.33.clone.1 | convolution fusion | flops 537107520 | bytes 17690880 | tf_op jit(solution)/shard_map/while/body/eval_jaxpr/hqk,qhd->khd/dot_general | solution.py:90
  394.0 8.7 %copy.85 = bf16[4,1020,768]{2,1,0:T(8,128)(2,1)} copy(bf16[4,1020,768]{1,2,0:T(8,128)(2,1)} %get-tuple-element.178) | data formatting | bytes 12533760 | tf_op jit(solution)/shard_map/while | solution.py:184
  402.7 5.3 reshape.561
  408.0 6.5 fusion.63
  423.5 7.8 %fusion.67 = (f32[256]{0:T(256)}, f32[4080]{0:T(1024)S(1)}, f32[4080,256]{1,0:T(8,128)}) fusion(f32[256]{0:T(256)S(1)} %bitcast.197, f32[4080]{0:T(1024)S(1)} %copy-done.25, bf16[4080,256]{1,0:T(8,128)(2,1)S(1)} %copy-done.4, bf16[4080,768]{1,0:T(8,128)(2,1)} %reshape.561, f32[256,768]{1,0:T(8,128)S(1)} %copy-done.21), kind=kOutput, calls=%fused_computation.167 | convolution fusion | flops 1610780416 | bytes 13354880 | tf_op jit(solution)/shard_map/dot_general | solution.py:46
  437.3 5.2 fusion.38
  442.6 9.4 %convert_reduce_fusion.5 = (f32[256]{0:T(256)}, f32[4080,256]{1,0:T(8,128)}) fusion(f32[4080,256]{1,0:T(8,128)S(1)} %copy-done.6, f32[4080]{0:T(1024)S(1)} %negate_multiply_fusion.1, f32[4080]{0:T(1024)S(1)} %multiply_multiply_fusion.8, f32[4080]{0:T(1024)S(1)} %copy-done.25, bf16[4080,256]{1,0:T(8,128)(2,1)S(1)} %copy-done.4, f32[4080]{0:T(1024)S(1)} %copy-done.27, ...), kind=kLoop, calls=%fused_computation.89 | loop fusion | flops 14622464 | bytes 18884288 | tf_op jit(solution)/shard_map/reduce_sum | solution.py:173
  452.8 105.7 %all-reduce.4.cloned.1.call-done = (f32[196608]{0:T(1024)}, f32[65536]{0:T(1024)}, f32[262144]{0:T(1024)}, f32[262144]{0:T(1024)}) async-done(((f32[196608]{0:T(1024)}, f32[65536]{0:T(1024)}, f32[262144]{0:T(1024)}, f32[262144]{0:T(1024)}), (f32[196608]{0:T(1024)}, f32[65536]{0:T(1024)}, f32[262144]{0:T(1024)}, f32[262144]{0:T(1024)})) %all-reduce.4.cloned.1.call-update) | async-done | bytes 3145744 | tf_op jit(solution)/shard_map/psum | solution.py:209
  567.2 39.5 %all-reduce = (f32[8,256]{1,0:T(8,128)S(1)}, f32[1024]{0:T(1024)S(1)}, f32[4]{0:T(128)S(1)}) all-reduce(f32[8,256]{1,0:T(8,128)S(1)} %stack.62, f32[1024]{0:T(1024)} %get-tuple-element.324, f32[4]{0:T(128)S(1)} %pad_maximum_fusion.2), channel_id=1, replica_groups=mesh['dp'=32] {'dp'}, use_global_device_ids=true, to_apply=%region_30.31 | all-reduce | flops 3076 | bytes 24608 | tf_op jit(solution)/shard_map/psum | solution.py:209
  617.2 8.6 %fusion.33 = bf16[4080,256]{1,0:T(8,128)(2,1)} fusion(f32[4080,256]{1,0:T(8,128)} %copy-done.8, bf16[4080,1024]{1,0:T(8,128)(2,1)} %get-tuple-element.289, f32[256]{0:T(256)} %bitcast.211, f32[1024,256]{1,0:T(8,128)} %param.31), kind=kOutput, calls=%fused_computation.80 | convolution fusion | flops 2142490624 | bytes 15672320 | tf_op jit(solution)/shard_map/dot_general | solution.py:169
  628.0 40.9 %all_gather.13 = f32[65536]{0:T(1024)S(1)} all-gather(f32[2048]{0:T(1024)S(1)} %multiply_subtract_fusion.3), channel_id=1, replica_groups=mesh['dp'=32] {'dp'}, dimensions={0}, use_global_device_ids=true | all-gather | bytes 270336 | tf_op jit(solution)/shard_map/all_gather | solution.py:227
  670.4 39.3 %all_gather.12 = f32[196608]{0:T(1024)S(1)} all-gather(f32[6144]{0:T(1024)S(1)} %multiply_subtract_fusion.2), channel_id=1, replica_groups=mesh['dp'=32] {'dp'}, dimensions={0}, use_global_device_ids=true | all-gather | bytes 811008 | tf_op jit(solution)/shard_map/all_gather | solution.py:227
  (301 shorter events, 208.5 us)
Async XLA Ops:
  7.2 551.2 %all-reduce.4.cloned.1.call-start = ((), (), s32[]{:S(2)}) async-start(), calls=%async_computation.2 | async-start | bytes 6291456 | tf_op jit(solution)/shard_map/psum | solution.py:209
  33.9 72.1 %copy-start.43 = (f32[1,256]{1,0:T(1,128)S(1)}, f32[1,256]{1,0:T(1,128)}, u32[]{:S(2)}) copy-start(f32[1,256]{1,0:T(1,128)} %get-tuple-element.306) | copy-start | bytes 3076
  108.4 44.1 %copy-start.8 = (f32[4080,256]{1,0:T(8,128)}, f32[4080,256]{1,0:T(8,128)S(1)}, u32[]{:S(2)}) copy-start(f32[4080,256]{1,0:T(8,128)S(1)} %get-tuple-element.320) | copy-start | bytes 12533764
  110.5 42.1 %copy-start.16 = (f32[1024,256]{1,0:T(8,128)S(1)}, f32[1024,256]{1,0:T(8,128)}, u32[]{:S(2)}) copy-start(f32[1024,256]{1,0:T(8,128)} %param.31) | copy-start | bytes 3145732
  171.1 8.2 %copy-start.9 = (f32[4080,256]{1,0:T(8,128)S(1)}, f32[4080,256]{1,0:T(8,128)}, u32[]{:S(2)}) copy-start(f32[4080,256]{1,0:T(8,128)} %copy-done.8) | copy-start | bytes 12533764
  171.1 8.3 %copy-start.52 = (bf16[4080,1024]{1,0:T(8,128)(2,1)S(1)}, bf16[4080,1024]{1,0:T(8,128)(2,1)}, u32[]{:S(2)}) copy-start(bf16[4080,1024]{1,0:T(8,128)(2,1)} %get-tuple-element.325) | copy-start | bytes 25067524
  240.3 8.6 %copy-start = (bf16[4,1020,1020]{1,2,0:T(8,128)(2,1)S(1)}, bf16[4,1020,1020]{1,2,0:T(8,128)(2,1)}, u32[]{:S(2)}) copy-start(bf16[4,1020,1020]{1,2,0:T(8,128)(2,1)} %multiply_convert_fusion.3) | copy-start | bytes 24969604 | tf_op jit(solution)/shard_map/while
  240.3 8.6 %copy-start.1 = (bf16[1020,256]{0,1:T(8,128)(2,1)S(1)}, bf16[1020,256]{0,1:T(8,128)(2,1)}, u32[]{:S(2)}) copy-start(bf16[1020,256]{0,1:T(8,128)(2,1)} %get-tuple-element.416) | copy-start | bytes 1566724 | tf_op jit(solution)/shard_map/while
  286.7 8.6 %copy-start = (bf16[4,1020,1020]{1,2,0:T(8,128)(2,1)S(1)}, bf16[4,1020,1020]{1,2,0:T(8,128)(2,1)}, u32[]{:S(2)}) copy-start(bf16[4,1020,1020]{1,2,0:T(8,128)(2,1)} %multiply_convert_fusion.3) | copy-start | bytes 24969604 | tf_op jit(solution)/shard_map/while
  286.7 8.6 %copy-start.1 = (bf16[1020,256]{0,1:T(8,128)(2,1)S(1)}, bf16[1020,256]{0,1:T(8,128)(2,1)}, u32[]{:S(2)}) copy-start(bf16[1020,256]{0,1:T(8,128)(2,1)} %get-tuple-element.416) | copy-start | bytes 1566724 | tf_op jit(solution)/shard_map/while
  333.1 8.6 %copy-start = (bf16[4,1020,1020]{1,2,0:T(8,128)(2,1)S(1)}, bf16[4,1020,1020]{1,2,0:T(8,128)(2,1)}, u32[]{:S(2)}) copy-start(bf16[4,1020,1020]{1,2,0:T(8,128)(2,1)} %multiply_convert_fusion.3) | copy-start | bytes 24969604 | tf_op jit(solution)/shard_map/while
  333.1 8.6 %copy-start.1 = (bf16[1020,256]{0,1:T(8,128)(2,1)S(1)}, bf16[1020,256]{0,1:T(8,128)(2,1)}, u32[]{:S(2)}) copy-start(bf16[1020,256]{0,1:T(8,128)(2,1)} %get-tuple-element.416) | copy-start | bytes 1566724 | tf_op jit(solution)/shard_map/while
  379.6 8.6 %copy-start = (bf16[4,1020,1020]{1,2,0:T(8,128)(2,1)S(1)}, bf16[4,1020,1020]{1,2,0:T(8,128)(2,1)}, u32[]{:S(2)}) copy-start(bf16[4,1020,1020]{1,2,0:T(8,128)(2,1)} %multiply_convert_fusion.3) | copy-start | bytes 24969604 | tf_op jit(solution)/shard_map/while
  379.6 8.6 %copy-start.1 = (bf16[1020,256]{0,1:T(8,128)(2,1)S(1)}, bf16[1020,256]{0,1:T(8,128)(2,1)}, u32[]{:S(2)}) copy-start(bf16[1020,256]{0,1:T(8,128)(2,1)} %get-tuple-element.416) | copy-start | bytes 1566724 | tf_op jit(solution)/shard_map/while
  416.7 295.8 %all-gather.5.cloned.1.call-start = ((), (), s32[]{:S(2)}) async-start(), calls=%async_computation.1 | async-start | bytes 1081344 | tf_op jit(solution)/shard_map/all_gather | solution.py:227
  423.5 8.5 %copy-start.13 = (f32[256,256]{1,0:T(8,128)S(1)}, f32[256,256]{1,0:T(8,128)}, u32[]{:S(2)}) copy-start(f32[256,256]{1,0:T(8,128)} %param.29) | copy-start | bytes 786436
  423.5 12.1 %copy-start.15 = (f32[256,1024]{1,0:T(8,128)S(1)}, f32[256,1024]{1,0:T(8,128)}, u32[]{:S(2)}) copy-start(f32[256,1024]{1,0:T(8,128)} %param.30) | copy-start | bytes 3145732
  442.6 115.9 %copy-start.36 = (f32[6144]{0:T(1024)S(1)}, f32[6144]{0:T(1024)}, u32[]{:S(2)}) copy-start(f32[6144]{0:T(1024)} %param.34) | copy-start | bytes 73732
  442.6 119.9 %copy-start.33 = (f32[8192]{0:T(1024)S(1)}, f32[8192]{0:T(1024)}, u32[]{:S(2)}) copy-start(f32[8192]{0:T(1024)} %param.40) | copy-start | bytes 98308
  442.6 119.8 %copy-start.34 = (f32[8192]{0:T(1024)S(1)}, f32[8192]{0:T(1024)}, u32[]{:S(2)}) copy-start(f32[8192]{0:T(1024)} %param.41) | copy-start | bytes 98308
  606.7 104.5 %copy-start.48 = (f32[1024]{0:T(1024)}, f32[1024]{0:T(1024)S(1)}, u32[]{:S(2)}) copy-start(f32[1024]{0:T(1024)S(1)} %get-tuple-element.253) | copy-start | bytes 12292
  606.7 105.1 %copy-start.41 = (f32[8,256]{1,0:T(8,128)}, f32[8,256]{1,0:T(8,128)S(1)}, u32[]{:S(2)}) copy-start(f32[8,256]{1,0:T(8,128)S(1)} %get-tuple-element.252) | copy-start | bytes 24580
  609.4 110.1 %all-gather.3.cloned.1.call-start = ((), (), s32[]{:S(2)}) async-start(), calls=%async_computation | async-start | bytes 1081344 | tf_op jit(solution)/shard_map/all_gather | solution.py:227
  625.8 85.4 %copy-start.45 = (f32[1024]{0:T(1024)S(1)}, f32[1024]{0:T(1024)}, u32[]{:S(2)}) copy-start(f32[1024]{0:T(1024)} %param.33) | copy-start | bytes 12292
  625.8 85.4 %copy-start.46 = (f32[1024]{0:T(1024)S(1)}, f32[1024]{0:T(1024)}, u32[]{:S(2)}) copy-start(f32[1024]{0:T(1024)} %param.45) | copy-start | bytes 12292
  625.8 85.4 %copy-start.47 = (f32[1024]{0:T(1024)S(1)}, f32[1024]{0:T(1024)}, u32[]{:S(2)}) copy-start(f32[1024]{0:T(1024)} %param.44) | copy-start | bytes 12292
  625.8 86.1 %copy-start.35 = (f32[8,256]{1,0:T(8,128)S(1)}, f32[8,256]{1,0:T(8,128)}, u32[]{:S(2)}) copy-start(f32[8,256]{1,0:T(8,128)} %param.32) | copy-start | bytes 24580
  625.8 86.1 %copy-start.39 = (f32[8,256]{1,0:T(8,128)S(1)}, f32[8,256]{1,0:T(8,128)}, u32[]{:S(2)}) copy-start(f32[8,256]{1,0:T(8,128)} %param.43) | copy-start | bytes 24580
  625.8 86.1 %copy-start.40 = (f32[8,256]{1,0:T(8,128)S(1)}, f32[8,256]{1,0:T(8,128)}, u32[]{:S(2)}) copy-start(f32[8,256]{1,0:T(8,128)} %param.42) | copy-start | bytes 24580
  668.9 52.0 %copy-start.23 = (f32[256,256]{1,0:T(8,128)}, f32[256,256]{1,0:T(8,128)S(1)}, u32[]{:S(2)}) copy-start(f32[256,256]{1,0:T(8,128)S(1)} %reshape.575) | copy-start | bytes 786436
  709.8 12.1 %copy-start.22 = (f32[256,768]{1,0:T(8,128)}, f32[256,768]{1,0:T(8,128)S(1)}, u32[]{:S(2)}) copy-start(f32[256,768]{1,0:T(8,128)S(1)} %reshape.574) | copy-start | bytes 2359300
  714.0 7.9 %copy-start.18 = (f32[1024,256]{1,0:T(8,128)}, f32[1024,256]{1,0:T(8,128)S(1)}, u32[]{:S(2)}) copy-start(f32[1024,256]{1,0:T(8,128)S(1)} %reshape.577) | copy-start | bytes 3145732
  (32 other events, 119.8 us)
Sparse Core Ops, SparseCore 0:
  416.8 141.6 all-reduce.3
  609.5 53.5 all-gather.4
  666.9 52.5 all-gather.2
where the time goes:
time: 740 us; the launch traced here: 729 us
  matrix products  248 us (34%)
  other arithmetic  130 us (18%)
  blocking collectives  120 us (16%)
  waiting for transfers between devices  110 us (15%)
  local copies, waits for them, and re-layouts  92.1 us (12%)
  between operations  20.3 us (3%)
  loops' own time  9.27 us (1%)
    psum x1, waiting for transfers between devices, on_device(): lax.psum((g_in, g_out, g_up, g_down, g_vec, g_bias), 'dp')  106 us
    all_gather x2, blocking collectives, on_device(): gathered = lax.all_gather(fresh_shares, 'dp', axis=0, tiled=True)  80.1 us
    dot_general x8, matrix products, scores_of(): jnp.einsum('qhd,khd->hqk', query, keys, preferred_element_type=jnp.float32)  59.7 us
    dot_general x1, matrix products, on_device(): pre = jnp.dot(h_two, w_up, preferred_element_type=jnp.float32) + ffn_bias  42.1 us
    convert_element_type x4, other arithmetic, attend_back(): d_score = (prob * (d_prob - delta)).astype(jnp.bfloat16)  41.4 us
    psum x1, blocking collectives, on_device(): lax.psum((g_in, g_out, g_up, g_down, g_vec, g_bias), 'dp')  39.5 us
    dot_general x4, matrix products, attend_back(): jnp.einsum('hqk,qhd->khd', prob.astype(jnp.bfloat16), d_heads, preferred_...  34.3 us
    dot_general x4, matrix products, by_transpose(): lax.dot_general(left, right, (((1,), (1,)), ((), ())), preferred_element_...  31.1 us
  transfers between devices with their start and end apart: 3, of which 2 were waited for; matrix products, arithmetic and copies ran while one was open for 8% of the time, Pallas kernels for 0%

commit v1 on v0

v1 whole, which is shorter than its diff:
```python
import functools
import math

import jax
import jax.numpy as jnp
from jax import lax
from jax.experimental import pallas as pl
from jax.experimental.pallas import tpu as pltpu
from jax.sharding import PartitionSpec as P

HEADS = 4
FRAME = 17
STEP = 10

EPS_NORM = 1e-05
EPS_ADAM = 1e-06
BETA = 0.5
DECAY = 0.01
RATE = 0.5
RATE_VEC = 0.2

TILE = 256
QT = 128
SPAN = 384
LEAD = 16
REACH = 16
BIG = 1e30

f32 = jnp.float32
bf16 = jnp.bfloat16


def dot(a, b):
    return jnp.dot(a, b, preferred_element_type=f32)


def dot_nt(a, b):
    return lax.dot_general(a, b, (((1,), (1,)), ((), ())), preferred_element_type=f32)


def normalize(x):
    inv = 1.0 / x.shape[1]
    center = x - jnp.sum(x, axis=1, keepdims=True) * inv
    rstd = lax.rsqrt(jnp.sum(center * center, axis=1, keepdims=True) * inv + EPS_NORM)
    return center * rstd, rstd


def norm_back(dy, gain, n, rstd):
    inv = 1.0 / n.shape[1]
    e = dy * gain
    mean_e = jnp.sum(e, axis=1, keepdims=True) * inv
    mean_en = jnp.sum(e * n, axis=1, keepdims=True) * inv
    return rstd * (e - mean_e - n * mean_en)


def gelu_parts(x):
    den = 1.0 + jnp.abs(x) * (0.3275911 / math.sqrt(2.0))
    t = pl.reciprocal(den, approx=True)
    t = t * (2.0 - den * t)
    bell = jnp.exp(x * x * -0.5)
    poly = 0.5 * 1.061405429
    for c in (-1.453152027, 1.421413741, -0.284496736, 0.254829592):
        poly = poly * t + 0.5 * c
    tail = poly * t * bell
    cdf = jnp.where(x < 0.0, tail, 1.0 - tail)
    return x * cdf, cdf + x * (bell * (1.0 / math.sqrt(2.0 * math.pi)))


def fold8(x):
    return jnp.sum(x.reshape(x.shape[0] // 8, 8, x.shape[1]), axis=0)


def local_kernel(
    frames_ref, x_hbm, cot_hbm, pin_ref, pout_ref, pup_ref, pdown_ref, vec_ref, bias_ref,
    bo_hbm, gi_hbm, ga_ref, gup_ref, gdown_ref,
    xs, cs, bos, qs, ks, vs, dq, dk, dv, dms, lse, dka, dva, turned, win, wout, wup, wdown, gdt, sums, bsum, sems,
):
    rows, width = x_hbm.shape
    padded = xs.shape[0]
    steps = padded // TILE
    pairs = width // 128
    hidden_width = pup_ref.shape[1]
    micro, packed = frames_ref.shape

    x_in = pltpu.make_async_copy(x_hbm, xs.at[pl.ds(0, rows)], sems.at[0])
    c_in = pltpu.make_async_copy(cot_hbm, cs.at[pl.ds(0, rows)], sems.at[1])
    x_in.start()
    c_in.start()

    win[...] = pin_ref[...].astype(bf16)
    wout[...] = pout_ref[...].astype(bf16)
    wup[...] = pup_ref[...].astype(bf16)
    wdown[...] = pdown_ref[...].astype(bf16)
    gap = padded - rows
    if gap:
        xs[pl.ds(rows, gap)] = jnp.zeros((gap, width), bf16)
        cs[pl.ds(rows, gap)] = jnp.zeros((gap, width), f32)
        dq[pl.ds(rows, gap)] = jnp.zeros((gap, width), bf16)
    for ref in (qs, ks, vs, dms):
        ref[pl.ds(padded, SPAN)] = jnp.zeros((SPAN, width), bf16)
    for ref in (ga_ref, gup_ref, gdt, sums, bsum):
        ref[...] = jnp.zeros_like(ref)
    x_in.wait()

    def tile_at(i):
        return pl.ds(pl.multiple_of(i * TILE, TILE), TILE)

    gain_one, shift_one = vec_ref[3:4, :], vec_ref[4:5, :]
    gain_two, shift_two = vec_ref[5:6, :], vec_ref[6:7, :]

    def project(i, _):
        at = tile_at(i)
        n, _r = normalize(xs[at].astype(f32))
        h = (n * gain_one + shift_one).astype(bf16)
        q = dot(h, win[:, :width]) + vec_ref[0:1, :]
        qs[at] = q.astype(bf16) * jnp.array(0.125, bf16)
        ks[at] = dot(h, win[:, width : 2 * width]).astype(bf16)
        vs[at] = (dot(h, win[:, 2 * width :]) + vec_ref[1:2, :]).astype(bf16)
        return 0

    lax.fori_loop(0, steps, project, 0)

    first_head = lax.broadcasted_iota(jnp.int32, (1, 128), 1) < 64
    keep0 = first_head.astype(f32).astype(bf16)
    keep1 = 1.0 - keep0

    def depth(j):
        return min(QT * (j + 1) + REACH, SPAN)

    def filled(j):
        return min(-(-depth(j) // 128) * 128, SPAN)

    def limits(j, off, stop):
        t = QT * j + (lax.broadcasted_iota(jnp.int32, (1, 2 * QT), 1) & (QT - 1))
        frame = ((t - off) * 241) >> 12
        end = jnp.minimum(off + FRAME * (frame + 1), stop)
        return end, (t >= off) & (t < stop)

    def hide(score, j, off, end):
        m = score.shape[0]
        edge = QT * j
        row = lambda lo, hi: lo + lax.broadcasted_iota(jnp.int32, (hi - lo, 2 * QT), 0)
        if j == 0:
            s = row(0, m)
            return jnp.where((s >= off) & (s < end), score, -BIG)
        return jnp.concatenate(
            [
                jnp.where(row(0, LEAD) >= off, score[:LEAD], -BIG),
                score[LEAD:edge],
                jnp.where(row(edge, m) < end, score[edge:], -BIG),
            ],
            axis=0,
        )

    def heads_apart(block):
        return jnp.concatenate([block * keep0, block * keep1], axis=0)

    def fill(block, j):
        short = filled(j) - depth(j)
        if not short:
            return block
        return jnp.concatenate([block, jnp.zeros((short, block.shape[1]), block.dtype)], axis=0)

    def heads_back(out):
        both = jnp.concatenate([out[:64, :QT], out[64:, QT:]], axis=0)
        return both.T

    def put(ref, at_row, lanes, value, off):
        lead = pl.ds(pl.multiple_of(at_row, LEAD), LEAD)
        own = lax.broadcasted_iota(jnp.int32, (LEAD, 128), 0) >= off
        old = ref[lead, lanes].astype(f32)
        ref[lead, lanes] = jnp.where(own, value[:LEAD], old).astype(bf16)
        rest = value.shape[0] - LEAD
        ref[pl.ds(pl.multiple_of(at_row + LEAD, LEAD), rest), lanes] = value[LEAD:].astype(bf16)

    def window(i, start):
        length = frames_ref[i // packed, i % packed] * FRAME
        off = start & (LEAD - 1)
        return pl.multiple_of(start - off, LEAD), off, off + length, start + length

    def attend(i, start):
        base, off, stop, after = window(i, start)
        for p in range(pairs):
            turned[p] = vs[pl.ds(base, SPAN), 128 * p : 128 * (p + 1)].T

        def step(j):
            end, valid = limits(j, off, stop)
            m = depth(j)
            for p in range(pairs):
                lanes = slice(128 * p, 128 * (p + 1))
                query = heads_apart(qs[pl.ds(pl.multiple_of(base + QT * j, LEAD), QT), lanes])
                score = hide(dot_nt(ks[pl.ds(base, m), lanes], query), j, off, end)
                peak = jnp.max(score, axis=0, keepdims=True)
                weight = jnp.exp(score - peak)
                total = jnp.sum(weight, axis=0, keepdims=True)
                prob = (weight * jnp.where(valid, 1.0 / total, 0.0)).astype(bf16)
                row = pairs * j + p
                lse[i, row : row + 1, :] = jnp.where(valid, peak + jnp.log(total), BIG)
                out = dot(turned[p, :, : filled(j)], fill(prob, j))
                block = heads_back(out)
                if j == 0:
                    put(dq, base, lanes, block, off)
                else:
                    dq[pl.ds(pl.multiple_of(base + QT * j, LEAD), QT), lanes] = block.astype(bf16)

        step(0)
        for j in range(1, SPAN // QT):
            pl.when(stop > QT * j)(functools.partial(step, j))
        return after

    lax.fori_loop(0, micro * packed, attend, 0)

    c_in.wait()

    def feed_forward(i, _):
        at = tile_at(i)
        mixed = dq[at]
        resid = xs[at].astype(f32) + dot(mixed, wout[...]) + vec_ref[2:3, :]
        n, rstd = normalize(resid)
        h = (n * gain_two + shift_two).astype(bf16)
        cot = cs[at]
        low = cot.astype(bf16)
        h_t, low_t = h.T, low.T
        feed = jnp.zeros((TILE, width), f32)
        d_h = jnp.zeros((TILE, width), f32)
        for c in range(0, hidden_width, 256):
            cols = slice(c, c + 256)
            pre = dot(h, wup[:, cols]) + bias_ref[:, cols]
            act, slope = gelu_parts(pre)
            act = act.astype(bf16)
            feed += dot(act, wdown[cols, :])
            d_pre = (dot_nt(low, wdown[cols, :]) * slope).astype(bf16)
            d_h += dot_nt(d_pre, wup[:, cols])
            gdt[:, cols] += dot(low_t, act)
            gup_ref[:, cols] += dot(h_t, d_pre)
            bsum[:, cols] += fold8(d_pre.astype(f32))
        bos[at] = (resid + feed + vec_ref[7:8, :]).astype(bf16)
        d_resid = cot + norm_back(d_h, gain_two, n, rstd)
        cs[at] = d_resid
        branch = d_resid.astype(bf16)
        sums[2] += fold8(branch.astype(f32))
        sums[5] += fold8(d_h * n)
        sums[6] += fold8(d_h)
        sums[7] += fold8(low.astype(f32))
        ga_ref[:, 3 * width : 4 * width] += dot(mixed.T, branch)
        dms[at] = dot_nt(branch, wout[...]).astype(bf16)
        return 0

    lax.fori_loop(0, steps, feed_forward, 0)
    bo_out = pltpu.make_async_copy(bos.at[pl.ds(0, rows)], bo_hbm, sems.at[2])
    bo_out.start()

    def attend_back(i, start):
        base, off, stop, after = window(i, start)
        for p in range(pairs):
            turned[p] = ks[pl.ds(base, SPAN), 128 * p : 128 * (p + 1)].T
        dka[...] = jnp.zeros_like(dka)
        dva[...] = jnp.zeros_like(dva)

        def step(j):
            end, _valid = limits(j, off, stop)
            m = depth(j)
            for p in range(pairs):
                lanes = slice(128 * p, 128 * (p + 1))
                here = pl.ds(pl.multiple_of(base + QT * j, LEAD), QT)
                query = heads_apart(qs[here, lanes])
                d_out = heads_apart(dms[here, lanes])
                row = pairs * j + p
                score = hide(dot_nt(ks[pl.ds(base, m), lanes], query), j, off, end)
                prob = jnp.exp(score - lse[i, row : row + 1, :])
                d_prob = dot_nt(vs[pl.ds(base, m), lanes], d_out)
                delta = jnp.sum(prob * d_prob, axis=0, keepdims=True)
                d_score = (prob * (d_prob - delta)).astype(bf16)
                dva[:m, lanes] += dot(prob.astype(bf16), d_out)
                dka[:m, lanes] += dot(d_score, query)
                out = dot(turned[p, :, : filled(j)], fill(d_score, j))
                block = heads_back(out) * 0.125
                if j == 0:
                    put(dq, base, lanes, block, off)
                else:
                    dq[here, lanes] = block.astype(bf16)

        step(0)
        for j in range(1, SPAN // QT):
            pl.when(stop > QT * j)(functools.partial(step, j))
        for p in range(pairs):
            lanes = slice(128 * p, 128 * (p + 1))
            put(dk, base, lanes, dka[:, lanes], off)
            put(dv, base, lanes, dva[:, lanes], off)
        return after

    lax.fori_loop(0, micro * packed, attend_back, 0)
    if gap:
        for ref in (dq, dk, dv):
            ref[pl.ds(rows, gap)] = jnp.zeros((gap, width), bf16)

    def project_back(i, _):
        at = tile_at(i)
        n, rstd = normalize(xs[at].astype(f32))
        h_t = (n * gain_one + shift_one).astype(bf16).T
        d_h = jnp.zeros((TILE, width), f32)
        for b, ref in enumerate((dq, dk, dv)):
            cols = slice(b * width, (b + 1) * width)
            block = ref[at]
            d_h += dot_nt(block, win[:, cols])
            ga_ref[:, cols] += dot(h_t, block)
            if b != 1:
                sums[b // 2] += fold8(block.astype(f32))
        sums[3] += fold8(d_h * n)
        sums[4] += fold8(d_h)
        cs[at] = cs[at] + norm_back(d_h, gain_one, n, rstd)
        return 0

    lax.fori_loop(0, steps, project_back, 0)
    gi_out = pltpu.make_async_copy(cs.at[pl.ds(0, rows)], gi_hbm, sems.at[3])
    gi_out.start()
    for c in range(0, hidden_width, 256):
        gdown_ref[c : c + 256, :] = gdt[:, c : c + 256].T
    vec = jnp.sum(sums[...], axis=1)
    tail = 4 * width
    for b in range(width // 128):
        ga_ref[8 * b : 8 * b + 8, tail : tail + 128] = vec[:, 128 * b : 128 * (b + 1)]
    bias = jnp.sum(bsum[...], axis=0, keepdims=True)
    for b in range(hidden_width // 128):
        row = 8 * (width // 128) + b
        ga_ref[row : row + 1, tail : tail + 128] = bias[:, 128 * b : 128 * (b + 1)]
    bo_out.wait()
    gi_out.wait()


def local_grads(inputs, frames, cotangent, proj_in, proj_out, ffn_up, ffn_down, vectors, ffn_bias):
    rows, width = inputs.shape
    hidden_width = ffn_up.shape[1]
    padded = -(-rows // TILE) * TILE
    wide = padded + SPAN
    pairs = width // 128
    vmem = pl.BlockSpec(memory_space=pltpu.VMEM)
    hbm = pl.BlockSpec(memory_space=pl.ANY)
    return pl.pallas_call(
        local_kernel,
        out_shape=(
            jax.ShapeDtypeStruct((rows, width), bf16),
            jax.ShapeDtypeStruct((rows, width), f32),
            jax.ShapeDtypeStruct((width, 4 * width + 128), f32),
            jax.ShapeDtypeStruct((width, hidden_width), f32),
            jax.ShapeDtypeStruct((hidden_width, width), f32),
        ),
        in_specs=[pl.BlockSpec(memory_space=pltpu.SMEM), hbm, hbm] + [vmem] * 6,
        out_specs=(hbm, hbm, vmem, vmem, vmem),
        scratch_shapes=[
            pltpu.VMEM((padded, width), bf16),
            pltpu.VMEM((padded, width), f32),
            pltpu.VMEM((padded, width), bf16),
            *[pltpu.VMEM((wide, width), bf16)] * 7,
            pltpu.VMEM((frames.size, 8, 2 * QT), f32),
            pltpu.VMEM((SPAN, width), f32),
            pltpu.VMEM((SPAN, width), f32),
            pltpu.VMEM((pairs, 128, SPAN), bf16),
            pltpu.VMEM((width, 3 * width), bf16),
            pltpu.VMEM((width, width), bf16),
            pltpu.VMEM((width, hidden_width), bf16),
            pltpu.VMEM((hidden_width, width), bf16),
            pltpu.VMEM((width, hidden_width), f32),
            pltpu.VMEM((8, 8, width), f32),
            pltpu.VMEM((8, hidden_width), f32),
            pltpu.SemaphoreType.DMA((4,)),
        ],
        compiler_params=pltpu.CompilerParams(vmem_limit_bytes=60 * 1024 * 1024),
        name="local_grads",
    )(frames, inputs, cotangent, proj_in, proj_out, ffn_up, ffn_down, vectors, ffn_bias.reshape(1, hidden_width))


def own_share(array, length, place):
    return lax.dynamic_slice_in_dim(array.reshape(-1), place * length, length)


def shard_steps(shares, firsts, seconds, weights, place, fix):
    results = []
    for share, first, second, weight in zip(shares, firsts, seconds, weights):
        momentum = BETA * first + (1.0 - BETA) * share
        variance = BETA * second + (1.0 - BETA) * share * share
        w_share = own_share(weight, first.shape[0], place)
        advance = momentum / fix / (jnp.sqrt(variance / fix) + EPS_ADAM) + DECAY * w_share
        results.append((momentum, variance, advance, w_share))
    return results


def adam_plain(weight, grad, first, second, fix):
    momentum = BETA * first + (1.0 - BETA) * grad
    variance = BETA * second + (1.0 - BETA) * grad * grad
    fresh = weight - RATE_VEC * (momentum / fix) / (jnp.sqrt(variance / fix) + EPS_ADAM)
    return (momentum, variance, fresh)


def on_device(
    inputs,
    frames,
    cotangent,
    proj_in,
    proj_out,
    ffn_up,
    ffn_down,
    vectors,
    ffn_bias,
    first_in,
    second_in,
    first_out,
    second_out,
    first_up,
    second_up,
    first_down,
    second_down,
    first_vec,
    second_vec,
    first_bias,
    second_bias,
):
    bf = jnp.bfloat16
    width = inputs.shape[1]
    block_out, grad_inputs, g_a, g_up, g_down = local_grads(
        inputs, frames, cotangent, proj_in, proj_out, ffn_up, ffn_down, vectors, ffn_bias
    )
    g_in = g_a[:, : 3 * width]
    g_out = g_a[:, 3 * width : 4 * width]
    extra = g_a[:24, 4 * width :]
    g_vec = jnp.concatenate([extra[:8], extra[8:16]], axis=1)
    g_bias = extra[16:24].reshape(-1)
    fix = 1.0 - BETA**STEP
    place = lax.axis_index("dp")
    weights = (proj_in, proj_out, ffn_up, ffn_down)
    firsts = (first_in, first_out, first_up, first_down)
    seconds = (second_in, second_out, second_up, second_down)
    g_in, g_out, g_up, g_down, g_vec, g_bias = lax.psum(
        (g_in, g_out, g_up, g_down, g_vec, g_bias), "dp"
    )
    shares = [
        own_share(full, first.shape[0], place)
        for full, first in zip((g_in, g_out, g_up, g_down), firsts)
    ]
    updated = shard_steps(shares, firsts, seconds, weights, place, fix)
    squares = jnp.stack([jnp.sum(entry[2] * entry[2]) for entry in updated])
    squares = lax.psum(squares, "dp")
    w_norms = jnp.stack([jnp.sqrt(jnp.sum(weight * weight)) for weight in weights])
    u_norms = jnp.sqrt(squares)
    fresh_shares = tuple(
        (
            entry[3] - RATE * (w_norms[index] / (u_norms[index] + EPS_ADAM)) * entry[2]
            for index, entry in enumerate(updated)
        )
    )
    gathered = lax.all_gather(fresh_shares, "dp", axis=0, tiled=True)
    fresh = [full.reshape(weight.shape) for full, weight in zip(gathered, weights)]
    m_vec, v_vec, w_vec = adam_plain(vectors, g_vec, first_vec, second_vec, fix)
    m_bias, v_bias, w_bias = adam_plain(ffn_bias, g_bias, first_bias, second_bias, fix)
    norms = jnp.stack([w_norms, u_norms], axis=1)
    return (
        block_out,
        grad_inputs,
        shares[0],
        shares[1],
        shares[2],
        shares[3],
        g_vec,
        g_bias,
        updated[0][0],
        updated[0][1],
        fresh[0],
        fresh[0].astype(bf),
        updated[1][0],
        updated[1][1],
        fresh[1],
        fresh[1].astype(bf),
        updated[2][0],
        updated[2][1],
        fresh[2],
        fresh[2].astype(bf),
        updated[3][0],
        updated[3][1],
        fresh[3],
        fresh[3].astype(bf),
        m_vec,
        v_vec,
        w_vec,
        m_bias,
        v_bias,
        w_bias,
        norms,
    )


def solution(mesh):
    placed = (
        P("dp", None),
        P("dp", None),
        P("dp", None),
        P(),
        P(),
        P(),
        P(),
        P(),
        P(),
        P("dp"),
        P("dp"),
        P("dp"),
        P("dp"),
        P("dp"),
        P("dp"),
        P("dp"),
        P("dp"),
        P(),
        P(),
        P(),
        P(),
    )
    return jax.shard_map(
        on_device,
        mesh=mesh,
        in_specs=placed,
        out_specs=(
            P("dp", None),
            P("dp", None),
            P("dp"),
            P("dp"),
            P("dp"),
            P("dp"),
            P(),
            P(),
            P("dp"),
            P("dp"),
            P(),
            P(),
            P("dp"),
            P("dp"),
            P(),
            P(),
            P("dp"),
            P("dp"),
            P(),
            P(),
            P("dp"),
            P("dp"),
            P(),
            P(),
            P(),
            P(),
            P(),
            P(),
            P(),
            P(),
            P(),
        ),
        check_vma=False,
    )
```

time: 740 us -> 460 us (0.62); the launches traced: 729 us -> 460 us
  matrix products: 248 us -> 0 us
  Pallas kernels: 0 us -> 131 us
  other arithmetic: 130 us -> 20.7 us
  local copies, waits for them, and re-layouts: 92.1 us -> 16.2 us
  waiting for transfers between devices: 110 us -> 153 us
  loops' own time: 9.27 us -> 0 us
    dot_general x40 -> x0, matrix products: 248 us -> none  [the longest x8 59.7 us: scores_of(): jnp.einsum('qhd,khd->hqk', query, keys, preferred_element_type=jnp.float32)]
    pallas_call x0 -> x1, Pallas kernels: none -> 131 us  [local_grads(): pl.pallas_call(local_kernel, out_shape=(jax.ShapeDtypeStruct((rows, width...]
    reduce_sum x20 -> x0, other arithmetic: 45.9 us -> none  [the longest x4 15.8 us: attend(): total = jnp.sum(weight, axis=-1, keepdims=True)]
    convert_element_type x4 -> x0, other arithmetic: 41.4 us -> none  [attend_back(): d_score = (prob * (d_prob - delta)).astype(jnp.bfloat16)]
    psum x1, waiting for transfers between devices: 106 us -> 138 us  [on_device(): lax.psum((g_in, g_out, g_up, g_down, g_vec, g_bias), 'dp')]
    while x18 -> x0, local copies, waits for them, and re-layouts: 17.3 us -> none  [the longest x1 8.66 us: on_device(): lax.map(attend_back, (joined_blocks, frames, logsum, d_mixed.reshape(bloc...]
    reshape x4 -> x1, local copies, waits for them, and re-layouts: 14.9 us -> 0.7 us  [on_device(): g_bias = extra[16:24].reshape(-1)]
    and x8 -> x0, other arithmetic: 12.6 us -> none  [allowed(): (owner[:, None] == owner[None, :]) & (frame[:, None] >= frame[None, :])]
  transfers between devices with their start and end apart: 3 -> 3, of which waited for: 2 -> 2; matrix products, arithmetic and copies ran while one was open for 8% -> 3% of each run, Pallas kernels for 0% -> 0%
where the time goes in v1:
time: 460 us
  waiting for transfers between devices  153 us (33%)
  Pallas kernels  131 us (28%)
  blocking collectives  119 us (26%)
  other arithmetic  20.7 us (4%)
  between operations  19.6 us (4%)
  local copies, waits for them, and re-layouts  16.2 us (4%)
    psum x1, waiting for transfers between devices, on_device(): lax.psum((g_in, g_out, g_up, g_down, g_vec, g_bias), 'dp')  138 us
    pallas_call x1, Pallas kernels, local_grads(): pl.pallas_call(local_kernel, out_shape=(jax.ShapeDtypeStruct((rows, width...  131 us
    all_gather x2, blocking collectives, on_device(): gathered = lax.all_gather(fresh_shares, 'dp', axis=0, tiled=True)  79.6 us
    psum x1, blocking collectives, on_device(): lax.psum((g_in, g_out, g_up, g_down, g_vec, g_bias), 'dp')  39.5 us
    all_gather x2, waiting for transfers between devices, on_device(): gathered = lax.all_gather(fresh_shares, 'dp', axis=0, tiled=True)  15.4 us
  transfers between devices with their start and end apart: 3, of which 2 were waited for; matrix products, arithmetic and copies ran while one was open for 3% of the time, Pallas kernels for 0%

profile of v1, /device:TPU:0, one launch (start us, length us, event | category | flops | bytes accessed | tf_op | source)
XLA Modules:
  0.0 460.0 jit_solution(18418900724279427282)
XLA Ops:
  7.3 131.0 %local_grads.1 = (bf16[4080,256]{1,0:T(8,128)(2,1)}, f32[4080,256]{1,0:T(8,128)}, f32[256,1152]{1,0:T(8,128)}, f32[256,1024]{1,0:T(8,128)}, f32[1024,256]{1,0:T(8,128)}) custom-call(s32[4,4]{1,0:T(4,128)} %frames_ref.1, bf16[4080,256]{1,0:T(8,128)(2,1)} %x_hbm.1, f32[4080,256]{1,0:T(8,128)} %cot_hbm.1, f32[256,768]{1,0:T(8,128)} %pin_ref.1, ...), custom_call_target="tpu_custom_call" | custom-call | tf_op jit(solution)/shard_map/local_grads/pallas_call | solution.py:339
  138.3 1.3 slice.31
  139.6 1.0 slice_bitcast_fusion
  140.6 0.9 reshape.113
  141.5 0.8 copy.52
  142.3 1.2 copy.53
  143.5 1.5 copy.54
  145.1 1.0 copy-done.2
  146.1 0.9 reshape.118
  147.1 1.2 copy.56
  148.3 1.5 copy.57
  150.0 0.9 multiply_reduce_fusion
  151.5 0.7 slice_bitcast_fusion.1
  152.2 137.9 %all-reduce.4.cloned.1.call-done = (f32[196608]{0:T(1024)}, f32[65536]{0:T(1024)}, f32[262144]{0:T(1024)}, f32[262144]{0:T(1024)}) async-done(((f32[196608]{0:T(1024)}, f32[65536]{0:T(1024)}, f32[262144]{0:T(1024)}, f32[262144]{0:T(1024)}), (f32[196608]{0:T(1024)}, f32[65536]{0:T(1024)}, f32[262144]{0:T(1024)}, f32[262144]{0:T(1024)})) %all-reduce.4.cloned.1.call-update) | async-done | bytes 3145744 | tf_op jit(solution)/shard_map/psum | solution.py:433
  290.1 1.9 multiply_reduce_fusion.7
  292.0 2.0 multiply_reduce_fusion.6
  294.1 2.1 multiply_reduce_fusion.4
  296.2 2.7 pad_maximum_fusion.2
  298.8 39.5 %all-reduce = (f32[8,256]{1,0:T(8,128)S(1)}, f32[1024]{0:T(1024)S(1)}, f32[4]{0:T(128)S(1)}) all-reduce(f32[8,256]{1,0:T(8,128)S(1)} %pad_maximum_fusion, f32[1024]{0:T(1024)S(1)} %get-tuple-element.74, f32[4]{0:T(128)S(1)} %pad_maximum_fusion.2), channel_id=1, replica_groups=mesh['dp'=32] {'dp'}, use_global_device_ids=true, to_apply=%region_4.0 | all-reduce | flops 3076 | bytes 24608 | tf_op jit(solution)/shard_map/psum | solution.py:433
  339.6 1.4 multiply_subtract_fusion
  341.1 0.9 multiply_reduce_fusion.1
  343.3 1.4 multiply_subtract_fusion.1
  346.1 0.8 multiply_reduce_fusion.2
  348.4 40.8 %all_gather.13 = f32[65536]{0:T(1024)S(1)} all-gather(f32[2048]{0:T(1024)S(1)} %multiply_subtract_fusion.3), channel_id=1, replica_groups=mesh['dp'=32] {'dp'}, dimensions={0}, use_global_device_ids=true | all-gather | bytes 270336 | tf_op jit(solution)/shard_map/all_gather | solution.py:451
  390.7 0.8 multiply_subtract_fusion.2
  391.4 38.8 %all_gather.12 = f32[196608]{0:T(1024)S(1)} all-gather(f32[6144]{0:T(1024)S(1)} %multiply_subtract_fusion.2), channel_id=1, replica_groups=mesh['dp'=32] {'dp'}, dimensions={0}, use_global_device_ids=true | all-gather | bytes 811008 | tf_op jit(solution)/shard_map/all_gather | solution.py:451
  430.4 0.8 convert_element_type.12
  433.1 1.5 reshape.125
  434.6 0.9 convert_element_type.15
  435.6 15.4 %all-gather.3.cloned.1.call-done = f32[262144]{0:T(1024)} async-done(((f32[8192]{0:T(1024)}), f32[262144]{0:T(1024)}) %all-gather.3.cloned.1.call-update) | async-done | bytes 1048592 | tf_op jit(solution)/shard_map/all_gather | solution.py:451
  451.0 1.4 reshape.124
  452.4 0.9 convert_element_type.14
  (67 shorter events, 4.7 us)
Async XLA Ops:
  7.2 282.9 %all-reduce.4.cloned.1.call-start = ((), (), s32[]{:S(2)}) async-start(), calls=%async_computation.2 | async-start | bytes 6291456 | tf_op jit(solution)/shard_map/psum | solution.py:433
  138.3 4.1 copy-start.8
  140.5 3.0 copy-start.7
  145.0 1.1 copy-start.2
  145.0 2.1 copy-start.1
  145.0 3.2 copy-start
  145.1 288.0 %all-gather.5.cloned.1.call-start = ((), (), s32[]{:S(2)}) async-start(), calls=%async_computation.1 | async-start | bytes 1081344 | tf_op jit(solution)/shard_map/all_gather | solution.py:451
  147.1 2.7 copy-start.6
  148.2 141.9 %copy-start.19 = (f32[2048]{0:T(1024)S(1)}, f32[2048]{0:T(1024)}, u32[]{:S(2)}) copy-start(f32[2048]{0:T(1024)} %param.32) | copy-start | bytes 24580
  148.2 141.9 %copy-start.20 = (f32[2048]{0:T(1024)S(1)}, f32[2048]{0:T(1024)}, u32[]{:S(2)}) copy-start(f32[2048]{0:T(1024)} %param.33) | copy-start | bytes 24580
  148.2 145.8 %copy-start.11 = (f32[8192]{0:T(1024)S(1)}, f32[8192]{0:T(1024)}, u32[]{:S(2)}) copy-start(f32[8192]{0:T(1024)} %param.36) | copy-start | bytes 98308
  148.3 145.8 %copy-start.12 = (f32[8192]{0:T(1024)S(1)}, f32[8192]{0:T(1024)}, u32[]{:S(2)}) copy-start(f32[8192]{0:T(1024)} %param.37) | copy-start | bytes 98308
  148.3 145.8 %copy-start.13 = (f32[8192]{0:T(1024)S(1)}, f32[8192]{0:T(1024)}, u32[]{:S(2)}) copy-start(f32[8192]{0:T(1024)} %param.35) | copy-start | bytes 98308
  148.3 145.8 %copy-start.14 = (f32[8192]{0:T(1024)S(1)}, f32[8192]{0:T(1024)}, u32[]{:S(2)}) copy-start(f32[8192]{0:T(1024)} %param.34) | copy-start | bytes 98308
  338.3 93.5 %copy-start.23 = (f32[1024]{0:T(1024)}, f32[1024]{0:T(1024)S(1)}, u32[]{:S(2)}) copy-start(f32[1024]{0:T(1024)S(1)} %get-tuple-element.42) | copy-start | bytes 12292
  338.3 94.1 %copy-start.18 = (f32[8,256]{1,0:T(8,128)}, f32[8,256]{1,0:T(8,128)S(1)}, u32[]{:S(2)}) copy-start(f32[8,256]{1,0:T(8,128)S(1)} %get-tuple-element.41) | copy-start | bytes 24580
  341.0 110.0 %all-gather.3.cloned.1.call-start = ((), (), s32[]{:S(2)}) async-start(), calls=%async_computation | async-start | bytes 1081344 | tf_op jit(solution)/shard_map/all_gather | solution.py:451
  389.2 45.4 %copy-start.9 = (f32[256,256]{1,0:T(8,128)}, f32[256,256]{1,0:T(8,128)S(1)}, u32[]{:S(2)}) copy-start(f32[256,256]{1,0:T(8,128)S(1)} %reshape.123) | copy-start | bytes 786436
  389.2 42.6 %copy-start.15 = (f32[1024]{0:T(1024)S(1)}, f32[1024]{0:T(1024)}, u32[]{:S(2)}) copy-start(f32[1024]{0:T(1024)} %param.29) | copy-start | bytes 12292
  389.2 42.6 %copy-start.21 = (f32[1024]{0:T(1024)S(1)}, f32[1024]{0:T(1024)}, u32[]{:S(2)}) copy-start(f32[1024]{0:T(1024)} %param.41) | copy-start | bytes 12292
  389.3 42.6 %copy-start.22 = (f32[1024]{0:T(1024)S(1)}, f32[1024]{0:T(1024)}, u32[]{:S(2)}) copy-start(f32[1024]{0:T(1024)} %param.40) | copy-start | bytes 12292
  389.3 43.2 %copy-start.10 = (f32[8,256]{1,0:T(8,128)S(1)}, f32[8,256]{1,0:T(8,128)}, u32[]{:S(2)}) copy-start(f32[8,256]{1,0:T(8,128)} %vec_ref.1) | copy-start | bytes 24580
  389.3 43.2 %copy-start.16 = (f32[8,256]{1,0:T(8,128)S(1)}, f32[8,256]{1,0:T(8,128)}, u32[]{:S(2)}) copy-start(f32[8,256]{1,0:T(8,128)} %param.39) | copy-start | bytes 24580
  389.3 43.2 %copy-start.17 = (f32[8,256]{1,0:T(8,128)S(1)}, f32[8,256]{1,0:T(8,128)}, u32[]{:S(2)}) copy-start(f32[8,256]{1,0:T(8,128)} %param.38) | copy-start | bytes 24580
  430.4 5.2 %copy-start.5 = (f32[256,768]{1,0:T(8,128)}, f32[256,768]{1,0:T(8,128)S(1)}, u32[]{:S(2)}) copy-start(f32[256,768]{1,0:T(8,128)S(1)} %reshape.122) | copy-start | bytes 2359300
  434.6 18.7 %copy-start.3 = (f32[1024,256]{1,0:T(8,128)}, f32[1024,256]{1,0:T(8,128)S(1)}, u32[]{:S(2)}) copy-start(f32[1024,256]{1,0:T(8,128)S(1)} %reshape.125) | copy-start | bytes 3145732
  452.4 1.1 copy-start.4
Sparse Core Ops, SparseCore 0:
  145.2 144.9 all-reduce.3
  341.1 53.3 all-gather.4
  398.4 52.5 all-gather.2

commit v2 on v1

--- a/solution.py
+++ b/solution.py
@@ -370,184 +370,288 @@
     )(frames, inputs, cotangent, proj_in, proj_out, ffn_up, ffn_down, vectors, ffn_bias.reshape(1, hidden_width))
 
 
-def own_share(array, length, place):
-    return lax.dynamic_slice_in_dim(array.reshape(-1), place * length, length)
-
-
-def shard_steps(shares, firsts, seconds, weights, place, fix):
-    results = []
-    for share, first, second, weight in zip(shares, firsts, seconds, weights):
-        momentum = BETA * first + (1.0 - BETA) * share
-        variance = BETA * second + (1.0 - BETA) * share * share
-        w_share = own_share(weight, first.shape[0], place)
-        advance = momentum / fix / (jnp.sqrt(variance / fix) + EPS_ADAM) + DECAY * w_share
-        results.append((momentum, variance, advance, w_share))
-    return results
-
-
-def adam_plain(weight, grad, first, second, fix):
-    momentum = BETA * first + (1.0 - BETA) * grad
-    variance = BETA * second + (1.0 - BETA) * grad * grad
-    fresh = weight - RATE_VEC * (momentum / fix) / (jnp.sqrt(variance / fix) + EPS_ADAM)
-    return (momentum, variance, fresh)
-
-
-def on_device(
-    inputs,
-    frames,
-    cotangent,
-    proj_in,
-    proj_out,
-    ffn_up,
-    ffn_down,
-    vectors,
-    ffn_bias,
-    first_in,
-    second_in,
-    first_out,
-    second_out,
-    first_up,
-    second_up,
-    first_down,
-    second_down,
-    first_vec,
-    second_vec,
-    first_bias,
-    second_bias,
-):
-    bf = jnp.bfloat16
-    width = inputs.shape[1]
-    block_out, grad_inputs, g_a, g_up, g_down = local_grads(
+def over_all(x):
+    return jnp.sum(jnp.sum(x, axis=0, keepdims=True), axis=1, keepdims=True)
+
+
+def momenta(first, second, grad):
+    return BETA * first + (1.0 - BETA) * grad, BETA * second + (1.0 - BETA) * grad * grad
+
+
+def direction(momentum, variance):
+    fix = 1.0 - BETA**STEP
+    return momentum / fix / (jnp.sqrt(variance / fix) + EPS_ADAM)
+
+
+def places(order):
+    top = len(order) - 1
+
+    def chunk_of(pos):
+        return sum((pos // (1 << (top - k))) % 2 * (1 << b) for k, b in enumerate(order))
+
+    def place_of(chunk):
+        return sum((chunk // (1 << b)) % 2 * (1 << (top - k)) for k, b in enumerate(order))
+
+    return chunk_of, place_of
+
+
+def matrix_lanes(shapes):
+    return ((0, 0), (0, shapes[0][-1]), (1, 0), (2, 0))
+
+
+def flat_rows(rows, blocks, b):
+    return pl.ds(b, rows, stride=blocks) if blocks > 1 else pl.ds(0, rows)
+
+
+def exchange_kernel(n, orders, stages, *refs):
+    sources, owns, firsts, seconds = refs[:3], refs[3:7], refs[7:11], refs[11:15]
+    full, shares = refs[15:18], refs[18:21]
+    parcels, landed, send_sems, recv_sems = refs[21:24], refs[24:27], refs[27], refs[28]
+    me = lax.axis_index("dp")
+
+    def bit(k):
+        return (me // (1 << k)) % 2
+
+    def partner(k):
+        return me + (1 - 2 * bit(k)) * (1 << k)
+
+    barrier = pltpu.get_barrier_semaphore()
+    for k in range(stages):
+        pl.semaphore_signal(barrier, inc=1, device_id=(partner(k),), device_id_type=pl.DeviceIdType.MESH)
+    pl.semaphore_wait(barrier, stages)
+
+    def region(k):
+        return n - (n >> k)
+
+    def remote(p, slot, src, dst, k):
+        return pltpu.make_async_remote_copy(
+            src_ref=src,
+            dst_ref=dst,
+            send_sem=send_sems.at[p, slot],
+            recv_sem=recv_sems.at[p, slot],
+            device_id=(partner(k),),
+            device_id_type=pl.DeviceIdType.MESH,
+        )
+
+    sent = []
+    halving = {}
+
+    def halve(p, k):
+        m = n >> (k + 1)
+        order = orders[p]
+        if k == 0:
+            away = (1 - bit(order[0])) * m
+
+            def pack(i, _):
+                parcels[p][i] = sources[p][places(order)[0](away + i)]
+                return 0
+
+            lax.fori_loop(0, m, pack, 0)
+            src = parcels[p]
+        else:
+            src = landed[p].at[pl.ds(region(k - 1) + (1 - bit(order[k])) * m, m)]
+        copy = remote(p, k, src, landed[p].at[pl.ds(region(k), m)], order[k])
+        copy.start()
+        halving[p, k] = copy
+        sent.append(copy)
+
+    def add(p, k):
+        m = n >> (k + 1)
+        order = orders[p]
+        mine = bit(order[k]) * m
+        halving[p, k].wait_recv()
+
+        def one(i, _):
+            if k == 0:
+                kept = sources[p][places(order)[0](mine + i)]
+            else:
+                kept = landed[p][region(k - 1) + mine + i]
+            at = region(k) + i
+            landed[p][at] = landed[p][at] + kept
+            return 0
+
+        lax.fori_loop(0, m, one, 0)
+
+    parts = range(len(orders))
+    for p in parts:
+        halve(p, 0)
+    for k in range(1, stages):
+        for p in parts:
+            add(p, k - 1)
+            halve(p, k)
+
+    homes = [places(order)[1](me) for order in orders]
+    matrices = matrix_lanes([own.shape for own in owns])
+    gathering = {}
+
+    def gather(p, k):
+        size = 1 << (stages - 1 - k)
+        at = pl.ds(homes[p] // size * size, size)
+        copy = remote(p, stages + k, full[p].at[at], full[p].at[at], orders[p][k])
+        copy.start()
+        gathering[p, k] = copy
+        sent.append(copy)
+
+    for p in parts:
+        add(p, stages - 1)
+        last = region(stages - 1)
+        for i, (part, lane) in enumerate(matrices):
+            if part != p:
+                continue
+            rows = sources[p].shape[1]
+            blocks = owns[i].shape[2] // 128
+            for b in range(blocks):
+                flat = flat_rows(rows, blocks, b)
+                lanes = slice(128 * b, 128 * (b + 1))
+                here = slice(lane + 128 * b, lane + 128 * (b + 1))
+                momentum, variance = momenta(firsts[i][flat, :], seconds[i][flat, :], landed[p][last, :, here])
+                full[p][homes[p], :, here] = direction(momentum, variance) + DECAY * owns[i][me, :, lanes]
+        if p == 0:
+            tail = slice(full[0].shape[2] - 128, full[0].shape[2])
+            full[0][homes[0], :, tail] = landed[0][last, :, tail]
+        shares[p][...] = landed[p][last]
+        gather(p, stages - 1)
+    for k in range(stages - 2, -1, -1):
+        for p in parts:
+            gathering[p, k + 1].wait_recv()
+            gather(p, k)
+    for p in parts:
+        gathering[p, 0].wait_recv()
+
+    for copy in sent:
+        copy.wait_send()
+
+
+def renew_kernel(n, orders, *refs):
+    full, shares = refs[:3], refs[3:6]
+    weights, firsts, seconds = refs[6:10], refs[10:14], refs[14:18]
+    vec, bias, fvec, svec, fbias, sbias = refs[18:24]
+    g_out, m_out, v_out = refs[24:28], refs[28:32], refs[32:36]
+    w_new, w_low = refs[36:40], refs[40:44]
+    gvec, gbias, mvec, vvec, wvec, mbias, vbias, wbias, norms = refs[44:53]
+    rows24 = refs[53]
+    for i, (part, lane) in enumerate(matrix_lanes([w.shape for w in weights])):
+        _, rows, columns = weights[i].shape
+        here = slice(lane, lane + columns)
+        place_of = places(orders[part])[1]
+        blocks = columns // 128
+        for b in range(blocks):
+            flat = flat_rows(rows, blocks, b)
+            g = shares[part][:, lane + 128 * b : lane + 128 * (b + 1)]
+            g_out[i][flat, :] = g
+            m_out[i][flat, :], v_out[i][flat, :] = momenta(firsts[i][flat, :], seconds[i][flat, :], g)
+        step = full[part][:, :, here]
+        u_norm = jnp.sqrt(over_all(jnp.sum(step * step, axis=0)))
+        old = weights[i][...]
+        w_norm = jnp.sqrt(over_all(jnp.sum(old * old, axis=0)))
+        norms[i : i + 1, 0:1] = w_norm
+        norms[i : i + 1, 1:2] = u_norm
+        ratio = RATE * (w_norm / (u_norm + EPS_ADAM))
+
+        def renew(chunk, _, i=i, part=part, here=here, place_of=place_of, ratio=ratio):
+            w_new[i][chunk] = weights[i][chunk] - ratio * full[part][place_of(chunk), :, here]
+            return 0
+
+        lax.fori_loop(0, n, renew, 0)
+        if rows % 8 == 0:
+            w_low[i][...] = w_new[i][...].reshape(n * rows, columns).astype(bf16)
+        else:
+            w_low[i][...] = jnp.zeros_like(w_low[i])
+
+    rows = full[0].shape[1]
+    tail = full[0].shape[2] - 128
+    for chunk in range(rows24.shape[0] // rows):
+        rows24[chunk * rows : (chunk + 1) * rows, :] = full[0][places(orders[0])[1](chunk), :, tail:]
+
+    def plain(weight, grad, first, second):
+        momentum, variance = momenta(first, second, grad)
+        return momentum, variance, weight - RATE_VEC * direction(momentum, variance)
+
+    grad = jnp.concatenate([rows24[0:8, :], rows24[8:16, :]], axis=1)
+    gvec[...] = grad
+    mvec[...], vvec[...], wvec[...] = plain(vec[...], grad, fvec[...], svec[...])
+    grad = rows24[16:24, :]
+    gbias[...] = grad
+    mbias[...], vbias[...], wbias[...] = plain(bias[...], grad, fbias[...], sbias[...])
+
+
+def exchange(n, grads, weights, vectors, ffn_bias, firsts, seconds, others):
+    stages = n.bit_length() - 1
+    far = list(range(1, stages))
+    turns = [far[s:] + far[:s] for s in (len(far) * p // 3 for p in range(3))]
+    orders = tuple((0, *turn) for turn in turns)
+    cut = lambda a: a.reshape(n, a.shape[0] // n, a.shape[1])
+    sources, blocks = list(map(cut, grads)), list(map(cut, weights))
+    flat = lambda a: a.reshape(-1, 128)
+    vmem = pl.BlockSpec(memory_space=pltpu.VMEM)
+    like = lambda a, dtype=f32: jax.ShapeDtypeStruct(a.shape, dtype)
+    firsts, seconds = list(map(flat, firsts)), list(map(flat, seconds))
+    operands = [*sources, *blocks, *firsts, *seconds]
+    shapes = [*map(like, sources), *[jax.ShapeDtypeStruct(s.shape[1:], f32) for s in sources]]
+    reduced = pl.pallas_call(
+        functools.partial(exchange_kernel, n, orders, stages),
+        out_shape=shapes,
+        in_specs=[vmem] * len(operands),
+        out_specs=[vmem] * len(shapes),
+        scratch_shapes=[
+            *[pltpu.VMEM((n // 2, *s.shape[1:]), f32) for s in sources],
+            *[pltpu.VMEM(s.shape, f32) for s in sources],
+            pltpu.SemaphoreType.DMA((3, 2 * stages)),
+            pltpu.SemaphoreType.DMA((3, 2 * stages)),
+        ],
+        compiler_params=pltpu.CompilerParams(
+            collective_id=0, has_side_effects=True, vmem_limit_bytes=32 * 1024 * 1024
+        ),
+        name="exchange",
+    )(*operands)
+    line_bias = flat(ffn_bias)
+    operands = [
+        *reduced, *blocks, *firsts, *seconds, vectors, line_bias, others[0], others[1], flat(others[2]), flat(others[3]),
+    ]
+    moments = list(map(like, firsts))
+    shapes = [
+        *moments, *moments, *moments, *map(like, blocks), *[like(w, bf16) for w in weights],
+        like(vectors), like(line_bias), *[like(vectors)] * 3, *[like(line_bias)] * 3, jax.ShapeDtypeStruct((4, 2), f32),
+    ]
+    results = pl.pallas_call(
+        functools.partial(renew_kernel, n, orders),
+        out_shape=shapes,
+        in_specs=[vmem] * len(operands),
+        out_specs=[vmem] * len(shapes),
+        scratch_shapes=[pltpu.VMEM((24, 128), f32)],
+        compiler_params=pltpu.CompilerParams(vmem_limit_bytes=32 * 1024 * 1024),
+        name="renew",
+    )(*operands)
+    g, m, v = ([a.reshape(-1) for a in results[4 * i : 4 * i + 4]] for i in range(3))
+    w = [new.reshape(old.shape) for new, old in zip(results[12:16], weights)]
+    low = [new.astype(bf16) if block.shape[1] % 8 else own for new, own, block in zip(w, results[16:20], blocks)]
+    gvec, gbias, mvec, vvec, wvec, mbias, vbias, wbias, norms = results[20:]
+    line = lambda a: a.reshape(-1)
+    steps = [entry for i in range(4) for entry in (m[i], v[i], w[i], low[i])]
+    return (*g, gvec, line(gbias), *steps, mvec, vvec, wvec, line(mbias), line(vbias), line(wbias), norms)
+
+
+def on_device(n, inputs, frames, cotangent, *rest):
+    proj_in, proj_out, ffn_up, ffn_down, vectors, ffn_bias = rest[:6]
+    moments, others = rest[6:14], rest[14:]
+    block_out, grad_inputs, *grads = local_grads(
         inputs, frames, cotangent, proj_in, proj_out, ffn_up, ffn_down, vectors, ffn_bias
     )
-    g_in = g_a[:, : 3 * width]
-    g_out = g_a[:, 3 * width : 4 * width]
-    extra = g_a[:24, 4 * width :]
-    g_vec = jnp.concatenate([extra[:8], extra[8:16]], axis=1)
-    g_bias = extra[16:24].reshape(-1)
-    fix = 1.0 - BETA**STEP
-    place = lax.axis_index("dp")
     weights = (proj_in, proj_out, ffn_up, ffn_down)
-    firsts = (first_in, first_out, first_up, first_down)
-    seconds = (second_in, second_out, second_up, second_down)
-    g_in, g_out, g_up, g_down, g_vec, g_bias = lax.psum(
-        (g_in, g_out, g_up, g_down, g_vec, g_bias), "dp"
-    )
-    shares = [
-        own_share(full, first.shape[0], place)
-        for full, first in zip((g_in, g_out, g_up, g_down), firsts)
-    ]
-    updated = shard_steps(shares, firsts, seconds, weights, place, fix)
-    squares = jnp.stack([jnp.sum(entry[2] * entry[2]) for entry in updated])
-    squares = lax.psum(squares, "dp")
-    w_norms = jnp.stack([jnp.sqrt(jnp.sum(weight * weight)) for weight in weights])
-    u_norms = jnp.sqrt(squares)
-    fresh_shares = tuple(
-        (
-            entry[3] - RATE * (w_norms[index] / (u_norms[index] + EPS_ADAM)) * entry[2]
-            for index, entry in enumerate(updated)
-        )
-    )
-    gathered = lax.all_gather(fresh_shares, "dp", axis=0, tiled=True)
-    fresh = [full.reshape(weight.shape) for full, weight in zip(gathered, weights)]
-    m_vec, v_vec, w_vec = adam_plain(vectors, g_vec, first_vec, second_vec, fix)
-    m_bias, v_bias, w_bias = adam_plain(ffn_bias, g_bias, first_bias, second_bias, fix)
-    norms = jnp.stack([w_norms, u_norms], axis=1)
     return (
         block_out,
         grad_inputs,
-        shares[0],
-        shares[1],
-        shares[2],
-        shares[3],
-        g_vec,
-        g_bias,
-        updated[0][0],
-        updated[0][1],
-        fresh[0],
-        fresh[0].astype(bf),
-        updated[1][0],
-        updated[1][1],
-        fresh[1],
-        fresh[1].astype(bf),
-        updated[2][0],
-        updated[2][1],
-        fresh[2],
-        fresh[2].astype(bf),
-        updated[3][0],
-        updated[3][1],
-        fresh[3],
-        fresh[3].astype(bf),
-        m_vec,
-        v_vec,
-        w_vec,
-        m_bias,
-        v_bias,
-        w_bias,
-        norms,
+        *exchange(n, grads, weights, vectors, ffn_bias, moments[0::2], moments[1::2], others),
     )
 
 
 def solution(mesh):
-    placed = (
-        P("dp", None),
-        P("dp", None),
-        P("dp", None),
-        P(),
-        P(),
-        P(),
-        P(),
-        P(),
-        P(),
-        P("dp"),
-        P("dp"),
-        P("dp"),
-        P("dp"),
-        P("dp"),
-        P("dp"),
-        P("dp"),
-        P("dp"),
-        P(),
-        P(),
-        P(),
-        P(),
-    )
+    split, rows, copied = P("dp"), P("dp", None), P()
+    step = (split, split, copied, copied)
     return jax.shard_map(
-        on_device,
+        functools.partial(on_device, mesh.shape["dp"]),
         mesh=mesh,
-        in_specs=placed,
-        out_specs=(
-            P("dp", None),
-            P("dp", None),
-            P("dp"),
-            P("dp"),
-            P("dp"),
-            P("dp"),
-            P(),
-            P(),
-            P("dp"),
-            P("dp"),
-            P(),
-            P(),
-            P("dp"),
-            P("dp"),
-            P(),
-            P(),
-            P("dp"),
-            P("dp"),
-            P(),
-            P(),
-            P("dp"),
-            P("dp"),
-            P(),
-            P(),
-            P(),
-            P(),
-            P(),
-            P(),
-            P(),
-            P(),
-            P(),
-        ),
+        in_specs=(rows, rows, rows, *[copied] * 6, *[split] * 8, *[copied] * 4),
+        out_specs=(rows, rows, *[split] * 4, copied, copied, *step * 4, *[copied] * 7),
         check_vma=False,
     )

time: 460 us -> 200 us (0.43)
  waiting for transfers between devices: 153 us -> 0 us
  blocking collectives: 119 us -> 0 us
  Pallas kernels: 131 us -> 193 us
  other arithmetic: 20.7 us -> 0 us
  between operations: 19.6 us -> 0.97 us
  local copies, waits for them, and re-layouts: 16.2 us -> 4.44 us
    psum x1 -> x0, waiting for transfers between devices: 138 us -> none  [on_device(): lax.psum((g_in, g_out, g_up, g_down, g_vec, g_bias), 'dp')]
    all_gather x2 -> x0, blocking collectives: 79.6 us -> none  [on_device(): gathered = lax.all_gather(fresh_shares, 'dp', axis=0, tiled=True)]
    pallas_call x0 -> x2, Pallas kernels: none -> 58.3 us  [the longest x1 51.1 us: exchange(): pl.pallas_call(functools.partial(exchange_kernel, n, orders, stages), out...]
    psum x1 -> x0, blocking collectives: 39.5 us -> none  [on_device(): lax.psum((g_in, g_out, g_up, g_down, g_vec, g_bias), 'dp')]
    all_gather x2 -> x0, waiting for transfers between devices: 15.4 us -> none  [on_device(): gathered = lax.all_gather(fresh_shares, 'dp', axis=0, tiled=True)]
    reduce_sum x7 -> x0, other arithmetic: 9.22 us -> none  [the longest x3 6.01 us: on_device(): squares = jnp.stack([jnp.sum(entry[2] * entry[2]) for entry in updated])]
    reshape x7 -> x0, local copies, waits for them, and re-layouts: 5.71 us -> none  [the longest x4 3.15 us: on_device(): full.reshape(weight.shape)]
    sub x6 -> x0, other arithmetic: 4.77 us -> none  [the longest x4 3.53 us: on_device(): entry[3] - RATE * (w_norms[index] / (u_norms[index] + EPS_ADAM)) * entry[2]]
  transfers between devices with their start and end apart: 3 -> 0, of which waited for: 2 -> 0; matrix products, arithmetic and copies ran while one was open for 3% -> 0% of each run, Pallas kernels for 0% -> 0%
where the time goes in v2:
time: 200 us; the launch traced here: 199 us
  Pallas kernels  193 us (96%)
  local copies, waits for them, and re-layouts  4.44 us (2%)
    pallas_call x1, Pallas kernels, local_grads(): pl.pallas_call(local_kernel, out_shape=(jax.ShapeDtypeStruct((rows, width...  135 us
    pallas_call x1, Pallas kernels, exchange(): pl.pallas_call(functools.partial(exchange_kernel, n, orders, stages), out...  51.1 us
    pallas_call x1, Pallas kernels, exchange(): pl.pallas_call(functools.partial(renew_kernel, n, orders), out_shape=shap...  7.2 us
    unnamed x43, local copies, waits for them, and re-layouts  4.44 us

profile of v2, /device:TPU:0, one launch (start us, length us, event | category | flops | bytes accessed | tf_op | source)
XLA Modules:
  0.0 198.8 jit_solution(3042237990900521002)
XLA Ops:
  0.7 0.0 copy-start
  0.7 0.0 copy-start.1
  0.7 0.0 copy-start.2
  0.7 0.0 copy-start.3
  0.7 0.0 copy-start.7
  0.7 0.0 copy-start.8
  0.7 0.0 copy-start.9
  0.7 0.0 copy-start.10
  0.8 0.0 copy-start.11
  0.8 0.0 copy-start.12
  0.8 0.0 copy-start.14
  0.8 0.0 copy-start.15
  0.8 135.0 %local_grads.1 = (bf16[4080,256]{1,0:T(8,128)(2,1)}, f32[4080,256]{1,0:T(8,128)}, f32[256,1152]{1,0:T(8,128)}, f32[256,1024]{1,0:T(8,128)}, f32[1024,256]{1,0:T(8,128)}) custom-call(s32[4,4]{1,0:T(4,128)} %frames_ref.1, bf16[4080,256]{1,0:T(8,128)(2,1)} %x_hbm.1, f32[4080,256]{1,0:T(8,128)} %cot_hbm.1, f32[256,768]{1,0:T(8,128)} %pin_ref.1, ...), custom_call_target="tpu_custom_call" | custom-call | tf_op jit(solution)/shard_map/local_grads/pallas_call | solution.py:339
  135.8 0.0 copy-done
  135.9 0.0 copy-done.1
  135.9 0.0 copy-done.2
  135.9 0.0 copy-done.3
  135.9 0.0 copy-done.7
  136.0 1.3 copy-done.4
  137.2 1.2 copy-done.5
  138.5 1.2 copy-done.6
  139.7 0.0 copy-start.19
  139.7 0.0 copy-start.20
  139.7 51.1 %exchange.1 = (f32[32,8,1152]{2,1,0:T(8,128)S(1)}, f32[32,8,1024]{2,1,0:T(8,128)S(1)}, f32[32,32,256]{2,1,0:T(8,128)S(1)}, f32[8,1152]{1,0:T(8,128)S(1)}, f32[8,1024]{1,0:T(8,128)S(1)}, /*index=5*/f32[32,256]{1,0:T(8,128)S(1)}) custom-call(f32[32,8,1152]{2,1,0:T(8,128)S(1)} %bitcast.47, f32[32,8,1024]{2,1,0:T(8,128)S(1)} %bitcast.48, ...), custom_call_target="tpu_custom_call" | custom-call | tf_op jit(solution)/shard_map/exchange/pallas_call | solution.py:591
  190.9 0.0 copy-done.13
  190.9 0.0 copy-done.16
  190.9 0.0 copy-done.17
  190.9 0.0 copy-done.18
  190.9 0.0 copy-done.19
  190.9 0.0 copy-done.20
  190.9 7.2 %renew.1 = (f32[48,128]{1,0:T(8,128)}, f32[16,128]{1,0:T(8,128)}, f32[64,128]{1,0:T(8,128)}, f32[64,128]{1,0:T(8,128)}, f32[48,128]{1,0:T(8,128)}, /*index=5*/f3...) custom-call(f32[32,8,1152]{2,1,0:T(8,128)S(1)} %get-tuple-element.76, ...), custom_call_target="tpu_custom_call" | custom-call | tf_op jit(solution)/shard_map/renew/pallas_call | solution.py:616
  198.1 0.6 copy.52
  (14 shorter events, 0.0 us)
Async XLA Ops:
  0.7 135.2 %copy-start = (f32[256,1024]{1,0:T(8,128)S(1)}, f32[256,1024]{1,0:T(8,128)}, u32[]{:S(2)}) copy-start(f32[256,1024]{1,0:T(8,128)} %pup_ref.1) | copy-start | bytes 3145732
  0.7 135.2 %copy-start.1 = (f32[1024,256]{1,0:T(8,128)S(1)}, f32[1024,256]{1,0:T(8,128)}, u32[]{:S(2)}) copy-start(f32[1024,256]{1,0:T(8,128)} %pdown_ref.1) | copy-start | bytes 3145732
  0.7 135.2 %copy-start.2 = (f32[256,768]{1,0:T(8,128)S(1)}, f32[256,768]{1,0:T(8,128)}, u32[]{:S(2)}) copy-start(f32[256,768]{1,0:T(8,128)} %pin_ref.1) | copy-start | bytes 2359300
  0.7 135.2 %copy-start.3 = (f32[256,256]{1,0:T(8,128)S(1)}, f32[256,256]{1,0:T(8,128)}, u32[]{:S(2)}) copy-start(f32[256,256]{1,0:T(8,128)} %pout_ref.1) | copy-start | bytes 786436
  0.7 135.2 %copy-start.7 = (f32[8192]{0:T(1024)S(1)}, f32[8192]{0:T(1024)}, u32[]{:S(2)}) copy-start(f32[8192]{0:T(1024)} %param.34) | copy-start | bytes 98308
  0.7 135.2 %copy-start.8 = (f32[8192]{0:T(1024)S(1)}, f32[8192]{0:T(1024)}, u32[]{:S(2)}) copy-start(f32[8192]{0:T(1024)} %param.36) | copy-start | bytes 98308
  0.7 135.2 %copy-start.9 = (f32[8192]{0:T(1024)S(1)}, f32[8192]{0:T(1024)}, u32[]{:S(2)}) copy-start(f32[8192]{0:T(1024)} %param.35) | copy-start | bytes 98308
  0.7 135.2 %copy-start.10 = (f32[8192]{0:T(1024)S(1)}, f32[8192]{0:T(1024)}, u32[]{:S(2)}) copy-start(f32[8192]{0:T(1024)} %param.37) | copy-start | bytes 98308
  0.8 135.2 %copy-start.11 = (f32[6144]{0:T(1024)S(1)}, f32[6144]{0:T(1024)}, u32[]{:S(2)}) copy-start(f32[6144]{0:T(1024)} %param.30) | copy-start | bytes 73732
  0.8 135.2 %copy-start.12 = (f32[6144]{0:T(1024)S(1)}, f32[6144]{0:T(1024)}, u32[]{:S(2)}) copy-start(f32[6144]{0:T(1024)} %param.31) | copy-start | bytes 73732
  0.8 135.2 %copy-start.14 = (f32[2048]{0:T(1024)S(1)}, f32[2048]{0:T(1024)}, u32[]{:S(2)}) copy-start(f32[2048]{0:T(1024)} %param.32) | copy-start | bytes 24580
  0.8 135.2 %copy-start.15 = (f32[2048]{0:T(1024)S(1)}, f32[2048]{0:T(1024)}, u32[]{:S(2)}) copy-start(f32[2048]{0:T(1024)} %param.33) | copy-start | bytes 24580
  136.0 1.3 copy-start.4
  137.2 1.2 copy-start.5
  138.5 1.2 copy-start.6
  139.7 51.2 %copy-start.13 = (f32[8,256]{1,0:T(8,128)S(1)}, f32[8,256]{1,0:T(8,128)}, u32[]{:S(2)}) copy-start(f32[8,256]{1,0:T(8,128)} %refs_18_.1) | copy-start | bytes 24580
  139.7 51.2 %copy-start.16 = (f32[1024]{0:T(1024)S(1)}, f32[1024]{0:T(1024)}, u32[]{:S(2)}) copy-start(f32[1024]{0:T(1024)} %param.29) | copy-start | bytes 12292
  139.7 51.2 %copy-start.17 = (f32[8,256]{1,0:T(8,128)S(1)}, f32[8,256]{1,0:T(8,128)}, u32[]{:S(2)}) copy-start(f32[8,256]{1,0:T(8,128)} %refs_20_.1) | copy-start | bytes 24580
  139.7 51.2 %copy-start.18 = (f32[8,256]{1,0:T(8,128)S(1)}, f32[8,256]{1,0:T(8,128)}, u32[]{:S(2)}) copy-start(f32[8,256]{1,0:T(8,128)} %refs_21_.1) | copy-start | bytes 24580
  139.7 51.2 %copy-start.19 = (f32[1024]{0:T(1024)S(1)}, f32[1024]{0:T(1024)}, u32[]{:S(2)}) copy-start(f32[1024]{0:T(1024)} %param.40) | copy-start | bytes 12292
  139.7 51.2 %copy-start.20 = (f32[1024]{0:T(1024)S(1)}, f32[1024]{0:T(1024)}, u32[]{:S(2)}) copy-start(f32[1024]{0:T(1024)} %param.41) | copy-start | bytes 12292

commit v3 on v2

--- a/solution.py
+++ b/solution.py
@@ -20,6 +20,10 @@
 RATE_VEC = 0.2
 
 TILE = 256
+GROUP = 2
+PROJECTED = 4
+SLOTS = 2
+LAG, LAG_BACK, LAG_FEED, LAG_PROJECT = 3, 2, 2, 1
 QT = 128
 SPAN = 384
 LEAD = 16
@@ -54,16 +58,25 @@
 
 
 def gelu_parts(x):
-    den = 1.0 + jnp.abs(x) * (0.3275911 / math.sqrt(2.0))
-    t = pl.reciprocal(den, approx=True)
-    t = t * (2.0 - den * t)
-    bell = jnp.exp(x * x * -0.5)
-    poly = 0.5 * 1.061405429
+    t = pltpu.reciprocal(1.0 + jnp.abs(x) * (0.3275911 / math.sqrt(2.0)), approx=True)
+    y = x * math.sqrt(0.5 / math.log(2.0))
+    bell = jnp.exp2(-0.5 * math.log2(2.0 * math.pi) - y * y)
+    unit = 0.5 * math.sqrt(2.0 * math.pi)
+    poly = unit * 1.061405429
     for c in (-1.453152027, 1.421413741, -0.284496736, 0.254829592):
-        poly = poly * t + 0.5 * c
+        poly = poly * t + unit * c
     tail = poly * t * bell
     cdf = jnp.where(x < 0.0, tail, 1.0 - tail)
-    return x * cdf, cdf + x * (bell * (1.0 / math.sqrt(2.0 * math.pi)))
+    return x * cdf, cdf + x * bell
+
+
+def stagger(work, stages, lag):
+    held = {}
+    for u in range(len(work) + lag * (len(stages) - 1)):
+        for k, stage in enumerate(stages):
+            at = u - k * lag
+            if 0 <= at < len(work):
+                held[at] = stage(work[at], held.get(at))
 
 
 def fold8(x):
@@ -71,26 +84,51 @@
 
 
 def local_kernel(
-    frames_ref, x_hbm, cot_hbm, pin_ref, pout_ref, pup_ref, pdown_ref, vec_ref, bias_ref,
-    bo_hbm, gi_hbm, ga_ref, gup_ref, gdown_ref,
-    xs, cs, bos, qs, ks, vs, dq, dk, dv, dms, lse, dka, dva, turned, win, wout, wup, wdown, gdt, sums, bsum, sems,
+    frames_hbm, x_hbm, cot_hbm, pin_hbm, pout_hbm, pup_hbm, pdown_hbm, vec_hbm, bias_hbm,
+    bo_hbm, gi_hbm, ga_ref, gup_hbm, gdown_hbm,
+    frames_ref, pin_ref, pout_ref, pup_ref, pdown_ref, vec_ref, bias_ref, xs, cs, bos, qs, ks, vs, dq, dk, dv, dms, lse, dka, dva, counts, members, starts, win, wout, wup, wdown, gup_ref, gdown_ref, gdt, sums, bsum, sems, x_sems, gi_sems,
 ):
     rows, width = x_hbm.shape
     padded = xs.shape[0]
     steps = padded // TILE
     pairs = width // 128
-    hidden_width = pup_ref.shape[1]
-    micro, packed = frames_ref.shape
-
-    x_in = pltpu.make_async_copy(x_hbm, xs.at[pl.ds(0, rows)], sems.at[0])
-    c_in = pltpu.make_async_copy(cot_hbm, cs.at[pl.ds(0, rows)], sems.at[1])
-    x_in.start()
-    c_in.start()
-
-    win[...] = pin_ref[...].astype(bf16)
-    wout[...] = pout_ref[...].astype(bf16)
-    wup[...] = pup_ref[...].astype(bf16)
-    wdown[...] = pdown_ref[...].astype(bf16)
+    hidden_width = pup_hbm.shape[1]
+    micro, packed = frames_hbm.shape
+
+    piece = TILE * PROJECTED
+    final = padded // piece - 1
+
+    def by_piece(i, act, hbm, local, sems_, out=False):
+        def at(start, size):
+            ends = hbm.at[pl.ds(start, size)], local.at[pl.ds(start, size)]
+            act(pltpu.make_async_copy(*(ends[::-1] if out else ends), sems_.at[i]))
+
+        pl.when(i < final)(lambda: at(pl.multiple_of(i * piece, piece), piece))
+        pl.when(i == final)(lambda: at(final * piece, rows - final * piece))
+
+    begin, finish = lambda copy: copy.start(), lambda copy: copy.wait()
+    loads = [
+        pltpu.make_async_copy(src, dst, sems.at[k])
+        for k, (src, dst) in enumerate(
+            (
+                (vec_hbm, vec_ref),
+                (pin_hbm, pin_ref),
+                (frames_hbm, frames_ref),
+                (bias_hbm, bias_ref),
+                (pout_hbm, pout_ref),
+                (pup_hbm, pup_ref),
+                (pdown_hbm, pdown_ref),
+                (cot_hbm, cs.at[pl.ds(0, rows)]),
+            )
+        )
+    ]
+    for copy in loads[:2]:
+        copy.start()
+    for i in range(final + 1):
+        by_piece(i, begin, x_hbm, xs, x_sems)
+    for copy in loads[2:]:
+        copy.start()
+
     gap = padded - rows
     if gap:
         xs[pl.ds(rows, gap)] = jnp.zeros((gap, width), bf16)
@@ -100,25 +138,43 @@
         ref[pl.ds(padded, SPAN)] = jnp.zeros((SPAN, width), bf16)
     for ref in (ga_ref, gup_ref, gdt, sums, bsum):
         ref[...] = jnp.zeros_like(ref)
-    x_in.wait()
-
-    def tile_at(i):
-        return pl.ds(pl.multiple_of(i * TILE, TILE), TILE)
+    for copy in loads[:2]:
+        copy.wait()
+    win[...] = pin_ref[...].astype(bf16)
 
     gain_one, shift_one = vec_ref[3:4, :], vec_ref[4:5, :]
     gain_two, shift_two = vec_ref[5:6, :], vec_ref[6:7, :]
 
+    def spot(i, g, group=GROUP):
+        return pl.ds(pl.multiple_of((i * group + g) * TILE, TILE), TILE)
+
     def project(i, _):
-        at = tile_at(i)
-        n, _r = normalize(xs[at].astype(f32))
-        h = (n * gain_one + shift_one).astype(bf16)
-        q = dot(h, win[:, :width]) + vec_ref[0:1, :]
-        qs[at] = q.astype(bf16) * jnp.array(0.125, bf16)
-        ks[at] = dot(h, win[:, width : 2 * width]).astype(bf16)
-        vs[at] = (dot(h, win[:, 2 * width :]) + vec_ref[1:2, :]).astype(bf16)
+        by_piece(i, finish, x_hbm, xs, x_sems)
+
+        def even(g, _):
+            n, _rstd = normalize(xs[spot(i, g, PROJECTED)].astype(f32))
+            return (n * gain_one + shift_one).astype(bf16)
+
+        def spread(g, h):
+            return [dot(h, win[:, b * width : (b + 1) * width]) for b in range(3)]
+
+        def keep(g, held):
+            q, k, v = held
+            at = spot(i, g, PROJECTED)
+            qs[at] = (q + vec_ref[0:1, :]).astype(bf16) * jnp.array(0.125, bf16)
+            ks[at] = k.astype(bf16)
+            vs[at] = (v + vec_ref[1:2, :]).astype(bf16)
+
+        stagger(list(range(PROJECTED)), (even, spread, keep), LAG_PROJECT)
         return 0
 
-    lax.fori_loop(0, steps, project, 0)
+    lax.fori_loop(0, steps // PROJECTED, project, 0)
+
+    for copy in loads[2:]:
+        copy.wait()
+    wout[...] = pout_ref[...].astype(bf16)
+    wup[...] = pup_ref[...].astype(bf16)
+    wdown[...] = pdown_ref[...].astype(bf16)
 
     first_head = lax.broadcasted_iota(jnp.int32, (1, 128), 1) < 64
     keep0 = first_head.astype(f32).astype(bf16)
@@ -165,177 +221,270 @@
         both = jnp.concatenate([out[:64, :QT], out[64:, QT:]], axis=0)
         return both.T
 
-    def put(ref, at_row, lanes, value, off):
-        lead = pl.ds(pl.multiple_of(at_row, LEAD), LEAD)
-        own = lax.broadcasted_iota(jnp.int32, (LEAD, 128), 0) >= off
-        old = ref[lead, lanes].astype(f32)
-        ref[lead, lanes] = jnp.where(own, value[:LEAD], old).astype(bf16)
-        rest = value.shape[0] - LEAD
-        ref[pl.ds(pl.multiple_of(at_row + LEAD, LEAD), rest), lanes] = value[LEAD:].astype(bf16)
-
-    def window(i, start):
+    def put(ref, base, lanes, block, j, off, stop):
+        at = pl.ds(pl.multiple_of(base + QT * j, LEAD), QT)
+        own = lax.broadcasted_iota(jnp.int32, (QT, 128), 0)
+        keep = own < stop - QT * j
+        if j == 0:
+            keep &= own >= off
+        ref[at, lanes] = jnp.where(keep, block, ref[at, lanes].astype(f32)).astype(bf16)
+
+    classes = SPAN // QT
+    for c in range(classes):
+        counts[c] = 0
+
+    def sort(i, start):
         length = frames_ref[i // packed, i % packed] * FRAME
+        tiles = ((start & (LEAD - 1)) + length + QT - 1) // QT - 1
+        seat = counts[tiles]
+        members[tiles, seat] = i
+        counts[tiles] = seat + 1
+        starts[i] = start
+        return start + length
+
+    lax.fori_loop(0, micro * packed, sort, 0)
+    for c in range(classes - 1):
+        odd = counts[c] & 1
+
+        @pl.when(odd == 1)
+        def _(c=c):
+            members[c + 1, counts[c + 1]] = members[c, counts[c] - 1]
+            counts[c + 1] = counts[c + 1] + 1
+
+    def window(n, tiles):
+        i = members[tiles - 1, n]
+        start = starts[i]
         off = start & (LEAD - 1)
-        return pl.multiple_of(start - off, LEAD), off, off + length, start + length
-
-    def attend(i, start):
-        base, off, stop, after = window(i, start)
-        for p in range(pairs):
-            turned[p] = vs[pl.ds(base, SPAN), 128 * p : 128 * (p + 1)].T
-
-        def step(j):
+        stop = off + frames_ref[i // packed, i % packed] * FRAME
+        return i, pl.multiple_of(start - off, LEAD), off, stop
+
+    def units(tiles, n):
+        windows = [window(SLOTS * n + slot, tiles) for slot in range(SLOTS)]
+        for j in reversed(range(tiles)):
+            for p in range(pairs):
+                for slot in range(SLOTS):
+                    yield slot, p, slice(128 * p, 128 * (p + 1)), j, windows[slot]
+
+    def attend(tiles, n, _):
+        todo, v_t = [], {}
+
+        def compare(unit, _):
+            _slot, _p, lanes, j, (_i, base, _off, _stop) = unit
+            query = heads_apart(qs[pl.ds(pl.multiple_of(base + QT * j, LEAD), QT), lanes])
+            return dot_nt(ks[pl.ds(base, depth(j)), lanes], query)
+
+        def soften(unit, raw):
+            slot, p, lanes, j, (i, base, off, stop) = unit
             end, valid = limits(j, off, stop)
+            score = hide(raw, j, off, end)
+            peak = jnp.max(score, axis=0, keepdims=True)
+            weight = jnp.exp(score - peak)
+            total = jnp.sum(weight, axis=0, keepdims=True)
+            row = pairs * j + p
+            lse[i, row : row + 1, :] = jnp.where(valid, peak + jnp.log(total), BIG)
+            prob = (weight * jnp.where(valid, 1.0 / total, 0.0)).astype(bf16)
+            if (slot, p) not in v_t:
+                v_t[slot, p] = vs[pl.ds(base, filled(tiles - 1)), lanes].T
+            return dot(v_t[slot, p][:, : filled(j)], fill(prob, j))
+
+        def turn(unit, out):
+            _slot, _p, lanes, j, (_i, base, off, stop) = unit
+            todo.append((dq, base, lanes, heads_back(out), j, off, stop))
+
+        stagger(list(units(tiles, n)), (compare, soften, turn), LAG)
+        for entry in todo:
+            put(*entry)
+        return 0
+
+    for tiles in range(1, classes + 1):
+        lax.fori_loop(0, counts[tiles - 1] // SLOTS, functools.partial(attend, tiles), 0)
+
+    ones = jnp.ones((16, TILE * GROUP), bf16)
+
+    def join(blocks, axis):
+        return jnp.concatenate(blocks, axis=axis)
+
+    def feed_forward(i, _):
+        state = []
+        for g in range(GROUP):
+            at = spot(i, g)
+            mixed = dq[at]
+            resid = xs[at].astype(f32) + dot(mixed, wout[...]) + vec_ref[2:3, :]
+            n, rstd = normalize(resid)
+            h = (n * gain_two + shift_two).astype(bf16)
+            state.append((at, mixed, resid, n, rstd, h, cs[at].astype(bf16)))
+        h_t = jnp.concatenate([join([e[5].T for e in state], 1), ones], axis=0)
+        low_t = join([e[6].T for e in state], 1)
+        feeds, d_hs, acts, d_pres = [None] * GROUP, [None] * GROUP, {}, {}
+
+        def expand(unit, _):
+            c, g = unit
+            cols = slice(c, c + 256)
+            return dot(state[g][5], wup[:, cols]), dot_nt(state[g][6], wdown[cols, :])
+
+        def bend(unit, held):
+            c, g = unit
+            pre, d_act = held
+            act, slope = gelu_parts(pre + bias_ref[:, c : c + 256])
+            act = act.astype(bf16)
+            d_pre = (d_act * slope).astype(bf16)
+            acts[c, g], d_pres[c, g] = act, d_pre
+            return act, d_pre
+
+        def shrink(unit, held):
+            c, g = unit
+            act, d_pre = held
+            cols = slice(c, c + 256)
+            feed, d_h = dot(act, wdown[cols, :]), dot_nt(d_pre, wup[:, cols])
+            feeds[g] = feed if feeds[g] is None else feeds[g] + feed
+            d_hs[g] = d_h if d_hs[g] is None else d_hs[g] + d_h
+            if g == GROUP - 1:
+                act = join([acts.get((c, k)) for k in range(GROUP)], 0)
+                d_pre = join([d_pres.get((c, k)) for k in range(GROUP)], 0)
+                gdt[:, cols] += dot(low_t, act)
+                both = dot(h_t, d_pre)
+                gup_ref[:, cols] += both[:width]
+                bsum[:, cols] += both[width : width + 8]
+
+        stagger([(c, g) for c in range(0, hidden_width, 256) for g in range(GROUP)], (expand, bend, shrink), LAG_FEED)
+        branches = []
+        for g in range(GROUP):
+            at, _mixed, resid, n, rstd, _h, _low = state[g]
+            feed, d_h = feeds[g], d_hs[g]
+            bos[at] = (resid + feed + vec_ref[7:8, :]).astype(bf16)
+            d_resid = cs[at] + norm_back(d_h, gain_two, n, rstd)
+            cs[at] = d_resid
+            branch = d_resid.astype(bf16)
+            branches.append(branch)
+            sums[5] += fold8(d_h * n)
+            sums[6] += fold8(d_h)
+            dms[at] = dot_nt(branch, wout[...]).astype(bf16)
+        mixed_t = jnp.concatenate([join([e[1].T for e in state], 1), ones], axis=0)
+        both = dot(mixed_t, join(branches, 0))
+        ga_ref[:, 3 * width : 4 * width] += both[:width]
+        sums[2] += both[width : width + 8] * 0.125
+        sums[7] += dot(ones, join([e[6] for e in state], 0))[:8] * 0.125
+        return 0
+
+    lax.fori_loop(0, steps // GROUP, feed_forward, 0)
+    bo_out = pltpu.make_async_copy(bos.at[pl.ds(0, rows)], bo_hbm, sems.at[8])
+    bo_out.start()
+    for c in range(0, hidden_width, 256):
+        gdown_ref[c : c + 256, :] = gdt[:, c : c + 256].T
+    grads_out = [
+        pltpu.make_async_copy(gup_ref, gup_hbm, sems.at[9]),
+        pltpu.make_async_copy(gdown_ref, gdown_hbm, sems.at[10]),
+    ]
+    for copy in grads_out:
+        copy.start()
+
+    def attend_back(tiles, n, _):
+        todo, k_t = [], {}
+
+        def compare(unit, _):
+            _slot, _p, lanes, j, (_i, base, _off, _stop) = unit
+            here = pl.ds(pl.multiple_of(base + QT * j, LEAD), QT)
+            query, d_out = heads_apart(qs[here, lanes]), heads_apart(dms[here, lanes])
             m = depth(j)
-            for p in range(pairs):
-                lanes = slice(128 * p, 128 * (p + 1))
-                query = heads_apart(qs[pl.ds(pl.multiple_of(base + QT * j, LEAD), QT), lanes])
-                score = hide(dot_nt(ks[pl.ds(base, m), lanes], query), j, off, end)
-                peak = jnp.max(score, axis=0, keepdims=True)
-                weight = jnp.exp(score - peak)
-                total = jnp.sum(weight, axis=0, keepdims=True)
-                prob = (weight * jnp.where(valid, 1.0 / total, 0.0)).astype(bf16)
-                row = pairs * j + p
-                lse[i, row : row + 1, :] = jnp.where(valid, peak + jnp.log(total), BIG)
-                out = dot(turned[p, :, : filled(j)], fill(prob, j))
-                block = heads_back(out)
-                if j == 0:
-                    put(dq, base, lanes, block, off)
-                else:
-                    dq[pl.ds(pl.multiple_of(base + QT * j, LEAD), QT), lanes] = block.astype(bf16)
-
-        step(0)
-        for j in range(1, SPAN // QT):
-            pl.when(stop > QT * j)(functools.partial(step, j))
-        return after
-
-    lax.fori_loop(0, micro * packed, attend, 0)
-
-    c_in.wait()
-
-    def feed_forward(i, _):
-        at = tile_at(i)
-        mixed = dq[at]
-        resid = xs[at].astype(f32) + dot(mixed, wout[...]) + vec_ref[2:3, :]
-        n, rstd = normalize(resid)
-        h = (n * gain_two + shift_two).astype(bf16)
-        cot = cs[at]
-        low = cot.astype(bf16)
-        h_t, low_t = h.T, low.T
-        feed = jnp.zeros((TILE, width), f32)
-        d_h = jnp.zeros((TILE, width), f32)
-        for c in range(0, hidden_width, 256):
-            cols = slice(c, c + 256)
-            pre = dot(h, wup[:, cols]) + bias_ref[:, cols]
-            act, slope = gelu_parts(pre)
-            act = act.astype(bf16)
-            feed += dot(act, wdown[cols, :])
-            d_pre = (dot_nt(low, wdown[cols, :]) * slope).astype(bf16)
-            d_h += dot_nt(d_pre, wup[:, cols])
-            gdt[:, cols] += dot(low_t, act)
-            gup_ref[:, cols] += dot(h_t, d_pre)
-            bsum[:, cols] += fold8(d_pre.astype(f32))
-        bos[at] = (resid + feed + vec_ref[7:8, :]).astype(bf16)
-        d_resid = cot + norm_back(d_h, gain_two, n, rstd)
-        cs[at] = d_resid
-        branch = d_resid.astype(bf16)
-        sums[2] += fold8(branch.astype(f32))
-        sums[5] += fold8(d_h * n)
-        sums[6] += fold8(d_h)
-        sums[7] += fold8(low.astype(f32))
-        ga_ref[:, 3 * width : 4 * width] += dot(mixed.T, branch)
-        dms[at] = dot_nt(branch, wout[...]).astype(bf16)
+            return query, d_out, dot_nt(ks[pl.ds(base, m), lanes], query), dot_nt(vs[pl.ds(base, m), lanes], d_out)
+
+        def soften(unit, held):
+            slot, p, lanes, j, (i, base, off, stop) = unit
+            query, d_out, raw, d_prob = held
+            end, _valid = limits(j, off, stop)
+            row = pairs * j + p
+            prob = jnp.exp(hide(raw, j, off, end) - lse[i, row : row + 1, :])
+            delta = jnp.sum(prob * d_prob, axis=0, keepdims=True)
+            d_score = (prob * (d_prob - delta)).astype(bf16)
+            if (slot, p) not in k_t:
+                k_t[slot, p] = ks[pl.ds(base, filled(tiles - 1)), lanes].T
+            out = dot(k_t[slot, p][:, : filled(j)], fill(d_score, j))
+            return dot(prob.astype(bf16), d_out), dot(d_score, query), out
+
+        def collect(unit, held):
+            slot, _p, lanes, j, (_i, base, off, stop) = unit
+            d_val, d_key, out = held
+            m = depth(j)
+            first = j == tiles - 1
+            dva[slot, :m, lanes] = d_val if first else dva[slot, :m, lanes] + d_val
+            dka[slot, :m, lanes] = d_key if first else dka[slot, :m, lanes] + d_key
+            todo.append((dq, base, lanes, heads_back(out) * 0.125, j, off, stop))
+
+        stagger(list(units(tiles, n)), (compare, soften, collect), LAG_BACK)
+        for entry in todo:
+            put(*entry)
+        for slot, p, lanes, j, (i, base, off, stop) in units(tiles, n):
+            at = slice(QT * j, QT * (j + 1))
+            put(dv, base, lanes, dva[slot, at, lanes], j, off, stop)
+            put(dk, base, lanes, dka[slot, at, lanes], j, off, stop)
         return 0
 
-    lax.fori_loop(0, steps, feed_forward, 0)
-    bo_out = pltpu.make_async_copy(bos.at[pl.ds(0, rows)], bo_hbm, sems.at[2])
-    bo_out.start()
-
-    def attend_back(i, start):
-        base, off, stop, after = window(i, start)
-        for p in range(pairs):
-            turned[p] = ks[pl.ds(base, SPAN), 128 * p : 128 * (p + 1)].T
-        dka[...] = jnp.zeros_like(dka)
-        dva[...] = jnp.zeros_like(dva)
-
-        def step(j):
-            end, _valid = limits(j, off, stop)
-            m = depth(j)
-            for p in range(pairs):
-                lanes = slice(128 * p, 128 * (p + 1))
-                here = pl.ds(pl.multiple_of(base + QT * j, LEAD), QT)
-                query = heads_apart(qs[here, lanes])
-                d_out = heads_apart(dms[here, lanes])
-                row = pairs * j + p
-                score = hide(dot_nt(ks[pl.ds(base, m), lanes], query), j, off, end)
-                prob = jnp.exp(score - lse[i, row : row + 1, :])
-                d_prob = dot_nt(vs[pl.ds(base, m), lanes], d_out)
-                delta = jnp.sum(prob * d_prob, axis=0, keepdims=True)
-                d_score = (prob * (d_prob - delta)).astype(bf16)
-                dva[:m, lanes] += dot(prob.astype(bf16), d_out)
-                dka[:m, lanes] += dot(d_score, query)
-                out = dot(turned[p, :, : filled(j)], fill(d_score, j))
-                block = heads_back(out) * 0.125
-                if j == 0:
-                    put(dq, base, lanes, block, off)
-                else:
-                    dq[here, lanes] = block.astype(bf16)
-
-        step(0)
-        for j in range(1, SPAN // QT):
-            pl.when(stop > QT * j)(functools.partial(step, j))
-        for p in range(pairs):
-            lanes = slice(128 * p, 128 * (p + 1))
-            put(dk, base, lanes, dka[:, lanes], off)
-            put(dv, base, lanes, dva[:, lanes], off)
-        return after
-
-    lax.fori_loop(0, micro * packed, attend_back, 0)
+    for tiles in range(1, classes + 1):
+        lax.fori_loop(0, counts[tiles - 1] // SLOTS, functools.partial(attend_back, tiles), 0)
     if gap:
         for ref in (dq, dk, dv):
             ref[pl.ds(rows, gap)] = jnp.zeros((gap, width), bf16)
 
     def project_back(i, _):
-        at = tile_at(i)
-        n, rstd = normalize(xs[at].astype(f32))
-        h_t = (n * gain_one + shift_one).astype(bf16).T
-        d_h = jnp.zeros((TILE, width), f32)
-        for b, ref in enumerate((dq, dk, dv)):
-            cols = slice(b * width, (b + 1) * width)
-            block = ref[at]
-            d_h += dot_nt(block, win[:, cols])
-            ga_ref[:, cols] += dot(h_t, block)
-            if b != 1:
-                sums[b // 2] += fold8(block.astype(f32))
-        sums[3] += fold8(d_h * n)
-        sums[4] += fold8(d_h)
-        cs[at] = cs[at] + norm_back(d_h, gain_one, n, rstd)
+        turned, blocks = {}, {}
+
+        def even(g, _):
+            n, rstd = normalize(xs[spot(i, g, PROJECTED)].astype(f32))
+            turned[g] = (n * gain_one + shift_one).astype(bf16).T
+            return n, rstd
+
+        def spread(g, held):
+            d_h = None
+            for b, ref in enumerate((dq, dk, dv)):
+                block = ref[spot(i, g, PROJECTED)]
+                blocks[b, g] = block
+                part = dot_nt(block, win[:, b * width : (b + 1) * width])
+                d_h = part if d_h is None else d_h + part
+            return *held, d_h
+
+        def keep(g, held):
+            n, rstd, d_h = held
+            sums[3] += fold8(d_h * n)
+            sums[4] += fold8(d_h)
+            at = spot(i, g, PROJECTED)
+            cs[at] = cs[at] + norm_back(d_h, gain_one, n, rstd)
+            if g == PROJECTED - 1:
+                h_t = jnp.concatenate([join([turned[k] for k in range(PROJECTED)], 1), jnp.ones((16, TILE * PROJECTED), bf16)], axis=0)
+                for b in range(3):
+                    both = dot(h_t, join([blocks[b, k] for k in range(PROJECTED)], 0))
+                    ga_ref[:, b * width : (b + 1) * width] += both[:width]
+                    if b != 1:
+                        sums[b // 2] += both[width : width + 8] * 0.125
+
+        stagger(list(range(PROJECTED)), (even, spread, keep), LAG_PROJECT)
+        by_piece(i, begin, gi_hbm, cs, gi_sems, out=True)
         return 0
 
-    lax.fori_loop(0, steps, project_back, 0)
-    gi_out = pltpu.make_async_copy(cs.at[pl.ds(0, rows)], gi_hbm, sems.at[3])
-    gi_out.start()
-    for c in range(0, hidden_width, 256):
-        gdown_ref[c : c + 256, :] = gdt[:, c : c + 256].T
+    lax.fori_loop(0, steps // PROJECTED, project_back, 0)
     vec = jnp.sum(sums[...], axis=1)
     tail = 4 * width
     for b in range(width // 128):
         ga_ref[8 * b : 8 * b + 8, tail : tail + 128] = vec[:, 128 * b : 128 * (b + 1)]
-    bias = jnp.sum(bsum[...], axis=0, keepdims=True)
+    bias = bsum[0:1, :]
     for b in range(hidden_width // 128):
         row = 8 * (width // 128) + b
         ga_ref[row : row + 1, tail : tail + 128] = bias[:, 128 * b : 128 * (b + 1)]
-    bo_out.wait()
-    gi_out.wait()
+    for copy in (bo_out, *grads_out):
+        copy.wait()
+    for i in range(final + 1):
+        by_piece(i, finish, gi_hbm, cs, gi_sems, out=True)
 
 
 def local_grads(inputs, frames, cotangent, proj_in, proj_out, ffn_up, ffn_down, vectors, ffn_bias):
     rows, width = inputs.shape
     hidden_width = ffn_up.shape[1]
-    padded = -(-rows // TILE) * TILE
+    step = TILE * max(GROUP, PROJECTED)
+    padded = -(-rows // step) * step
     wide = padded + SPAN
     pairs = width // 128
     vmem = pl.BlockSpec(memory_space=pltpu.VMEM)
-    hbm = pl.BlockSpec(memory_space=pl.ANY)
+    hbm = pl.BlockSpec(memory_space=pltpu.HBM)
+    bias = ffn_bias.reshape(1, hidden_width)
     return pl.pallas_call(
         local_kernel,
         out_shape=(
@@ -345,29 +494,36 @@
             jax.ShapeDtypeStruct((width, hidden_width), f32),
             jax.ShapeDtypeStruct((hidden_width, width), f32),
         ),
-        in_specs=[pl.BlockSpec(memory_space=pltpu.SMEM), hbm, hbm] + [vmem] * 6,
-        out_specs=(hbm, hbm, vmem, vmem, vmem),
+        in_specs=[hbm] * 9,
+        out_specs=(hbm, hbm, vmem, hbm, hbm),
         scratch_shapes=[
+            pltpu.SMEM(frames.shape, jnp.int32),
+            *[pltpu.VMEM(a.shape, f32) for a in (proj_in, proj_out, ffn_up, ffn_down, vectors, bias)],
             pltpu.VMEM((padded, width), bf16),
             pltpu.VMEM((padded, width), f32),
             pltpu.VMEM((padded, width), bf16),
             *[pltpu.VMEM((wide, width), bf16)] * 7,
             pltpu.VMEM((frames.size, 8, 2 * QT), f32),
-            pltpu.VMEM((SPAN, width), f32),
-            pltpu.VMEM((SPAN, width), f32),
-            pltpu.VMEM((pairs, 128, SPAN), bf16),
+            pltpu.VMEM((2, SPAN, width), f32),
+            pltpu.VMEM((2, SPAN, width), f32),
+            pltpu.SMEM((SPAN // QT,), jnp.int32),
+            pltpu.SMEM((SPAN // QT, frames.size + 1), jnp.int32),
+            pltpu.SMEM((frames.size,), jnp.int32),
             pltpu.VMEM((width, 3 * width), bf16),
             pltpu.VMEM((width, width), bf16),
             pltpu.VMEM((width, hidden_width), bf16),
             pltpu.VMEM((hidden_width, width), bf16),
             pltpu.VMEM((width, hidden_width), f32),
+            pltpu.VMEM((hidden_width, width), f32),
+            pltpu.VMEM((width, hidden_width), f32),
             pltpu.VMEM((8, 8, width), f32),
             pltpu.VMEM((8, hidden_width), f32),
-            pltpu.SemaphoreType.DMA((4,)),
+            pltpu.SemaphoreType.DMA((11,)),
+            *[pltpu.SemaphoreType.DMA((padded // (TILE * PROJECTED),))] * 2,
         ],
         compiler_params=pltpu.CompilerParams(vmem_limit_bytes=60 * 1024 * 1024),
         name="local_grads",
-    )(frames, inputs, cotangent, proj_in, proj_out, ffn_up, ffn_down, vectors, ffn_bias.reshape(1, hidden_width))
+    )(frames, inputs, cotangent, proj_in, proj_out, ffn_up, ffn_down, vectors, bias)
 
 
 def over_all(x):

time: 200 us -> 137 us (0.69)
  Pallas kernels: 193 us -> 132 us
    pallas_call x1, Pallas kernels: 135 us -> 69 us  [local_grads(): pl.pallas_call(local_kernel, out_shape=(jax.ShapeDtypeStruct((rows, width...]
    pallas_call x1, Pallas kernels: 51.1 us -> 55.5 us  [exchange(): pl.pallas_call(functools.partial(exchange_kernel, n, orders, stages), out...]
where the time goes in v3:
time: 137 us
  Pallas kernels  132 us (96%)
  local copies, waits for them, and re-layouts  4.44 us (3%)
    pallas_call x1, Pallas kernels, local_grads(): pl.pallas_call(local_kernel, out_shape=(jax.ShapeDtypeStruct((rows, width...  69 us
    pallas_call x1, Pallas kernels, exchange(): pl.pallas_call(functools.partial(exchange_kernel, n, orders, stages), out...  55.5 us
    pallas_call x1, Pallas kernels, exchange(): pl.pallas_call(functools.partial(renew_kernel, n, orders), out_shape=shap...  7.2 us
    unnamed x43, local copies, waits for them, and re-layouts  4.44 us

profile of v3, /device:TPU:0, one launch (start us, length us, event | category | flops | bytes accessed | tf_op | source)
XLA Modules:
  0.0 137.1 jit_solution(10340377934785472865)
XLA Ops:
  0.7 0.0 copy-start
  0.7 0.0 copy-start.1
  0.7 0.0 copy-start.2
  0.7 0.0 copy-start.3
  0.7 0.0 copy-start.7
  0.7 0.0 copy-start.8
  0.7 0.0 copy-start.9
  0.7 0.0 copy-start.10
  0.8 0.0 copy-start.11
  0.8 0.0 copy-start.12
  0.8 0.0 copy-start.14
  0.8 0.0 copy-start.15
  0.8 69.0 %local_grads.1 = (bf16[4080,256]{1,0:T(8,128)(2,1)}, f32[4080,256]{1,0:T(8,128)}, f32[256,1152]{1,0:T(8,128)}, f32[256,1024]{1,0:T(8,128)}, f32[1024,256]{1,0:T(8,128)}) custom-call(s32[4,4]{1,0:T(4,128)} %frames_hbm.1, bf16[4080,256]{1,0:T(8,128)(2,1)} %x_hbm.1, f32[4080,256]{1,0:T(8,128)} %cot_hbm.1, f32[256,768]{1,0:T(8,128)} %pin_hbm.1, ...), custom_call_target="tpu_custom_call" | custom-call | tf_op jit(solution)/shard_map/local_grads/pallas_call | solution.py:488
  69.8 0.0 copy-done
  69.8 0.0 copy-done.1
  69.8 0.0 copy-done.2
  69.8 0.0 copy-done.3
  69.8 0.0 copy-done.7
  69.9 0.0 copy-done.8
  69.9 0.0 copy-done.9
  69.9 0.0 copy-done.10
  69.9 0.0 copy-done.11
  69.9 0.0 copy-done.12
  69.9 0.0 copy-done.14
  69.9 1.3 copy-done.4
  71.2 1.2 copy-done.5
  72.4 1.2 copy-done.6
  73.7 0.0 copy-start.19
  73.7 0.0 copy-start.20
  73.7 55.5 %exchange.1 = (f32[32,8,1152]{2,1,0:T(8,128)S(1)}, f32[32,8,1024]{2,1,0:T(8,128)S(1)}, f32[32,32,256]{2,1,0:T(8,128)S(1)}, f32[8,1152]{1,0:T(8,128)S(1)}, f32[8,1024]{1,0:T(8,128)S(1)}, /*index=5*/f32[32,256]{1,0:T(8,128)S(1)}) custom-call(f32[32,8,1152]{2,1,0:T(8,128)S(1)} %bitcast.47, f32[32,8,1024]{2,1,0:T(8,128)S(1)} %bitcast.48, ...), custom_call_target="tpu_custom_call" | custom-call | tf_op jit(solution)/shard_map/exchange/pallas_call | solution.py:747
  129.2 7.2 %renew.1 = (f32[48,128]{1,0:T(8,128)}, f32[16,128]{1,0:T(8,128)}, f32[64,128]{1,0:T(8,128)}, f32[64,128]{1,0:T(8,128)}, f32[48,128]{1,0:T(8,128)}, /*index=5*/f3...) custom-call(f32[32,8,1152]{2,1,0:T(8,128)S(1)} %get-tuple-element.76, ...), custom_call_target="tpu_custom_call" | custom-call | tf_op jit(solution)/shard_map/renew/pallas_call | solution.py:772
  136.4 0.6 copy.52
  (14 shorter events, 0.0 us)
Async XLA Ops:
  0.7 69.1 %copy-start = (f32[256,1024]{1,0:T(8,128)S(1)}, f32[256,1024]{1,0:T(8,128)}, u32[]{:S(2)}) copy-start(f32[256,1024]{1,0:T(8,128)} %pup_hbm.1) | copy-start | bytes 3145732
  0.7 69.1 %copy-start.1 = (f32[1024,256]{1,0:T(8,128)S(1)}, f32[1024,256]{1,0:T(8,128)}, u32[]{:S(2)}) copy-start(f32[1024,256]{1,0:T(8,128)} %pdown_hbm.1) | copy-start | bytes 3145732
  0.7 69.1 %copy-start.2 = (f32[256,768]{1,0:T(8,128)S(1)}, f32[256,768]{1,0:T(8,128)}, u32[]{:S(2)}) copy-start(f32[256,768]{1,0:T(8,128)} %pin_hbm.1) | copy-start | bytes 2359300
  0.7 69.1 %copy-start.3 = (f32[256,256]{1,0:T(8,128)S(1)}, f32[256,256]{1,0:T(8,128)}, u32[]{:S(2)}) copy-start(f32[256,256]{1,0:T(8,128)} %pout_hbm.1) | copy-start | bytes 786436
  0.7 69.1 %copy-start.7 = (f32[8192]{0:T(1024)S(1)}, f32[8192]{0:T(1024)}, u32[]{:S(2)}) copy-start(f32[8192]{0:T(1024)} %param.34) | copy-start | bytes 98308
  0.7 69.1 %copy-start.8 = (f32[8192]{0:T(1024)S(1)}, f32[8192]{0:T(1024)}, u32[]{:S(2)}) copy-start(f32[8192]{0:T(1024)} %param.36) | copy-start | bytes 98308
  0.7 69.1 %copy-start.9 = (f32[8192]{0:T(1024)S(1)}, f32[8192]{0:T(1024)}, u32[]{:S(2)}) copy-start(f32[8192]{0:T(1024)} %param.35) | copy-start | bytes 98308
  0.7 69.1 %copy-start.10 = (f32[8192]{0:T(1024)S(1)}, f32[8192]{0:T(1024)}, u32[]{:S(2)}) copy-start(f32[8192]{0:T(1024)} %param.37) | copy-start | bytes 98308
  0.8 69.1 %copy-start.11 = (f32[6144]{0:T(1024)S(1)}, f32[6144]{0:T(1024)}, u32[]{:S(2)}) copy-start(f32[6144]{0:T(1024)} %param.30) | copy-start | bytes 73732
  0.8 69.1 %copy-start.12 = (f32[6144]{0:T(1024)S(1)}, f32[6144]{0:T(1024)}, u32[]{:S(2)}) copy-start(f32[6144]{0:T(1024)} %param.31) | copy-start | bytes 73732
  0.8 69.1 %copy-start.14 = (f32[2048]{0:T(1024)S(1)}, f32[2048]{0:T(1024)}, u32[]{:S(2)}) copy-start(f32[2048]{0:T(1024)} %param.32) | copy-start | bytes 24580
  0.8 69.1 %copy-start.15 = (f32[2048]{0:T(1024)S(1)}, f32[2048]{0:T(1024)}, u32[]{:S(2)}) copy-start(f32[2048]{0:T(1024)} %param.33) | copy-start | bytes 24580
  69.9 1.3 copy-start.4
  71.2 1.2 copy-start.5
  72.4 1.2 copy-start.6
  73.7 55.5 %copy-start.13 = (f32[8,256]{1,0:T(8,128)S(1)}, f32[8,256]{1,0:T(8,128)}, u32[]{:S(2)}) copy-start(f32[8,256]{1,0:T(8,128)} %refs_18_.1) | copy-start | bytes 24580
  73.7 55.5 %copy-start.16 = (f32[1024]{0:T(1024)S(1)}, f32[1024]{0:T(1024)}, u32[]{:S(2)}) copy-start(f32[1024]{0:T(1024)} %param.29) | copy-start | bytes 12292
  73.7 55.5 %copy-start.17 = (f32[8,256]{1,0:T(8,128)S(1)}, f32[8,256]{1,0:T(8,128)}, u32[]{:S(2)}) copy-start(f32[8,256]{1,0:T(8,128)} %refs_20_.1) | copy-start | bytes 24580
  73.7 55.5 %copy-start.18 = (f32[8,256]{1,0:T(8,128)S(1)}, f32[8,256]{1,0:T(8,128)}, u32[]{:S(2)}) copy-start(f32[8,256]{1,0:T(8,128)} %refs_21_.1) | copy-start | bytes 24580
  73.7 55.5 %copy-start.19 = (f32[1024]{0:T(1024)S(1)}, f32[1024]{0:T(1024)}, u32[]{:S(2)}) copy-start(f32[1024]{0:T(1024)} %param.40) | copy-start | bytes 12292
  73.7 55.5 %copy-start.20 = (f32[1024]{0:T(1024)S(1)}, f32[1024]{0:T(1024)}, u32[]{:S(2)}) copy-start(f32[1024]{0:T(1024)} %param.41) | copy-start | bytes 12292

commit v4 on v3

--- a/solution.py
+++ b/solution.py
@@ -551,173 +551,251 @@
     return chunk_of, place_of
 
 
-def matrix_lanes(shapes):
-    return ((0, 0), (0, shapes[0][-1]), (1, 0), (2, 0))
-
-
-def flat_rows(rows, blocks, b):
-    return pl.ds(b, rows, stride=blocks) if blocks > 1 else pl.ds(0, rows)
-
-
-def exchange_kernel(n, orders, stages, *refs):
+def each(count, body, block=32):
+    block = min(count, block)
+    if count == block:
+        for i in range(count):
+            body(i)
+        return
+
+    def some(outer, _):
+        for i in range(block):
+            body(outer * block + i)
+        return 0
+
+    lax.fori_loop(0, count // block, some, 0)
+
+
+def cut_pieces(shapes):
+    wide, tall = shapes[1][2] // 2, shapes[2][1] // 2
+    return (
+        (0, slice(0, shapes[0][1]), slice(0, 640)),
+        (0, slice(0, shapes[0][1]), slice(640, shapes[0][2])),
+        (1, slice(0, shapes[1][1]), slice(0, wide)),
+        (1, slice(0, shapes[1][1]), slice(wide, 2 * wide)),
+        (2, slice(0, tall), slice(0, shapes[2][2])),
+        (2, slice(tall, 2 * tall), slice(0, shapes[2][2])),
+    )
+
+
+def cut_matrices(shapes):
+    (_, r_in, w_in), (_, _, w_out), (_, r_up, w_up), (_, r_down, w_down) = shapes
+    rest = w_in - 640
+    return (
+        (0, 0, r_in, 0, 640, 0, 0),
+        (0, 0, r_in, 640, rest, 1, 0),
+        (1, 0, r_in, 0, w_out, 1, rest),
+        (2, 0, r_up, 0, w_up // 2, 2, 0),
+        (2, 0, r_up, w_up // 2, w_up // 2, 3, 0),
+        (3, 0, r_down // 2, 0, w_down, 4, 0),
+        (3, r_down // 2, r_down // 2, 0, w_down, 5, 0),
+    )
+
+
+def flat_rows(first, rows, blocks, b):
+    return pl.ds(first * blocks + b, rows, stride=blocks)
+
+
+def exchange_kernel(n, walks, *refs):
+    count, stages = len(walks), len(walks[0])
     sources, owns, firsts, seconds = refs[:3], refs[3:7], refs[7:11], refs[11:15]
-    full, shares = refs[15:18], refs[18:21]
-    parcels, landed, send_sems, recv_sems = refs[21:24], refs[24:27], refs[27], refs[28]
+    full, shares = refs[15 : 15 + count], refs[15 + count : 15 + 2 * count]
+    parcels, landed = refs[15 + 2 * count : 15 + 3 * count], refs[15 + 3 * count : 15 + 4 * count]
+    send_sems, recv_sems = refs[15 + 4 * count :]
+    pieces = cut_pieces([s.shape for s in sources])
+    orders = [[b for bits in walk for b in bits] for walk in walks]
     me = lax.axis_index("dp")
 
     def bit(k):
         return (me // (1 << k)) % 2
 
-    def partner(k):
-        return me + (1 - 2 * bit(k)) * (1 << k)
+    def flips(bits):
+        return [[b for j, b in enumerate(bits) if t >> j & 1] for t in range(1, 1 << len(bits))]
+
+    def other(flip):
+        return me + sum((1 - 2 * bit(b)) * (1 << b) for b in flip)
+
+    def digit(bits, flip=()):
+        top = len(bits) - 1
+        return sum((1 - bit(b) if b in flip else bit(b)) * (1 << (top - j)) for j, b in enumerate(bits))
+
+    def left(p, k):
+        return n >> sum(len(bits) for bits in walks[p][: k + 1])
+
+    def slot(p, k):
+        return n - left(p, k - 1) if k else 0
 
     barrier = pltpu.get_barrier_semaphore()
-    for k in range(stages):
-        pl.semaphore_signal(barrier, inc=1, device_id=(partner(k),), device_id_type=pl.DeviceIdType.MESH)
-    pl.semaphore_wait(barrier, stages)
-
-    def region(k):
-        return n - (n >> k)
-
-    def remote(p, slot, src, dst, k):
-        return pltpu.make_async_remote_copy(
+    met = sorted({tuple(sorted(flip)) for walk in walks for bits in walk for flip in flips(bits)})
+    for flip in met:
+        pl.semaphore_signal(barrier, inc=1, device_id=(other(flip),), device_id_type=pl.DeviceIdType.MESH)
+    pl.semaphore_wait(barrier, len(met))
+
+    sent, used = {}, [0] * count
+
+    def remote(p, src, dst, flip, key):
+        copy = pltpu.make_async_remote_copy(
             src_ref=src,
             dst_ref=dst,
-            send_sem=send_sems.at[p, slot],
-            recv_sem=recv_sems.at[p, slot],
-            device_id=(partner(k),),
+            send_sem=send_sems.at[p, used[p]],
+            recv_sem=recv_sems.at[p, used[p]],
+            device_id=(other(flip),),
             device_id_type=pl.DeviceIdType.MESH,
         )
-
-    sent = []
-    halving = {}
-
-    def halve(p, k):
-        m = n >> (k + 1)
-        order = orders[p]
-        if k == 0:
-            away = (1 - bit(order[0])) * m
-
-            def pack(i, _):
-                parcels[p][i] = sources[p][places(order)[0](away + i)]
-                return 0
-
-            lax.fori_loop(0, m, pack, 0)
-            src = parcels[p]
-        else:
-            src = landed[p].at[pl.ds(region(k - 1) + (1 - bit(order[k])) * m, m)]
-        copy = remote(p, k, src, landed[p].at[pl.ds(region(k), m)], order[k])
+        used[p] += 1
         copy.start()
-        halving[p, k] = copy
-        sent.append(copy)
+        sent.setdefault(key, []).append(copy)
+        return copy
+
+    def leave(key):
+        for copy in sent.pop(key, ()):
+            copy.wait_send()
+
+    def chunk_of(p, i, first):
+        return places(orders[p][1:])[0](i) + first * (1 << orders[p][0])
+
+    arriving = {}
+
+    def split(p, k):
+        m, bits = left(p, k), walks[p][k]
+        copies = []
+        for t, flip in enumerate(flips(bits)):
+            if k == 0:
+                source, rows, lanes = pieces[p]
+
+                def pack(i):
+                    parcels[p][i] = sources[source][chunk_of(p, i, 1 - bit(bits[0])), rows, lanes]
+
+                each(m, pack)
+                src = parcels[p]
+            else:
+                src = landed[p].at[pl.ds(slot(p, k - 1) + digit(bits, flip) * m, m)]
+            copies.append(remote(p, src, landed[p].at[pl.ds(slot(p, k) + t * m, m)], flip, ("split", p, k)))
+        arriving[p, k] = copies
 
     def add(p, k):
-        m = n >> (k + 1)
-        order = orders[p]
-        mine = bit(order[k]) * m
-        halving[p, k].wait_recv()
-
-        def one(i, _):
-            if k == 0:
-                kept = sources[p][places(order)[0](mine + i)]
-            else:
-                kept = landed[p][region(k - 1) + mine + i]
-            at = region(k) + i
-            landed[p][at] = landed[p][at] + kept
-            return 0
-
-        lax.fori_loop(0, m, one, 0)
-
-    parts = range(len(orders))
+        m, bits = left(p, k), walks[p][k]
+        for copy in arriving[p, k]:
+            copy.wait_recv()
+        new = pl.ds(slot(p, k), m)
+        if k:
+            total = landed[p][pl.ds(slot(p, k - 1) + digit(bits) * m, m)]
+            for t in range(len(arriving[p, k])):
+                total = total + landed[p][pl.ds(slot(p, k) + t * m, m)]
+            landed[p][new] = total
+            return
+        source, rows, lanes = pieces[p]
+
+        def one(i):
+            landed[p][i] = landed[p][i] + sources[source][chunk_of(p, i, bit(bits[0])), rows, lanes]
+
+        each(m, one)
+
+    parts = range(count)
+    half = count // 2
     for p in parts:
-        halve(p, 0)
+        split(p, 0)
     for k in range(1, stages):
         for p in parts:
             add(p, k - 1)
-            halve(p, k)
+            if p >= half:
+                leave(("split", p - half, k))
+            split(p, k)
 
     homes = [places(order)[1](me) for order in orders]
-    matrices = matrix_lanes([own.shape for own in owns])
-    gathering = {}
+    matrices = cut_matrices([own.shape for own in owns])
 
     def gather(p, k):
-        size = 1 << (stages - 1 - k)
-        at = pl.ds(homes[p] // size * size, size)
-        copy = remote(p, stages + k, full[p].at[at], full[p].at[at], orders[p][k])
-        copy.start()
-        gathering[p, k] = copy
-        sent.append(copy)
-
+        m = left(p, k)
+        at = pl.ds(homes[p] // m * m, m)
+        arriving[p, stages + k] = [
+            remote(p, full[p].at[at], full[p].at[at], flip, ("gather", p, k)) for flip in flips(walks[p][k])
+        ]
+
+    last = stages - 1
     for p in parts:
-        add(p, stages - 1)
-        last = region(stages - 1)
-        for i, (part, lane) in enumerate(matrices):
-            if part != p:
+        add(p, last)
+        share = slot(p, last)
+        for i, row, rows, lane, lanes, piece, start in matrices:
+            if piece != p:
                 continue
-            rows = sources[p].shape[1]
             blocks = owns[i].shape[2] // 128
-            for b in range(blocks):
-                flat = flat_rows(rows, blocks, b)
-                lanes = slice(128 * b, 128 * (b + 1))
-                here = slice(lane + 128 * b, lane + 128 * (b + 1))
-                momentum, variance = momenta(firsts[i][flat, :], seconds[i][flat, :], landed[p][last, :, here])
-                full[p][homes[p], :, here] = direction(momentum, variance) + DECAY * owns[i][me, :, lanes]
-        if p == 0:
-            tail = slice(full[0].shape[2] - 128, full[0].shape[2])
-            full[0][homes[0], :, tail] = landed[0][last, :, tail]
-        shares[p][...] = landed[p][last]
-        gather(p, stages - 1)
-    for k in range(stages - 2, -1, -1):
+            for b in range(lanes // 128):
+                flat = flat_rows(row, rows, blocks, lane // 128 + b)
+                here = slice(start + 128 * b, start + 128 * (b + 1))
+                own = owns[i][me, row : row + rows, lane + 128 * b : lane + 128 * (b + 1)]
+                momentum, variance = momenta(firsts[i][flat, :], seconds[i][flat, :], landed[p][share, :, here])
+                full[p][homes[p], :, here] = direction(momentum, variance) + DECAY * own
+        if p == 1:
+            tail = slice(full[1].shape[2] - 128, full[1].shape[2])
+            full[1][homes[1], :, tail] = landed[1][share, :, tail]
+        shares[p][...] = landed[p][share]
+        gather(p, last)
+    for k in range(last - 1, -1, -1):
         for p in parts:
-            gathering[p, k + 1].wait_recv()
+            for copy in arriving[p, stages + k + 1]:
+                copy.wait_recv()
+            if p >= half and k:
+                leave(("gather", p - half, k))
             gather(p, k)
     for p in parts:
-        gathering[p, 0].wait_recv()
-
-    for copy in sent:
-        copy.wait_send()
+        for copy in arriving[p, stages]:
+            copy.wait_recv()
+    for key in list(sent):
+        leave(key)
 
 
 def renew_kernel(n, orders, *refs):
-    full, shares = refs[:3], refs[3:6]
-    weights, firsts, seconds = refs[6:10], refs[10:14], refs[14:18]
-    vec, bias, fvec, svec, fbias, sbias = refs[18:24]
-    g_out, m_out, v_out = refs[24:28], refs[28:32], refs[32:36]
-    w_new, w_low = refs[36:40], refs[40:44]
-    gvec, gbias, mvec, vvec, wvec, mbias, vbias, wbias, norms = refs[44:53]
-    rows24 = refs[53]
-    for i, (part, lane) in enumerate(matrix_lanes([w.shape for w in weights])):
-        _, rows, columns = weights[i].shape
-        here = slice(lane, lane + columns)
-        place_of = places(orders[part])[1]
-        blocks = columns // 128
-        for b in range(blocks):
-            flat = flat_rows(rows, blocks, b)
-            g = shares[part][:, lane + 128 * b : lane + 128 * (b + 1)]
+    count = len(orders)
+    full, shares, refs = refs[:count], refs[count : 2 * count], refs[2 * count :]
+    weights, firsts, seconds = refs[:4], refs[4:8], refs[8:12]
+    vec, bias, fvec, svec, fbias, sbias = refs[12:18]
+    g_out, m_out, v_out = refs[18:22], refs[22:26], refs[26:30]
+    w_out, low_out = refs[30:34], refs[34:38]
+    gvec, gbias, mvec, vvec, wvec, mbias, vbias, wbias, norms = refs[38:47]
+    rows24, w_new, w_low, sems = refs[47], refs[48:52], refs[52:56], refs[56]
+    matrices = cut_matrices([w.shape for w in weights])
+    for i, row, rows, lane, lanes, piece, start in matrices:
+        blocks = weights[i].shape[2] // 128
+        for b in range(lanes // 128):
+            flat = flat_rows(row, rows, blocks, lane // 128 + b)
+            g = shares[piece][:, start + 128 * b : start + 128 * (b + 1)]
             g_out[i][flat, :] = g
             m_out[i][flat, :], v_out[i][flat, :] = momenta(firsts[i][flat, :], seconds[i][flat, :], g)
-        step = full[part][:, :, here]
-        u_norm = jnp.sqrt(over_all(jnp.sum(step * step, axis=0)))
+    leaving = []
+    for i in (2, 3, 0, 1):
+        _, rows, columns = weights[i].shape
+        own = [entry for entry in matrices if entry[0] == i]
+        total = 0.0
+        for _i, _row, _rows, _lane, lanes, piece, start in own:
+            step = full[piece][:, :, start : start + lanes]
+            total = total + over_all(jnp.sum(step * step, axis=0))
+        u_norm = jnp.sqrt(total)
         old = weights[i][...]
         w_norm = jnp.sqrt(over_all(jnp.sum(old * old, axis=0)))
         norms[i : i + 1, 0:1] = w_norm
         norms[i : i + 1, 1:2] = u_norm
         ratio = RATE * (w_norm / (u_norm + EPS_ADAM))
 
-        def renew(chunk, _, i=i, part=part, here=here, place_of=place_of, ratio=ratio):
-            w_new[i][chunk] = weights[i][chunk] - ratio * full[part][place_of(chunk), :, here]
-            return 0
-
-        lax.fori_loop(0, n, renew, 0)
+        def renew(chunk, own=own, ratio=ratio, i=i):
+            for _i, row, rows, lane, lanes, piece, start in own:
+                at, to = slice(row, row + rows), slice(lane, lane + lanes)
+                step = full[piece][places(orders[piece])[1](chunk), :, start : start + lanes]
+                w_new[i][chunk, at, to] = weights[i][chunk, at, to] - ratio * step
+
+        each(n, renew)
         if rows % 8 == 0:
             w_low[i][...] = w_new[i][...].reshape(n * rows, columns).astype(bf16)
         else:
             w_low[i][...] = jnp.zeros_like(w_low[i])
-
-    rows = full[0].shape[1]
-    tail = full[0].shape[2] - 128
+        for k, (src, dst) in enumerate(((w_new[i], w_out[i]), (w_low[i], low_out[i]))):
+            leaving.append(pltpu.make_async_copy(src, dst, sems.at[2 * i + k]))
+            leaving[-1].start()
+
+    rows = full[1].shape[1]
+    tail = full[1].shape[2] - 128
     for chunk in range(rows24.shape[0] // rows):
-        rows24[chunk * rows : (chunk + 1) * rows, :] = full[0][places(orders[0])[1](chunk), :, tail:]
+        rows24[chunk * rows : (chunk + 1) * rows, :] = full[1][places(orders[1])[1](chunk), :, tail:]
 
     def plain(weight, grad, first, second):
         momentum, variance = momenta(first, second, grad)
@@ -729,13 +807,19 @@
     grad = rows24[16:24, :]
     gbias[...] = grad
     mbias[...], vbias[...], wbias[...] = plain(bias[...], grad, fbias[...], sbias[...])
+    for copy in leaving:
+        copy.wait()
 
 
 def exchange(n, grads, weights, vectors, ffn_bias, firsts, seconds, others):
-    stages = n.bit_length() - 1
-    far = list(range(1, stages))
-    turns = [far[s:] + far[:s] for s in (len(far) * p // 3 for p in range(3))]
-    orders = tuple((0, *turn) for turn in turns)
+    far = list(range(1, n.bit_length() - 1))
+    axes = [far[len(far) * p // 3 : len(far) * (p + 1) // 3] for p in range(3)]
+    x, y, z = ([(b,) for b in axis] for axis in axes)
+    walks = tuple(
+        ((0,), *a, *b, *c) for a, b, c in ((x, y, z), (y, z, x), (z, x, y), (x, z, y), (y, x, z), (z, y, x))
+    )
+    orders = tuple(tuple(b for bits in walk for b in bits) for walk in walks)
+    copies = 2 * sum((1 << len(bits)) - 1 for bits in walks[0])
     cut = lambda a: a.reshape(n, a.shape[0] // n, a.shape[1])
     sources, blocks = list(map(cut, grads)), list(map(cut, weights))
     flat = lambda a: a.reshape(-1, 128)
@@ -743,17 +827,20 @@
     like = lambda a, dtype=f32: jax.ShapeDtypeStruct(a.shape, dtype)
     firsts, seconds = list(map(flat, firsts)), list(map(flat, seconds))
     operands = [*sources, *blocks, *firsts, *seconds]
-    shapes = [*map(like, sources), *[jax.ShapeDtypeStruct(s.shape[1:], f32) for s in sources]]
+    sizes = [
+        (rows.stop - rows.start, lanes.stop - lanes.start) for _, rows, lanes in cut_pieces([s.shape for s in sources])
+    ]
+    shapes = [jax.ShapeDtypeStruct((n, *s), f32) for s in sizes] + [jax.ShapeDtypeStruct(s, f32) for s in sizes]
     reduced = pl.pallas_call(
-        functools.partial(exchange_kernel, n, orders, stages),
+        functools.partial(exchange_kernel, n, walks),
         out_shape=shapes,
         in_specs=[vmem] * len(operands),
         out_specs=[vmem] * len(shapes),
         scratch_shapes=[
-            *[pltpu.VMEM((n // 2, *s.shape[1:]), f32) for s in sources],
-            *[pltpu.VMEM(s.shape, f32) for s in sources],
-            pltpu.SemaphoreType.DMA((3, 2 * stages)),
-            pltpu.SemaphoreType.DMA((3, 2 * stages)),
+            *[pltpu.VMEM((n // 2, *s), f32) for s in sizes],
+            *[pltpu.VMEM((n, *s), f32) for s in sizes],
+            pltpu.SemaphoreType.DMA((len(sizes), copies)),
+            pltpu.SemaphoreType.DMA((len(sizes), copies)),
         ],
         compiler_params=pltpu.CompilerParams(
             collective_id=0, has_side_effects=True, vmem_limit_bytes=32 * 1024 * 1024
@@ -773,8 +860,13 @@
         functools.partial(renew_kernel, n, orders),
         out_shape=shapes,
         in_specs=[vmem] * len(operands),
-        out_specs=[vmem] * len(shapes),
-        scratch_shapes=[pltpu.VMEM((24, 128), f32)],
+        out_specs=[vmem] * 12 + [pl.BlockSpec(memory_space=pl.ANY)] * 8 + [vmem] * 9,
+        scratch_shapes=[
+            pltpu.VMEM((24, 128), f32),
+            *[pltpu.VMEM(b.shape, f32) for b in blocks],
+            *[pltpu.VMEM(w.shape, bf16) for w in weights],
+            pltpu.SemaphoreType.DMA((8,)),
+        ],
         compiler_params=pltpu.CompilerParams(vmem_limit_bytes=32 * 1024 * 1024),
         name="renew",
     )(*operands)

time: 137 us -> 128 us (0.934)
  Pallas kernels: 132 us -> 123 us
    pallas_call x1, Pallas kernels: 55.5 us -> 50.1 us  [exchange(): pl.pallas_call(functools.partial(exchange_kernel, n, walks), out_shape=sh...]
    pallas_call x1, Pallas kernels: 7.2 us -> 3.83 us  [exchange(): pl.pallas_call(functools.partial(renew_kernel, n, orders), out_shape=shap...]
where the time goes in v4:
time: 128 us
  Pallas kernels  123 us (96%)
  local copies, waits for them, and re-layouts  4.44 us (3%)
    pallas_call x1, Pallas kernels, local_grads(): pl.pallas_call(local_kernel, out_shape=(jax.ShapeDtypeStruct((rows, width...  68.7 us
    pallas_call x1, Pallas kernels, exchange(): pl.pallas_call(functools.partial(exchange_kernel, n, walks), out_shape=sh...  50.1 us
    unnamed x43, local copies, waits for them, and re-layouts  4.44 us
    pallas_call x1, Pallas kernels, exchange(): pl.pallas_call(functools.partial(renew_kernel, n, orders), out_shape=shap...  3.83 us

profile of v4, /device:TPU:0, one launch (start us, length us, event | category | flops | bytes accessed | tf_op | source)
XLA Modules:
  0.0 128.0 jit_solution(2619445096157024102)
XLA Ops:
  0.7 0.0 copy-start
  0.7 0.0 copy-start.1
  0.7 0.0 copy-start.2
  0.7 0.0 copy-start.3
  0.7 0.0 copy-start.7
  0.7 0.0 copy-start.8
  0.7 0.0 copy-start.9
  0.7 0.0 copy-start.10
  0.8 0.0 copy-start.11
  0.8 0.0 copy-start.12
  0.8 0.0 copy-start.14
  0.8 0.0 copy-start.15
  0.8 68.7 %local_grads.1 = (bf16[4080,256]{1,0:T(8,128)(2,1)}, f32[4080,256]{1,0:T(8,128)}, f32[256,1152]{1,0:T(8,128)}, f32[256,1024]{1,0:T(8,128)}, f32[1024,256]{1,0:T(8,128)}) custom-call(s32[4,4]{1,0:T(4,128)} %frames_hbm.1, bf16[4080,256]{1,0:T(8,128)(2,1)} %x_hbm.1, f32[4080,256]{1,0:T(8,128)} %cot_hbm.1, f32[256,768]{1,0:T(8,128)} %pin_hbm.1, ...), custom_call_target="tpu_custom_call" | custom-call | tf_op jit(solution)/shard_map/local_grads/pallas_call | solution.py:488
  69.5 0.0 copy-done
  69.5 0.0 copy-done.1
  69.5 0.0 copy-done.2
  69.5 0.0 copy-done.3
  69.5 0.0 copy-done.7
  69.5 0.0 copy-done.8
  69.5 0.0 copy-done.9
  69.5 0.0 copy-done.10
  69.6 0.0 copy-done.11
  69.6 0.0 copy-done.12
  69.6 0.0 copy-done.14
  69.6 1.3 copy-done.4
  70.9 1.2 copy-done.5
  72.1 1.2 copy-done.6
  73.3 0.0 copy-start.19
  73.3 0.0 copy-start.20
  73.3 50.1 %exchange.1 = (f32[32,8,640]{2,1,0:T(8,128)S(1)}, f32[32,8,512]{2,1,0:T(8,128)S(1)}, f32[32,8,512]{2,1,0:T(8,128)S(1)}, f32[32,8,512]{2,1,0:T(8,128)S(1)}, f32[3...) custom-call(f32[32,8,1152]{2,1,0:T(8,128)S(1)} %bitcast.47, ...), custom_call_target="tpu_custom_call" | custom-call | tf_op jit(solution)/shard_map/exchange/pallas_call | solution.py:834
  123.5 3.8 %renew.1 = (f32[48,128]{1,0:T(8,128)}, f32[16,128]{1,0:T(8,128)}, f32[64,128]{1,0:T(8,128)}, f32[64,128]{1,0:T(8,128)}, f32[48,128]{1,0:T(8,128)}, /*index=5*/f3...) custom-call(f32[32,8,640]{2,1,0:T(8,128)S(1)} %get-tuple-element.82., ...), custom_call_target="tpu_custom_call" | custom-call | tf_op jit(solution)/shard_map/renew/pallas_call | solution.py:859
  127.3 0.6 copy.52
  (14 shorter events, 0.0 us)
Async XLA Ops:
  0.7 68.8 %copy-start = (f32[256,1024]{1,0:T(8,128)S(1)}, f32[256,1024]{1,0:T(8,128)}, u32[]{:S(2)}) copy-start(f32[256,1024]{1,0:T(8,128)} %pup_hbm.1) | copy-start | bytes 3145732
  0.7 68.8 %copy-start.1 = (f32[1024,256]{1,0:T(8,128)S(1)}, f32[1024,256]{1,0:T(8,128)}, u32[]{:S(2)}) copy-start(f32[1024,256]{1,0:T(8,128)} %pdown_hbm.1) | copy-start | bytes 3145732
  0.7 68.8 %copy-start.2 = (f32[256,768]{1,0:T(8,128)S(1)}, f32[256,768]{1,0:T(8,128)}, u32[]{:S(2)}) copy-start(f32[256,768]{1,0:T(8,128)} %pin_hbm.1) | copy-start | bytes 2359300
  0.7 68.8 %copy-start.3 = (f32[256,256]{1,0:T(8,128)S(1)}, f32[256,256]{1,0:T(8,128)}, u32[]{:S(2)}) copy-start(f32[256,256]{1,0:T(8,128)} %pout_hbm.1) | copy-start | bytes 786436
  0.7 68.8 %copy-start.7 = (f32[8192]{0:T(1024)S(1)}, f32[8192]{0:T(1024)}, u32[]{:S(2)}) copy-start(f32[8192]{0:T(1024)} %param.34) | copy-start | bytes 98308
  0.7 68.8 %copy-start.8 = (f32[8192]{0:T(1024)S(1)}, f32[8192]{0:T(1024)}, u32[]{:S(2)}) copy-start(f32[8192]{0:T(1024)} %param.36) | copy-start | bytes 98308
  0.7 68.8 %copy-start.9 = (f32[8192]{0:T(1024)S(1)}, f32[8192]{0:T(1024)}, u32[]{:S(2)}) copy-start(f32[8192]{0:T(1024)} %param.35) | copy-start | bytes 98308
  0.7 68.8 %copy-start.10 = (f32[8192]{0:T(1024)S(1)}, f32[8192]{0:T(1024)}, u32[]{:S(2)}) copy-start(f32[8192]{0:T(1024)} %param.37) | copy-start | bytes 98308
  0.8 68.8 %copy-start.11 = (f32[6144]{0:T(1024)S(1)}, f32[6144]{0:T(1024)}, u32[]{:S(2)}) copy-start(f32[6144]{0:T(1024)} %param.30) | copy-start | bytes 73732
  0.8 68.8 %copy-start.12 = (f32[6144]{0:T(1024)S(1)}, f32[6144]{0:T(1024)}, u32[]{:S(2)}) copy-start(f32[6144]{0:T(1024)} %param.31) | copy-start | bytes 73732
  0.8 68.8 %copy-start.14 = (f32[2048]{0:T(1024)S(1)}, f32[2048]{0:T(1024)}, u32[]{:S(2)}) copy-start(f32[2048]{0:T(1024)} %param.32) | copy-start | bytes 24580
  0.8 68.8 %copy-start.15 = (f32[2048]{0:T(1024)S(1)}, f32[2048]{0:T(1024)}, u32[]{:S(2)}) copy-start(f32[2048]{0:T(1024)} %param.33) | copy-start | bytes 24580
  69.6 1.3 copy-start.4
  70.9 1.2 copy-start.5
  72.1 1.2 copy-start.6
  73.3 50.1 %copy-start.13 = (f32[8,256]{1,0:T(8,128)S(1)}, f32[8,256]{1,0:T(8,128)}, u32[]{:S(2)}) copy-start(f32[8,256]{1,0:T(8,128)} %refs_24_.1) | copy-start | bytes 24580
  73.3 50.1 %copy-start.16 = (f32[1024]{0:T(1024)S(1)}, f32[1024]{0:T(1024)}, u32[]{:S(2)}) copy-start(f32[1024]{0:T(1024)} %param.29) | copy-start | bytes 12292
  73.3 50.1 %copy-start.17 = (f32[8,256]{1,0:T(8,128)S(1)}, f32[8,256]{1,0:T(8,128)}, u32[]{:S(2)}) copy-start(f32[8,256]{1,0:T(8,128)} %refs_26_.1) | copy-start | bytes 24580
  73.3 50.1 %copy-start.18 = (f32[8,256]{1,0:T(8,128)S(1)}, f32[8,256]{1,0:T(8,128)}, u32[]{:S(2)}) copy-start(f32[8,256]{1,0:T(8,128)} %refs_27_.1) | copy-start | bytes 24580
  73.3 50.1 %copy-start.19 = (f32[1024]{0:T(1024)S(1)}, f32[1024]{0:T(1024)}, u32[]{:S(2)}) copy-start(f32[1024]{0:T(1024)} %param.40) | copy-start | bytes 12292
  73.3 50.1 %copy-start.20 = (f32[1024]{0:T(1024)S(1)}, f32[1024]{0:T(1024)}, u32[]{:S(2)}) copy-start(f32[1024]{0:T(1024)} %param.41) | copy-start | bytes 12292

commit v5 on v4

--- a/solution.py
+++ b/solution.py
@@ -85,8 +85,8 @@
 
 def local_kernel(
     frames_hbm, x_hbm, cot_hbm, pin_hbm, pout_hbm, pup_hbm, pdown_hbm, vec_hbm, bias_hbm,
-    bo_hbm, gi_hbm, ga_ref, gup_hbm, gdown_hbm,
-    frames_ref, pin_ref, pout_ref, pup_ref, pdown_ref, vec_ref, bias_ref, xs, cs, bos, qs, ks, vs, dq, dk, dv, dms, lse, dka, dva, counts, members, starts, win, wout, wup, wdown, gup_ref, gdown_ref, gdt, sums, bsum, sems, x_sems, gi_sems,
+    bo_hbm, gi_hbm, ga_hbm, gup_hbm, gdown_hbm,
+    frames_ref, pin_ref, pout_ref, pup_ref, pdown_ref, vec_ref, bias_ref, xs, cs, bos, qs, ks, vs, dq, dk, dv, dms, lse, dka, dva, counts, members, starts, win, wout, wup, wdown, ga_ref, gup_ref, gdown_ref, gdt, sums, bsum, sems, x_sems, gi_sems,
 ):
     rows, width = x_hbm.shape
     padded = xs.shape[0]
@@ -372,8 +372,8 @@
     for c in range(0, hidden_width, 256):
         gdown_ref[c : c + 256, :] = gdt[:, c : c + 256].T
     grads_out = [
-        pltpu.make_async_copy(gup_ref, gup_hbm, sems.at[9]),
-        pltpu.make_async_copy(gdown_ref, gdown_hbm, sems.at[10]),
+        pltpu.make_async_copy(gup_ref, gup_hbm.at[pl.ds(0, width)], sems.at[9]),
+        pltpu.make_async_copy(gdown_ref, gdown_hbm.at[pl.ds(0, hidden_width)], sems.at[10]),
     ]
     for copy in grads_out:
         copy.start()
@@ -469,20 +469,21 @@
     for b in range(hidden_width // 128):
         row = 8 * (width // 128) + b
         ga_ref[row : row + 1, tail : tail + 128] = bias[:, 128 * b : 128 * (b + 1)]
+    grads_out.append(pltpu.make_async_copy(ga_ref, ga_hbm.at[pl.ds(0, width)], sems.at[11]))
+    grads_out[-1].start()
     for copy in (bo_out, *grads_out):
         copy.wait()
     for i in range(final + 1):
         by_piece(i, finish, gi_hbm, cs, gi_sems, out=True)
 
 
-def local_grads(inputs, frames, cotangent, proj_in, proj_out, ffn_up, ffn_down, vectors, ffn_bias):
+def local_grads(spare, inputs, frames, cotangent, proj_in, proj_out, ffn_up, ffn_down, vectors, ffn_bias):
     rows, width = inputs.shape
     hidden_width = ffn_up.shape[1]
     step = TILE * max(GROUP, PROJECTED)
     padded = -(-rows // step) * step
     wide = padded + SPAN
     pairs = width // 128
-    vmem = pl.BlockSpec(memory_space=pltpu.VMEM)
     hbm = pl.BlockSpec(memory_space=pltpu.HBM)
     bias = ffn_bias.reshape(1, hidden_width)
     return pl.pallas_call(
@@ -490,12 +491,12 @@
         out_shape=(
             jax.ShapeDtypeStruct((rows, width), bf16),
             jax.ShapeDtypeStruct((rows, width), f32),
-            jax.ShapeDtypeStruct((width, 4 * width + 128), f32),
-            jax.ShapeDtypeStruct((width, hidden_width), f32),
-            jax.ShapeDtypeStruct((hidden_width, width), f32),
+            jax.ShapeDtypeStruct((spare * width, 4 * width + 128), f32),
+            jax.ShapeDtypeStruct((spare * width, hidden_width), f32),
+            jax.ShapeDtypeStruct((spare * hidden_width, width), f32),
         ),
         in_specs=[hbm] * 9,
-        out_specs=(hbm, hbm, vmem, hbm, hbm),
+        out_specs=(hbm,) * 5,
         scratch_shapes=[
             pltpu.SMEM(frames.shape, jnp.int32),
             *[pltpu.VMEM(a.shape, f32) for a in (proj_in, proj_out, ffn_up, ffn_down, vectors, bias)],
@@ -513,12 +514,13 @@
             pltpu.VMEM((width, width), bf16),
             pltpu.VMEM((width, hidden_width), bf16),
             pltpu.VMEM((hidden_width, width), bf16),
+            pltpu.VMEM((width, 4 * width + 128), f32),
             pltpu.VMEM((width, hidden_width), f32),
             pltpu.VMEM((hidden_width, width), f32),
             pltpu.VMEM((width, hidden_width), f32),
             pltpu.VMEM((8, 8, width), f32),
             pltpu.VMEM((8, hidden_width), f32),
-            pltpu.SemaphoreType.DMA((11,)),
+            pltpu.SemaphoreType.DMA((12,)),
             *[pltpu.SemaphoreType.DMA((padded // (TILE * PROJECTED),))] * 2,
         ],
         compiler_params=pltpu.CompilerParams(vmem_limit_bytes=60 * 1024 * 1024),
@@ -598,10 +600,10 @@
 
 def exchange_kernel(n, walks, *refs):
     count, stages = len(walks), len(walks[0])
-    sources, owns, firsts, seconds = refs[:3], refs[3:7], refs[7:11], refs[11:15]
+    grads, owns, firsts, seconds = refs[:3], refs[3:7], refs[7:11], refs[11:15]
     full, shares = refs[15 : 15 + count], refs[15 + count : 15 + 2 * count]
     parcels, landed = refs[15 + 2 * count : 15 + 3 * count], refs[15 + 3 * count : 15 + 4 * count]
-    send_sems, recv_sems = refs[15 + 4 * count :]
+    sources, (send_sems, recv_sems, load_sems) = refs[15 + 4 * count : 18 + 4 * count], refs[18 + 4 * count :]
     pieces = cut_pieces([s.shape for s in sources])
     orders = [[b for bits in walk for b in bits] for walk in walks]
     me = lax.axis_index("dp")
@@ -625,15 +627,21 @@
     def slot(p, k):
         return n - left(p, k - 1) if k else 0
 
+    loads = [
+        pltpu.make_async_copy(grad.at[pl.ds(0, n)], source, load_sems.at[k])
+        for k, (grad, source) in enumerate(zip(grads, sources))
+    ]
+    for copy in loads:
+        copy.start()
     barrier = pltpu.get_barrier_semaphore()
     met = sorted({tuple(sorted(flip)) for walk in walks for bits in walk for flip in flips(bits)})
     for flip in met:
         pl.semaphore_signal(barrier, inc=1, device_id=(other(flip),), device_id_type=pl.DeviceIdType.MESH)
     pl.semaphore_wait(barrier, len(met))
 
-    sent, used = {}, [0] * count
-
-    def remote(p, src, dst, flip, key):
+    sent, used = [], [0] * count
+
+    def remote(p, src, dst, flip):
         copy = pltpu.make_async_remote_copy(
             src_ref=src,
             dst_ref=dst,
@@ -644,12 +652,8 @@
         )
         used[p] += 1
         copy.start()
-        sent.setdefault(key, []).append(copy)
+        sent.append(copy)
         return copy
-
-    def leave(key):
-        for copy in sent.pop(key, ()):
-            copy.wait_send()
 
     def chunk_of(p, i, first):
         return places(orders[p][1:])[0](i) + first * (1 << orders[p][0])
@@ -670,7 +674,7 @@
                 src = parcels[p]
             else:
                 src = landed[p].at[pl.ds(slot(p, k - 1) + digit(bits, flip) * m, m)]
-            copies.append(remote(p, src, landed[p].at[pl.ds(slot(p, k) + t * m, m)], flip, ("split", p, k)))
+            copies.append(remote(p, src, landed[p].at[pl.ds(slot(p, k) + t * m, m)], flip))
         arriving[p, k] = copies
 
     def add(p, k):
@@ -692,14 +696,13 @@
         each(m, one)
 
     parts = range(count)
-    half = count // 2
     for p in parts:
+        if pieces[p][0] not in [source for source, _, _ in pieces[:p]]:
+            loads[pieces[p][0]].wait()
         split(p, 0)
     for k in range(1, stages):
         for p in parts:
             add(p, k - 1)
-            if p >= half:
-                leave(("split", p - half, k))
             split(p, k)
 
     homes = [places(order)[1](me) for order in orders]
@@ -709,7 +712,7 @@
         m = left(p, k)
         at = pl.ds(homes[p] // m * m, m)
         arriving[p, stages + k] = [
-            remote(p, full[p].at[at], full[p].at[at], flip, ("gather", p, k)) for flip in flips(walks[p][k])
+            remote(p, full[p].at[at], full[p].at[at], flip) for flip in flips(walks[p][k])
         ]
 
     last = stages - 1
@@ -735,14 +738,12 @@
         for p in parts:
             for copy in arriving[p, stages + k + 1]:
                 copy.wait_recv()
-            if p >= half and k:
-                leave(("gather", p - half, k))
             gather(p, k)
     for p in parts:
         for copy in arriving[p, stages]:
             copy.wait_recv()
-    for key in list(sent):
-        leave(key)
+    for copy in sent:
+        copy.wait_send()
 
 
 def renew_kernel(n, orders, *refs):
@@ -773,8 +774,8 @@
         u_norm = jnp.sqrt(total)
         old = weights[i][...]
         w_norm = jnp.sqrt(over_all(jnp.sum(old * old, axis=0)))
-        norms[i : i + 1, 0:1] = w_norm
-        norms[i : i + 1, 1:2] = u_norm
+        norms[0:1, i : i + 1] = w_norm
+        norms[1:2, i : i + 1] = u_norm
         ratio = RATE * (w_norm / (u_norm + EPS_ADAM))
 
         def renew(chunk, own=own, ratio=ratio, i=i):
@@ -811,39 +812,47 @@
         copy.wait()
 
 
-def exchange(n, grads, weights, vectors, ffn_bias, firsts, seconds, others):
+def exchange(n, spare, grads, weights, vectors, ffn_bias, firsts, seconds, others):
     far = list(range(1, n.bit_length() - 1))
     axes = [far[len(far) * p // 3 : len(far) * (p + 1) // 3] for p in range(3)]
     x, y, z = ([(b,) for b in axis] for axis in axes)
     walks = tuple(
         ((0,), *a, *b, *c) for a, b, c in ((x, y, z), (y, z, x), (z, x, y), (x, z, y), (y, x, z), (z, y, x))
     )
+    if len(far) == 4:
+        sets = ("xyab", "yxba", "ayxb", "xayb", "ybxa", "bxya")
+        walks = tuple(((0,), *((far["xyab".index(c)],) for c in order)) for order in sets)
     orders = tuple(tuple(b for bits in walk for b in bits) for walk in walks)
     copies = 2 * sum((1 << len(bits)) - 1 for bits in walks[0])
     cut = lambda a: a.reshape(n, a.shape[0] // n, a.shape[1])
-    sources, blocks = list(map(cut, grads)), list(map(cut, weights))
+    blocks = list(map(cut, weights))
+    chunks = [(g.shape[0] // (n * spare), g.shape[1]) for g in grads]
+    sources = [g.reshape(n * spare, *chunk) for g, chunk in zip(grads, chunks)]
+    held = [(n, *chunk) for chunk in chunks]
     flat = lambda a: a.reshape(-1, 128)
     vmem = pl.BlockSpec(memory_space=pltpu.VMEM)
     like = lambda a, dtype=f32: jax.ShapeDtypeStruct(a.shape, dtype)
     firsts, seconds = list(map(flat, firsts)), list(map(flat, seconds))
     operands = [*sources, *blocks, *firsts, *seconds]
     sizes = [
-        (rows.stop - rows.start, lanes.stop - lanes.start) for _, rows, lanes in cut_pieces([s.shape for s in sources])
+        (rows.stop - rows.start, lanes.stop - lanes.start) for _, rows, lanes in cut_pieces(held)
     ]
     shapes = [jax.ShapeDtypeStruct((n, *s), f32) for s in sizes] + [jax.ShapeDtypeStruct(s, f32) for s in sizes]
     reduced = pl.pallas_call(
         functools.partial(exchange_kernel, n, walks),
         out_shape=shapes,
-        in_specs=[vmem] * len(operands),
+        in_specs=[pl.BlockSpec(memory_space=pl.ANY)] * 3 + [vmem] * 12,
         out_specs=[vmem] * len(shapes),
         scratch_shapes=[
             *[pltpu.VMEM((n // 2, *s), f32) for s in sizes],
             *[pltpu.VMEM((n, *s), f32) for s in sizes],
+            *[pltpu.VMEM(shape, f32) for shape in held],
             pltpu.SemaphoreType.DMA((len(sizes), copies)),
             pltpu.SemaphoreType.DMA((len(sizes), copies)),
+            pltpu.SemaphoreType.DMA((3,)),
         ],
         compiler_params=pltpu.CompilerParams(
-            collective_id=0, has_side_effects=True, vmem_limit_bytes=32 * 1024 * 1024
+            collective_id=0, has_side_effects=True, vmem_limit_bytes=44 * 1024 * 1024
         ),
         name="exchange",
     )(*operands)
@@ -854,7 +863,7 @@
     moments = list(map(like, firsts))
     shapes = [
         *moments, *moments, *moments, *map(like, blocks), *[like(w, bf16) for w in weights],
-        like(vectors), like(line_bias), *[like(vectors)] * 3, *[like(line_bias)] * 3, jax.ShapeDtypeStruct((4, 2), f32),
+        like(vectors), like(line_bias), *[like(vectors)] * 3, *[like(line_bias)] * 3, jax.ShapeDtypeStruct((2, 4), f32),
     ]
     results = pl.pallas_call(
         functools.partial(renew_kernel, n, orders),
@@ -876,20 +885,21 @@
     gvec, gbias, mvec, vvec, wvec, mbias, vbias, wbias, norms = results[20:]
     line = lambda a: a.reshape(-1)
     steps = [entry for i in range(4) for entry in (m[i], v[i], w[i], low[i])]
-    return (*g, gvec, line(gbias), *steps, mvec, vvec, wvec, line(mbias), line(vbias), line(wbias), norms)
+    return (*g, gvec, line(gbias), *steps, mvec, vvec, wvec, line(mbias), line(vbias), line(wbias), norms.T)
 
 
 def on_device(n, inputs, frames, cotangent, *rest):
     proj_in, proj_out, ffn_up, ffn_down, vectors, ffn_bias = rest[:6]
     moments, others = rest[6:14], rest[14:]
+    spare = 24 if proj_in.shape[0] % (8 * n) == 0 else 1
     block_out, grad_inputs, *grads = local_grads(
-        inputs, frames, cotangent, proj_in, proj_out, ffn_up, ffn_down, vectors, ffn_bias
+        spare, inputs, frames, cotangent, proj_in, proj_out, ffn_up, ffn_down, vectors, ffn_bias
     )
     weights = (proj_in, proj_out, ffn_up, ffn_down)
     return (
         block_out,
         grad_inputs,
-        *exchange(n, grads, weights, vectors, ffn_bias, moments[0::2], moments[1::2], others),
+        *exchange(n, spare, grads, weights, vectors, ffn_bias, moments[0::2], moments[1::2], others),
     )
 
 

time: 128 us -> 121 us (0.945)
  local copies, waits for them, and re-layouts: 4.44 us -> 0.09 us
  Pallas kernels: 123 us -> 119 us
    unnamed x43 -> x36, local copies, waits for them, and re-layouts: 4.44 us -> 0.09 us
    pallas_call x1, Pallas kernels: 50.1 us -> 45.8 us  [exchange(): pl.pallas_call(functools.partial(exchange_kernel, n, walks), out_shape=sh...]
where the time goes in v5:
time: 121 us
  Pallas kernels  119 us (98%)
    pallas_call x1, Pallas kernels, local_grads(): pl.pallas_call(local_kernel, out_shape=(jax.ShapeDtypeStruct((rows, width...  69.8 us
    pallas_call x1, Pallas kernels, exchange(): pl.pallas_call(functools.partial(exchange_kernel, n, walks), out_shape=sh...  45.8 us
    pallas_call x1, Pallas kernels, exchange(): pl.pallas_call(functools.partial(renew_kernel, n, orders), out_shape=shap...  3.77 us

profile of v5, /device:TPU:0, one launch (start us, length us, event | category | flops | bytes accessed | tf_op | source)
XLA Modules:
  0.0 120.6 jit_solution(6456014617193952317)
XLA Ops:
  0.7 0.0 copy-start
  0.7 0.0 copy-start.1
  0.7 0.0 copy-start.2
  0.7 0.0 copy-start.3
  0.7 0.0 copy-start.4
  0.7 0.0 copy-start.5
  0.7 0.0 copy-start.6
  0.7 0.0 copy-start.7
  0.8 0.0 copy-start.8
  0.8 0.0 copy-start.9
  0.8 0.0 copy-start.11
  0.8 0.0 copy-start.12
  0.8 69.8 %local_grads.1 = (bf16[4080,256]{1,0:T(8,128)(2,1)}, f32[4080,256]{1,0:T(8,128)}, f32[6144,1152]{1,0:T(8,128)}, f32[6144,1024]{1,0:T(8,128)}, f32[24576,256]{1,0:T(8,128)}) custom-call(s32[4,4]{1,0:T(4,128)} %frames_hbm.1, bf16[4080,256]{1,0:T(8,128)(2,1)} %x_hbm.1, f32[4080,256]{1,0:T(8,128)} %cot_hbm.1, f32[256,768]{1,0:T(8,128)} %pin_hbm.1, ...), custom_call_target="tpu_custom_call" | custom-call | tf_op jit(solution)/shard_map/local_grads/pallas_call | solution.py:489
  70.6 0.0 copy-done
  70.6 0.0 copy-done.1
  70.7 0.0 copy-done.2
  70.7 0.0 copy-done.3
  70.7 0.0 copy-done.4
  70.7 0.0 copy-done.5
  70.7 0.0 copy-done.6
  70.7 0.0 copy-done.7
  70.7 0.0 copy-done.8
  70.7 0.0 copy-done.9
  70.7 0.0 copy-done.11
  70.8 0.0 copy-start.10
  70.8 0.0 copy-start.13
  70.8 0.0 copy-start.14
  70.8 0.0 copy-start.15
  70.8 0.0 copy-start.16
  70.8 0.0 copy-start.17
  70.8 45.8 %exchange.1 = (f32[32,8,640]{2,1,0:T(8,128)S(1)}, f32[32,8,512]{2,1,0:T(8,128)S(1)}, f32[32,8,512]{2,1,0:T(8,128)S(1)}, f32[32,8,512]{2,1,0:T(8,128)S(1)}, f32[3...) custom-call(f32[768,8,1152]{2,1,0:T(8,128)} %bitcast.68, ...), custom_call_target="tpu_custom_call" | custom-call | tf_op jit(solution)/shard_map/exchange/pallas_call | solution.py:841
  116.7 3.8 %renew.1 = (f32[48,128]{1,0:T(8,128)}, f32[16,128]{1,0:T(8,128)}, f32[64,128]{1,0:T(8,128)}, f32[64,128]{1,0:T(8,128)}, f32[48,128]{1,0:T(8,128)}, /*index=5*/f3...) custom-call(f32[32,8,640]{2,1,0:T(8,128)S(1)} %get-tuple-element.82., ...), custom_call_target="tpu_custom_call" | custom-call | tf_op jit(solution)/shard_map/renew/pallas_call | solution.py:868
  (7 shorter events, 0.0 us)
Async XLA Ops:
  0.7 70.0 %copy-start = (f32[256,1024]{1,0:T(8,128)S(1)}, f32[256,1024]{1,0:T(8,128)}, u32[]{:S(2)}) copy-start(f32[256,1024]{1,0:T(8,128)} %pup_hbm.1) | copy-start | bytes 3145732
  0.7 70.0 %copy-start.1 = (f32[1024,256]{1,0:T(8,128)S(1)}, f32[1024,256]{1,0:T(8,128)}, u32[]{:S(2)}) copy-start(f32[1024,256]{1,0:T(8,128)} %pdown_hbm.1) | copy-start | bytes 3145732
  0.7 70.0 %copy-start.2 = (f32[256,768]{1,0:T(8,128)S(1)}, f32[256,768]{1,0:T(8,128)}, u32[]{:S(2)}) copy-start(f32[256,768]{1,0:T(8,128)} %pin_hbm.1) | copy-start | bytes 2359300
  0.7 70.0 %copy-start.3 = (f32[256,256]{1,0:T(8,128)S(1)}, f32[256,256]{1,0:T(8,128)}, u32[]{:S(2)}) copy-start(f32[256,256]{1,0:T(8,128)} %pout_hbm.1) | copy-start | bytes 786436
  0.7 70.0 %copy-start.4 = (f32[8192]{0:T(1024)S(1)}, f32[8192]{0:T(1024)}, u32[]{:S(2)}) copy-start(f32[8192]{0:T(1024)} %param.34) | copy-start | bytes 98308
  0.7 70.0 %copy-start.5 = (f32[8192]{0:T(1024)S(1)}, f32[8192]{0:T(1024)}, u32[]{:S(2)}) copy-start(f32[8192]{0:T(1024)} %param.36) | copy-start | bytes 98308
  0.7 70.0 %copy-start.6 = (f32[8192]{0:T(1024)S(1)}, f32[8192]{0:T(1024)}, u32[]{:S(2)}) copy-start(f32[8192]{0:T(1024)} %param.35) | copy-start | bytes 98308
  0.7 70.0 %copy-start.7 = (f32[8192]{0:T(1024)S(1)}, f32[8192]{0:T(1024)}, u32[]{:S(2)}) copy-start(f32[8192]{0:T(1024)} %param.37) | copy-start | bytes 98308
  0.8 70.0 %copy-start.8 = (f32[6144]{0:T(1024)S(1)}, f32[6144]{0:T(1024)}, u32[]{:S(2)}) copy-start(f32[6144]{0:T(1024)} %param.30) | copy-start | bytes 73732
  0.8 70.0 %copy-start.9 = (f32[6144]{0:T(1024)S(1)}, f32[6144]{0:T(1024)}, u32[]{:S(2)}) copy-start(f32[6144]{0:T(1024)} %param.31) | copy-start | bytes 73732
  0.8 70.0 %copy-start.11 = (f32[2048]{0:T(1024)S(1)}, f32[2048]{0:T(1024)}, u32[]{:S(2)}) copy-start(f32[2048]{0:T(1024)} %param.32) | copy-start | bytes 24580
  0.8 70.0 %copy-start.12 = (f32[2048]{0:T(1024)S(1)}, f32[2048]{0:T(1024)}, u32[]{:S(2)}) copy-start(f32[2048]{0:T(1024)} %param.33) | copy-start | bytes 24580
  70.8 45.9 %copy-start.10 = (f32[8,256]{1,0:T(8,128)S(1)}, f32[8,256]{1,0:T(8,128)}, u32[]{:S(2)}) copy-start(f32[8,256]{1,0:T(8,128)} %refs_24_.1) | copy-start | bytes 24580
  70.8 45.9 %copy-start.13 = (f32[1024]{0:T(1024)S(1)}, f32[1024]{0:T(1024)}, u32[]{:S(2)}) copy-start(f32[1024]{0:T(1024)} %param.29) | copy-start | bytes 12292
  70.8 45.9 %copy-start.14 = (f32[8,256]{1,0:T(8,128)S(1)}, f32[8,256]{1,0:T(8,128)}, u32[]{:S(2)}) copy-start(f32[8,256]{1,0:T(8,128)} %refs_26_.1) | copy-start | bytes 24580
  70.8 45.9 %copy-start.15 = (f32[8,256]{1,0:T(8,128)S(1)}, f32[8,256]{1,0:T(8,128)}, u32[]{:S(2)}) copy-start(f32[8,256]{1,0:T(8,128)} %refs_27_.1) | copy-start | bytes 24580
  70.8 45.9 %copy-start.16 = (f32[1024]{0:T(1024)S(1)}, f32[1024]{0:T(1024)}, u32[]{:S(2)}) copy-start(f32[1024]{0:T(1024)} %param.40) | copy-start | bytes 12292
  70.8 45.9 %copy-start.17 = (f32[1024]{0:T(1024)S(1)}, f32[1024]{0:T(1024)}, u32[]{:S(2)}) copy-start(f32[1024]{0:T(1024)} %param.41) | copy-start | bytes 12292

commit v6 on v5

--- a/solution.py
+++ b/solution.py
@@ -627,11 +627,12 @@
     def slot(p, k):
         return n - left(p, k - 1) if k else 0
 
+    quarters = [pl.ds(q * n // 4, n // 4) for q in range(4)]
     loads = [
-        pltpu.make_async_copy(grad.at[pl.ds(0, n)], source, load_sems.at[k])
+        [pltpu.make_async_copy(grad.at[at], source.at[at], load_sems.at[k, q]) for q, at in enumerate(quarters)]
         for k, (grad, source) in enumerate(zip(grads, sources))
     ]
-    for copy in loads:
+    for copy in (copy for group in loads for copy in group):
         copy.start()
     barrier = pltpu.get_barrier_semaphore()
     met = sorted({tuple(sorted(flip)) for walk in walks for bits in walk for flip in flips(bits)})
@@ -698,7 +699,8 @@
     parts = range(count)
     for p in parts:
         if pieces[p][0] not in [source for source, _, _ in pieces[:p]]:
-            loads[pieces[p][0]].wait()
+            for copy in loads[pieces[p][0]]:
+                copy.wait()
         split(p, 0)
     for k in range(1, stages):
         for p in parts:
@@ -849,7 +851,7 @@
             *[pltpu.VMEM(shape, f32) for shape in held],
             pltpu.SemaphoreType.DMA((len(sizes), copies)),
             pltpu.SemaphoreType.DMA((len(sizes), copies)),
-            pltpu.SemaphoreType.DMA((3,)),
+            pltpu.SemaphoreType.DMA((3, 4)),
         ],
         compiler_params=pltpu.CompilerParams(
             collective_id=0, has_side_effects=True, vmem_limit_bytes=44 * 1024 * 1024

time: 121 us -> 122 us (level)
    pallas_call x1, Pallas kernels: 45.8 us -> 48.2 us  [exchange(): pl.pallas_call(functools.partial(exchange_kernel, n, walks), out_shape=sh...]
    pallas_call x1, Pallas kernels: 69.8 us -> 68.1 us  [local_grads(): pl.pallas_call(local_kernel, out_shape=(jax.ShapeDtypeStruct((rows, width...]
where the time goes in v6:
time: 122 us; the launch traced here: 121 us
  Pallas kernels  120 us (98%)
    pallas_call x1, Pallas kernels, local_grads(): pl.pallas_call(local_kernel, out_shape=(jax.ShapeDtypeStruct((rows, width...  68.1 us
    pallas_call x1, Pallas kernels, exchange(): pl.pallas_call(functools.partial(exchange_kernel, n, walks), out_shape=sh...  48.2 us
    pallas_call x1, Pallas kernels, exchange(): pl.pallas_call(functools.partial(renew_kernel, n, orders), out_shape=shap...  3.77 us

profile of v6, /device:TPU:0, one launch (start us, length us, event | category | flops | bytes accessed | tf_op | source)
XLA Modules:
  0.0 121.2 jit_solution(14372929485622720966)
XLA Ops:
  0.7 0.0 copy-start
  0.7 0.0 copy-start.1
  0.7 0.0 copy-start.2
  0.7 0.0 copy-start.3
  0.7 0.0 copy-start.4
  0.7 0.0 copy-start.5
  0.7 0.0 copy-start.6
  0.7 0.0 copy-start.7
  0.8 0.0 copy-start.8
  0.8 0.0 copy-start.9
  0.8 0.0 copy-start.11
  0.8 68.1 %local_grads.1 = (bf16[4080,256]{1,0:T(8,128)(2,1)}, f32[4080,256]{1,0:T(8,128)}, f32[6144,1152]{1,0:T(8,128)}, f32[6144,1024]{1,0:T(8,128)}, f32[24576,256]{1,0:T(8,128)}) custom-call(s32[4,4]{1,0:T(4,128)} %frames_hbm.1, bf16[4080,256]{1,0:T(8,128)(2,1)} %x_hbm.1, f32[4080,256]{1,0:T(8,128)} %cot_hbm.1, f32[256,768]{1,0:T(8,128)} %pin_hbm.1, ...), custom_call_target="tpu_custom_call" | custom-call | tf_op jit(solution)/shard_map/local_grads/pallas_call | solution.py:489
  68.9 0.0 copy-done
  68.9 0.0 copy-done.1
  68.9 0.0 copy-done.2
  68.9 0.0 copy-done.3
  68.9 0.0 copy-done.4
  68.9 0.0 copy-done.5
  69.0 0.0 copy-done.6
  69.0 0.0 copy-done.7
  69.0 0.0 copy-done.8
  69.0 0.0 copy-done.9
  69.0 0.0 copy-done.11
  69.0 0.0 copy-done.12
  69.0 0.0 copy-start.10
  69.0 0.0 copy-start.13
  69.0 0.0 copy-start.14
  69.0 0.0 copy-start.15
  69.1 0.0 copy-start.16
  69.1 0.0 copy-start.17
  69.1 48.2 %exchange.1 = (f32[32,8,640]{2,1,0:T(8,128)S(1)}, f32[32,8,512]{2,1,0:T(8,128)S(1)}, f32[32,8,512]{2,1,0:T(8,128)S(1)}, f32[32,8,512]{2,1,0:T(8,128)S(1)}, f32[3...) custom-call(f32[768,8,1152]{2,1,0:T(8,128)} %bitcast.68, ...), custom_call_target="tpu_custom_call" | custom-call | tf_op jit(solution)/shard_map/exchange/pallas_call | solution.py:843
  117.3 3.8 %renew.1 = (f32[48,128]{1,0:T(8,128)}, f32[16,128]{1,0:T(8,128)}, f32[64,128]{1,0:T(8,128)}, f32[64,128]{1,0:T(8,128)}, f32[48,128]{1,0:T(8,128)}, /*index=5*/f3...) custom-call(f32[32,8,640]{2,1,0:T(8,128)S(1)} %get-tuple-element.82., ...), custom_call_target="tpu_custom_call" | custom-call | tf_op jit(solution)/shard_map/renew/pallas_call | solution.py:870
  (7 shorter events, 0.0 us)
Async XLA Ops:
  0.7 68.2 %copy-start = (f32[256,1024]{1,0:T(8,128)S(1)}, f32[256,1024]{1,0:T(8,128)}, u32[]{:S(2)}) copy-start(f32[256,1024]{1,0:T(8,128)} %pup_hbm.1) | copy-start | bytes 3145732
  0.7 68.2 %copy-start.1 = (f32[1024,256]{1,0:T(8,128)S(1)}, f32[1024,256]{1,0:T(8,128)}, u32[]{:S(2)}) copy-start(f32[1024,256]{1,0:T(8,128)} %pdown_hbm.1) | copy-start | bytes 3145732
  0.7 68.2 %copy-start.2 = (f32[256,768]{1,0:T(8,128)S(1)}, f32[256,768]{1,0:T(8,128)}, u32[]{:S(2)}) copy-start(f32[256,768]{1,0:T(8,128)} %pin_hbm.1) | copy-start | bytes 2359300
  0.7 68.2 %copy-start.3 = (f32[256,256]{1,0:T(8,128)S(1)}, f32[256,256]{1,0:T(8,128)}, u32[]{:S(2)}) copy-start(f32[256,256]{1,0:T(8,128)} %pout_hbm.1) | copy-start | bytes 786436
  0.7 68.2 %copy-start.4 = (f32[8192]{0:T(1024)S(1)}, f32[8192]{0:T(1024)}, u32[]{:S(2)}) copy-start(f32[8192]{0:T(1024)} %param.34) | copy-start | bytes 98308
  0.7 68.2 %copy-start.5 = (f32[8192]{0:T(1024)S(1)}, f32[8192]{0:T(1024)}, u32[]{:S(2)}) copy-start(f32[8192]{0:T(1024)} %param.36) | copy-start | bytes 98308
  0.7 68.2 %copy-start.6 = (f32[8192]{0:T(1024)S(1)}, f32[8192]{0:T(1024)}, u32[]{:S(2)}) copy-start(f32[8192]{0:T(1024)} %param.35) | copy-start | bytes 98308
  0.7 68.2 %copy-start.7 = (f32[8192]{0:T(1024)S(1)}, f32[8192]{0:T(1024)}, u32[]{:S(2)}) copy-start(f32[8192]{0:T(1024)} %param.37) | copy-start | bytes 98308
  0.8 68.2 %copy-start.8 = (f32[6144]{0:T(1024)S(1)}, f32[6144]{0:T(1024)}, u32[]{:S(2)}) copy-start(f32[6144]{0:T(1024)} %param.30) | copy-start | bytes 73732
  0.8 68.2 %copy-start.9 = (f32[6144]{0:T(1024)S(1)}, f32[6144]{0:T(1024)}, u32[]{:S(2)}) copy-start(f32[6144]{0:T(1024)} %param.31) | copy-start | bytes 73732
  0.8 68.2 %copy-start.11 = (f32[2048]{0:T(1024)S(1)}, f32[2048]{0:T(1024)}, u32[]{:S(2)}) copy-start(f32[2048]{0:T(1024)} %param.32) | copy-start | bytes 24580
  0.8 68.2 %copy-start.12 = (f32[2048]{0:T(1024)S(1)}, f32[2048]{0:T(1024)}, u32[]{:S(2)}) copy-start(f32[2048]{0:T(1024)} %param.33) | copy-start | bytes 24580
  69.0 48.2 %copy-start.10 = (f32[8,256]{1,0:T(8,128)S(1)}, f32[8,256]{1,0:T(8,128)}, u32[]{:S(2)}) copy-start(f32[8,256]{1,0:T(8,128)} %refs_24_.1) | copy-start | bytes 24580
  69.0 48.2 %copy-start.13 = (f32[1024]{0:T(1024)S(1)}, f32[1024]{0:T(1024)}, u32[]{:S(2)}) copy-start(f32[1024]{0:T(1024)} %param.29) | copy-start | bytes 12292
  69.0 48.2 %copy-start.14 = (f32[8,256]{1,0:T(8,128)S(1)}, f32[8,256]{1,0:T(8,128)}, u32[]{:S(2)}) copy-start(f32[8,256]{1,0:T(8,128)} %refs_26_.1) | copy-start | bytes 24580
  69.0 48.2 %copy-start.15 = (f32[8,256]{1,0:T(8,128)S(1)}, f32[8,256]{1,0:T(8,128)}, u32[]{:S(2)}) copy-start(f32[8,256]{1,0:T(8,128)} %refs_27_.1) | copy-start | bytes 24580
  69.1 48.2 %copy-start.16 = (f32[1024]{0:T(1024)S(1)}, f32[1024]{0:T(1024)}, u32[]{:S(2)}) copy-start(f32[1024]{0:T(1024)} %param.40) | copy-start | bytes 12292
  69.1 48.2 %copy-start.17 = (f32[1024]{0:T(1024)S(1)}, f32[1024]{0:T(1024)}, u32[]{:S(2)}) copy-start(f32[1024]{0:T(1024)} %param.41) | copy-start | bytes 12292

commit v7 on v6

--- a/solution.py
+++ b/solution.py
@@ -792,8 +792,11 @@
         else:
             w_low[i][...] = jnp.zeros_like(w_low[i])
         for k, (src, dst) in enumerate(((w_new[i], w_out[i]), (w_low[i], low_out[i]))):
-            leaving.append(pltpu.make_async_copy(src, dst, sems.at[2 * i + k]))
-            leaving[-1].start()
+            part = src.shape[0] // 4
+            for q in range(4):
+                at = pl.ds(q * part, part)
+                leaving.append(pltpu.make_async_copy(src.at[at], dst.at[at], sems.at[2 * i + k, q]))
+                leaving[-1].start()
 
     rows = full[1].shape[1]
     tail = full[1].shape[2] - 128
@@ -876,7 +879,7 @@
             pltpu.VMEM((24, 128), f32),
             *[pltpu.VMEM(b.shape, f32) for b in blocks],
             *[pltpu.VMEM(w.shape, bf16) for w in weights],
-            pltpu.SemaphoreType.DMA((8,)),
+            pltpu.SemaphoreType.DMA((8, 4)),
         ],
         compiler_params=pltpu.CompilerParams(vmem_limit_bytes=32 * 1024 * 1024),
         name="renew",

time: 122 us -> 120 us (0.984); the launches traced: 121 us -> 120 us
    pallas_call x1, Pallas kernels: 48.2 us -> 45.5 us  [exchange(): pl.pallas_call(functools.partial(exchange_kernel, n, walks), out_shape=sh...]
    pallas_call x1, Pallas kernels: 68.1 us -> 69.8 us  [local_grads(): pl.pallas_call(local_kernel, out_shape=(jax.ShapeDtypeStruct((rows, width...]
where the time goes in v7:
time: 120 us
  Pallas kernels  119 us (99%)
    pallas_call x1, Pallas kernels, local_grads(): pl.pallas_call(local_kernel, out_shape=(jax.ShapeDtypeStruct((rows, width...  69.8 us
    pallas_call x1, Pallas kernels, exchange(): pl.pallas_call(functools.partial(exchange_kernel, n, walks), out_shape=sh...  45.5 us
    pallas_call x1, Pallas kernels, exchange(): pl.pallas_call(functools.partial(renew_kernel, n, orders), out_shape=shap...  3.95 us

profile of v7, /device:TPU:0, one launch (start us, length us, event | category | flops | bytes accessed | tf_op | source)
XLA Modules:
  0.0 120.5 jit_solution(13915622958246623290)
XLA Ops:
  0.7 0.0 copy-start
  0.7 0.0 copy-start.1
  0.7 0.0 copy-start.2
  0.7 0.0 copy-start.3
  0.7 0.0 copy-start.4
  0.7 0.0 copy-start.5
  0.7 0.0 copy-start.6
  0.7 0.0 copy-start.7
  0.8 0.0 copy-start.8
  0.8 0.0 copy-start.9
  0.8 0.0 copy-start.11
  0.8 0.0 copy-start.12
  0.8 69.8 %local_grads.1 = (bf16[4080,256]{1,0:T(8,128)(2,1)}, f32[4080,256]{1,0:T(8,128)}, f32[6144,1152]{1,0:T(8,128)}, f32[6144,1024]{1,0:T(8,128)}, f32[24576,256]{1,0:T(8,128)}) custom-call(s32[4,4]{1,0:T(4,128)} %frames_hbm.1, bf16[4080,256]{1,0:T(8,128)(2,1)} %x_hbm.1, f32[4080,256]{1,0:T(8,128)} %cot_hbm.1, f32[256,768]{1,0:T(8,128)} %pin_hbm.1, ...), custom_call_target="tpu_custom_call" | custom-call | tf_op jit(solution)/shard_map/local_grads/pallas_call | solution.py:489
  70.6 0.0 copy-done
  70.6 0.0 copy-done.1
  70.6 0.0 copy-done.2
  70.6 0.0 copy-done.3
  70.6 0.0 copy-done.4
  70.6 0.0 copy-done.5
  70.6 0.0 copy-done.6
  70.7 0.0 copy-done.7
  70.7 0.0 copy-done.8
  70.7 0.0 copy-done.9
  70.7 0.0 copy-done.11
  70.7 0.0 copy-start.10
  70.7 0.0 copy-start.13
  70.7 0.0 copy-start.14
  70.7 0.0 copy-start.15
  70.8 0.0 copy-start.16
  70.8 0.0 copy-start.17
  70.8 45.5 %exchange.1 = (f32[32,8,640]{2,1,0:T(8,128)S(1)}, f32[32,8,512]{2,1,0:T(8,128)S(1)}, f32[32,8,512]{2,1,0:T(8,128)S(1)}, f32[32,8,512]{2,1,0:T(8,128)S(1)}, f32[3...) custom-call(f32[768,8,1152]{2,1,0:T(8,128)} %bitcast.68, ...), custom_call_target="tpu_custom_call" | custom-call | tf_op jit(solution)/shard_map/exchange/pallas_call | solution.py:846
  116.4 4.0 %renew.1 = (f32[48,128]{1,0:T(8,128)}, f32[16,128]{1,0:T(8,128)}, f32[64,128]{1,0:T(8,128)}, f32[64,128]{1,0:T(8,128)}, f32[48,128]{1,0:T(8,128)}, /*index=5*/f3...) custom-call(f32[32,8,640]{2,1,0:T(8,128)S(1)} %get-tuple-element.82., ...), custom_call_target="tpu_custom_call" | custom-call | tf_op jit(solution)/shard_map/renew/pallas_call | solution.py:873
  (7 shorter events, 0.0 us)
Async XLA Ops:
  0.7 69.9 %copy-start = (f32[256,1024]{1,0:T(8,128)S(1)}, f32[256,1024]{1,0:T(8,128)}, u32[]{:S(2)}) copy-start(f32[256,1024]{1,0:T(8,128)} %pup_hbm.1) | copy-start | bytes 3145732
  0.7 69.9 %copy-start.1 = (f32[1024,256]{1,0:T(8,128)S(1)}, f32[1024,256]{1,0:T(8,128)}, u32[]{:S(2)}) copy-start(f32[1024,256]{1,0:T(8,128)} %pdown_hbm.1) | copy-start | bytes 3145732
  0.7 69.9 %copy-start.2 = (f32[256,768]{1,0:T(8,128)S(1)}, f32[256,768]{1,0:T(8,128)}, u32[]{:S(2)}) copy-start(f32[256,768]{1,0:T(8,128)} %pin_hbm.1) | copy-start | bytes 2359300
  0.7 69.9 %copy-start.3 = (f32[256,256]{1,0:T(8,128)S(1)}, f32[256,256]{1,0:T(8,128)}, u32[]{:S(2)}) copy-start(f32[256,256]{1,0:T(8,128)} %pout_hbm.1) | copy-start | bytes 786436
  0.7 69.9 %copy-start.4 = (f32[8192]{0:T(1024)S(1)}, f32[8192]{0:T(1024)}, u32[]{:S(2)}) copy-start(f32[8192]{0:T(1024)} %param.34) | copy-start | bytes 98308
  0.7 69.9 %copy-start.5 = (f32[8192]{0:T(1024)S(1)}, f32[8192]{0:T(1024)}, u32[]{:S(2)}) copy-start(f32[8192]{0:T(1024)} %param.36) | copy-start | bytes 98308
  0.7 69.9 %copy-start.6 = (f32[8192]{0:T(1024)S(1)}, f32[8192]{0:T(1024)}, u32[]{:S(2)}) copy-start(f32[8192]{0:T(1024)} %param.35) | copy-start | bytes 98308
  0.7 69.9 %copy-start.7 = (f32[8192]{0:T(1024)S(1)}, f32[8192]{0:T(1024)}, u32[]{:S(2)}) copy-start(f32[8192]{0:T(1024)} %param.37) | copy-start | bytes 98308
  0.8 69.9 %copy-start.8 = (f32[6144]{0:T(1024)S(1)}, f32[6144]{0:T(1024)}, u32[]{:S(2)}) copy-start(f32[6144]{0:T(1024)} %param.30) | copy-start | bytes 73732
  0.8 69.9 %copy-start.9 = (f32[6144]{0:T(1024)S(1)}, f32[6144]{0:T(1024)}, u32[]{:S(2)}) copy-start(f32[6144]{0:T(1024)} %param.31) | copy-start | bytes 73732
  0.8 69.9 %copy-start.11 = (f32[2048]{0:T(1024)S(1)}, f32[2048]{0:T(1024)}, u32[]{:S(2)}) copy-start(f32[2048]{0:T(1024)} %param.32) | copy-start | bytes 24580
  0.8 69.9 %copy-start.12 = (f32[2048]{0:T(1024)S(1)}, f32[2048]{0:T(1024)}, u32[]{:S(2)}) copy-start(f32[2048]{0:T(1024)} %param.33) | copy-start | bytes 24580
  70.7 45.6 %copy-start.10 = (f32[8,256]{1,0:T(8,128)S(1)}, f32[8,256]{1,0:T(8,128)}, u32[]{:S(2)}) copy-start(f32[8,256]{1,0:T(8,128)} %refs_24_.1) | copy-start | bytes 24580
  70.7 45.6 %copy-start.13 = (f32[1024]{0:T(1024)S(1)}, f32[1024]{0:T(1024)}, u32[]{:S(2)}) copy-start(f32[1024]{0:T(1024)} %param.29) | copy-start | bytes 12292
  70.7 45.6 %copy-start.14 = (f32[8,256]{1,0:T(8,128)S(1)}, f32[8,256]{1,0:T(8,128)}, u32[]{:S(2)}) copy-start(f32[8,256]{1,0:T(8,128)} %refs_26_.1) | copy-start | bytes 24580
  70.7 45.6 %copy-start.15 = (f32[8,256]{1,0:T(8,128)S(1)}, f32[8,256]{1,0:T(8,128)}, u32[]{:S(2)}) copy-start(f32[8,256]{1,0:T(8,128)} %refs_27_.1) | copy-start | bytes 24580
  70.8 45.6 %copy-start.16 = (f32[1024]{0:T(1024)S(1)}, f32[1024]{0:T(1024)}, u32[]{:S(2)}) copy-start(f32[1024]{0:T(1024)} %param.40) | copy-start | bytes 12292
  70.8 45.6 %copy-start.17 = (f32[1024]{0:T(1024)S(1)}, f32[1024]{0:T(1024)}, u32[]{:S(2)}) copy-start(f32[1024]{0:T(1024)} %param.41) | copy-start | bytes 12292
